TPU v7x, 32 devices: a whole 2x2x4 slice. The times are simulated.
32 devices in a mesh: wide: 8 (over y, x, core), narrow: 4 (over z).
Axes of the slice: x: 2, y: 2, z: 4, core: 2. Of those that a mesh axis runs over, the one named last changes fastest.
Arguments:
- loads: float32 [24576, 512], P('wide', 'narrow'), may hold values from -6 to 6
- start: float32 [24576, 512], P('wide', 'narrow'), may hold values from -6 to 6
- stiffness: bfloat16 [32, 1024, 1024], P('wide')
- local_inverse: bfloat16 [32, 1024, 1024], P('wide')
- modes: bfloat16 [32, 1024, 32], P('wide'), may hold values from -0.1875 to 0.1875
- coarse_inverse: float32 [1024, 1024], P('wide', 'narrow'), as said below
- margin_rows: int32 [32, 256], P('wide'), may hold values from 0 to 24575, as said below
Outputs:
- displacement: float32 [24576, 512], P('wide', 'narrow')
- final_residual: float32 [24576, 512], P('wide', 'narrow')
Inputs may be any that keep to these rules, and one draw needn't show every extreme that they name: Row s lists 256 distinct rows of loads, none of them rows s * 768 to s * 768 + 767. Call rows i * 4 * 768 to (i + 1) * 4 * 768 - 1 block i. For every i, the entries of rows i * 4 to (i + 1) * 4 - 1 of margin_rows fall at most 192 times into any one block, and exactly 192 times into some block. coarse_inverse equals its transpose.
All inputs are finite; a program needn't handle non-finite values.
Results may differ from a plain program's by a relative error of at most 0.0062.
Values may be sent and summed in bfloat16 or wider, within the bound.
No kernel may reach another device: no remote copies, remote signals or barrier semaphores. Data moves between devices by JAX's collectives and lax.ppermute only.
A program may use at most 128 MiB of HBM per device.

v0:
```python
import functools

import jax
import jax.numpy as jnp
from jax import lax
from jax.experimental import pallas as pl
from jax.experimental.pallas import tpu as pltpu
from jax.sharding import PartitionSpec as P

ITERS = 2
damping = 0.5
LANES = 128
VMEM_LIMIT = 32 * 1024 * 1024
f32, bf16, i32 = jnp.float32, jnp.bfloat16, jnp.int32


def dot(a, b):
    return jnp.dot(a, b, preferred_element_type=f32)


def hot_rows(column, first, width):
    offset = column - lax.broadcasted_iota(i32, column.shape, 1)
    tiles = [(offset == first + t).astype(f32).astype(bf16) for t in range(0, width, LANES)]
    return jnp.concatenate(tiles, axis=1)


def hot_cols(row, first, height):
    numbers = lax.broadcasted_iota(i32, (height, row.shape[1]), 0) + first
    return (numbers == row).astype(f32).astype(bf16)


def hot_pairs(column, row):
    tiles = [
        (column == row[:, t : t + LANES]).astype(f32).astype(bf16) for t in range(0, row.shape[1], LANES)
    ]
    return jnp.concatenate(tiles, axis=1)


def chunks(count, body, parts):
    size = count // parts
    for first in range(0, count, size):
        body(pl.ds(first, size), first)


def product(matrix_ref, vectors, out_ref):
    def rows(at, _):
        out_ref[0, at, :] = dot(matrix_ref[0, at, :], vectors)

    chunks(out_ref.shape[1], rows, 2)


def turned_dot(a, b):
    return lax.dot_general(a, b, (((0,), (0,)), ((), ())), preferred_element_type=f32)


def call(body, grid, in_specs, out_specs, out_shape, scratch, flops, moved, near=(), near_out=()):
    listed = isinstance(out_shape, (list, tuple))
    shapes = [
        (pltpu.VMEM if i in near_out else pltpu.HBM)(x.shape, x.dtype)
        for i, x in enumerate(out_shape if listed else [out_shape])
    ]
    shapes = shapes if listed else shapes[0]
    run = pl.pallas_call(
        body,
        grid=grid,
        in_specs=in_specs,
        out_specs=out_specs,
        out_shape=shapes,
        scratch_shapes=scratch,
        compiler_params=pltpu.CompilerParams(vmem_limit_bytes=VMEM_LIMIT),
        cost_estimate=pl.CostEstimate(flops=int(flops), bytes_accessed=int(moved), transcendentals=0),
    )

    def placed(i, x, spec):
        if spec.memory_space == pltpu.SMEM:
            return x
        return pltpu.with_memory_space_constraint(x, pltpu.VMEM if i in near else pltpu.HBM)

    return lambda *args: run(*(placed(i, x, spec) for i, (x, spec) in enumerate(zip(args, in_specs))))


def whole(shape):
    return pl.BlockSpec(shape, lambda s: (0,) * len(shape))


def open_body(field_ref, matrix_ref, part_ref):
    product(matrix_ref, field_ref[...].astype(bf16), part_ref)


def first_body(row_ref, field_ref, out_ref, column_ref, low):
    same = (
        lax.broadcasted_iota(i32, (LANES, LANES), 0) == lax.broadcasted_iota(i32, (LANES, LANES), 1)
    ).astype(f32)
    ones = jnp.ones((LANES, LANES), bf16)
    for t in range(0, row_ref.shape[1], LANES):
        number = row_ref[:, t : t + LANES]
        number = jnp.where(number < 0, -2, number) + 2
        high = number // LANES
        column = dot((same * high.astype(f32)).astype(bf16), ones) * LANES
        column += dot((same * (number - high * LANES).astype(f32)).astype(bf16), ones)
        column_ref[pl.ds(t, LANES), :] = column.astype(i32) - 2
    low[...] = field_ref[...].astype(bf16)

    def rows(at, _):
        out_ref[at, :] = dot(hot_rows(column_ref[at, :], 0, low.shape[0]), low[...]).astype(bf16)

    chunks(out_ref.shape[0], rows, 3)


def settle_body(sign, has_modes, base_ref, in_ref, row_ref, matrix_ref, *rest):
    if has_modes:
        modes_ref, part_ref, proj_ref, low = rest
    else:
        field_ref, part_ref, low = rest
    core = base_ref.shape[0]
    first = pl.program_id(0) * core

    def fields(at, c):
        added = dot(hot_cols(row_ref[...], first + c, at.size), in_ref[...])
        value = base_ref[at, :] + sign * added
        if not has_modes:
            field_ref[at, :] = value
        low[at, :] = value.astype(bf16)

    chunks(core, fields, 2)
    if has_modes:
        proj_ref[...] = dot(modes_ref[0], low[...])
    product(matrix_ref, low[...], part_ref)


def finish_body(sign, base_ref, in_ref, row_ref, field_ref):
    core = field_ref.shape[0]
    first = pl.program_id(0) * core

    def fields(at, c):
        added = dot(hot_cols(row_ref[...], first + c, at.size), in_ref[...])
        field_ref[at, :] = base_ref[at, :] + sign * added

    chunks(core, fields, 2)


def take_margins(in_ref, column_ref, margin_ref):
    def rows(at, _):
        hot = hot_rows(column_ref[at, :], 0, in_ref.shape[0])
        margin_ref[at, :] = dot(hot, in_ref[...]).astype(bf16)

    chunks(margin_ref.shape[0], rows, 2)


def pack(place_ref, outer, out_ref):
    def rows(at, c):
        out_ref[at, :] = dot(hot_cols(place_ref[...], c, at.size), outer[...]).astype(bf16)

    chunks(out_ref.shape[0], rows, 2)


def outer_body(in_ref, column_ref, place_ref, matrix_ref, part_ref, margin_ref, out_ref, outer):
    subs, margins, _ = matrix_ref.shape
    take_margins(in_ref, column_ref, margin_ref)
    for s in range(subs):
        taken = margin_ref[pl.ds(s * margins, margins), :]
        outer[pl.ds(s * margins, margins), :] = (part_ref[s] + dot(matrix_ref[s], taken)).astype(bf16)
    pack(place_ref, outer, out_ref)


def project_body(in_ref, column_ref, modes_ref, proj_ref, margin_ref, out_ref):
    subs, count, margins = modes_ref.shape
    take_margins(in_ref, column_ref, margin_ref)
    for s in range(subs):
        taken = margin_ref[pl.ds(s * margins, margins), :]
        at = pl.ds(s * count, count)
        out_ref[at, :] = (proj_ref[at, :] + dot(modes_ref[s], taken)).astype(bf16)


def split(x):
    high = x.astype(bf16)
    return jnp.concatenate([high, (x - high.astype(f32)).astype(bf16)], axis=1)


def both(x):
    half = x.shape[1] // 2
    return x[:, :half] + x[:, half:]


def coarse_body(side, here_ref, all_ref, *rest):
    inverse_refs = rest[:side]
    margin_ref, place_ref, matrix_ref, part_ref, modes_ref, coarse_ref, out_ref, outer = rest[side:]
    subs, count, margins = modes_ref.shape
    made = 0.0
    for k, inverse_ref in enumerate(inverse_refs):
        width = inverse_ref.shape[1]
        first = pl.multiple_of((here_ref[0] ^ k) * width, width)
        made += dot(inverse_ref[...], all_ref[pl.ds(first, width), :])
    coarse_ref[...] = made
    halves = split(made)
    for s in range(subs):
        at = pl.ds(s * margins, margins)
        solved = part_ref[s] + dot(matrix_ref[s], margin_ref[at, :])
        lifted = both(turned_dot(modes_ref[s], halves[s * count : (s + 1) * count]))
        outer[at, :] = (damping * solved + lifted).astype(bf16)
    pack(place_ref, outer, out_ref)


def inner_body(sign, has_modes, part_ref, matrix_ref, margin_ref, base_ref, column_ref, *rest):
    if has_modes:
        coarse_ref, modes_ref, new_ref, sent_ref, halves, total = rest
    else:
        new_ref, sent_ref, halves, total = rest
    s = pl.program_id(0)
    core = new_ref.shape[0]
    made = part_ref[0] + dot(matrix_ref[0], margin_ref[...])
    if has_modes:
        made = damping * made + both(turned_dot(modes_ref[0], split(coarse_ref[...])))
    value = base_ref[...] + sign * made
    new_ref[...] = value
    halves[...] = split(value)

    @pl.when(s == 0)
    def _():
        total[...] = jnp.zeros_like(total)

    def rows(at, _):
        total[at, :] += dot(hot_rows(column_ref[at, :], s * core, core), halves[...])

    chunks(total.shape[0], rows, 2)

    @pl.when(s == pl.num_programs(0) - 1)
    def _():
        sent_ref[...] = both(total[...])


def relay_body(sign, sent_ref, in_ref, column_ref, row_ref, out_ref):
    def rows(at, _):
        added = dot(hot_pairs(column_ref[at, :], row_ref[...]), in_ref[...])
        out_ref[at, :] = (sent_ref[at, :] + sign * added).astype(bf16)

    chunks(out_ref.shape[0], rows, 2)


def shards(loads, start, stiffness, local_inverse, modes, coarse_inverse, margin_rows):
    owners = lax.axis_size("wide")
    subs, margins = margin_rows.shape
    order = stiffness.shape[1]
    core = order - margins
    held, cols = loads.shape
    count = modes.shape[2]
    coarse_rows = subs * count
    capacity = 3 * subs * margins // (2 * owners)
    slots = owners * capacity
    many = subs * margins
    m_at = core // margins

    flat = margin_rows.reshape(-1)
    source = flat // held
    row = flat - source * held
    onehot = (source[:, None] == jnp.arange(owners, dtype=i32)[None, :]).astype(bf16)
    earlier = (jnp.arange(many)[:, None] > jnp.arange(many)[None, :]).astype(bf16)
    rank = jnp.sum(dot(earlier, onehot) * onehot.astype(f32), axis=1).astype(i32)
    place = source * capacity + rank
    hit = place[:, None] == jnp.arange(slots, dtype=i32)[None, :]
    asked = jnp.sum(jnp.where(hit, row[:, None] + 1, 0), axis=0) - 1

    def trade(x):
        blocks = x.reshape((owners, x.shape[0] // owners) + x.shape[1:])
        got = lax.all_to_all(blocks, "wide", split_axis=0, concat_axis=0, tiled=True)
        return got.reshape(x.shape)

    wanted = trade(asked)
    wanted_row = wanted[None, :]
    place_row = place[None, :]
    place_column = jnp.broadcast_to(place[:, None], (many, LANES))
    wanted_row, place_column = lax.optimization_barrier((wanted_row, place_column))
    modes_turned = jnp.swapaxes(modes, 1, 2)

    rows_spec = pl.BlockSpec((core, cols), lambda s: (s, 0))
    left_spec = pl.BlockSpec((1, order, core), lambda s: (s, 0, 0))
    part_spec = pl.BlockSpec((1, order, cols), lambda s: (s, 0, 0))
    slots_spec = whole((slots, cols))
    held_shape = jax.ShapeDtypeStruct((held, cols), f32)
    part_shape = jax.ShapeDtypeStruct((subs, order, cols), f32)
    slots_low = jax.ShapeDtypeStruct((slots, cols), bf16)
    margin_shape = jax.ShapeDtypeStruct((many, cols), bf16)
    matrix_flops = 2 * subs * order * core * cols
    slot_flops = 2 * held * slots * cols

    going, wanted_column = call(
        first_body, (1,), [whole((1, slots)), whole((held, cols))], [slots_spec, whole((slots, LANES))],
        [slots_low, jax.ShapeDtypeStruct((slots, LANES), i32)], [pltpu.VMEM((held, cols), bf16)],
        slot_flops, 2e6, (0,), (1,),
    )(wanted_row, start)
    begun, own, going = lax.optimization_barrier((start, coarse_inverse.astype(bf16), going))
    part = call(
        open_body, (subs,), [rows_spec, left_spec], part_spec, part_shape, [], matrix_flops, 10e6,
    )(begun, stiffness)

    side = lax.axis_size("narrow")
    here = lax.axis_index("narrow").reshape(1).astype(i32)
    pieces = [own] + [
        lax.ppermute(own, "narrow", [(i, i ^ k) for i in range(side)]) for k in range(1, side)
    ]
    core_modes_spec = pl.BlockSpec((1, count, core), lambda s: (s, 0, 0))
    outer_modes_spec = pl.BlockSpec((subs, count, margins), lambda s: (0, 0, m_at))

    def settle(sign, base, came, matrices, has_modes):
        specs = [rows_spec, slots_spec, whole((1, slots)), left_spec]
        args = [base, came, wanted_row, matrices]
        outs, shapes = [rows_spec, part_spec], [held_shape, part_shape]
        if has_modes:
            specs.append(core_modes_spec)
            args.append(modes_turned)
            outs = [part_spec, pl.BlockSpec((count, cols), lambda s: (s, 0))]
            shapes = [part_shape, jax.ShapeDtypeStruct((coarse_rows, cols), f32)]
        return call(
            functools.partial(settle_body, sign, has_modes), (subs,), specs, outs, shapes,
            [pltpu.VMEM((core, cols), bf16)], slot_flops + matrix_flops, 14e6, (1, 2),
            (),
        )(*args)

    corner_spec = pl.BlockSpec((subs, margins, margins), lambda s: (0, m_at, m_at))
    part_outer_spec = pl.BlockSpec((subs, margins, cols), lambda s: (0, m_at, 0))
    outer_scratch = [pltpu.VMEM((many, cols), bf16)]

    def inner(sign, base, margin, part, matrices, coarse):
        specs = [
            pl.BlockSpec((1, core, cols), lambda s: (s, 0, 0)),
            pl.BlockSpec((1, core, margins), lambda s: (s, 0, m_at)),
            pl.BlockSpec((margins, cols), lambda s: (s, 0)),
            rows_spec,
            whole((slots, LANES)),
        ]
        args = [part, matrices, margin, base, wanted_column]
        if coarse is not None:
            specs += [
                pl.BlockSpec((count, cols), lambda s: (s, 0)),
                core_modes_spec,
            ]
            args += [coarse, modes_turned]
        return call(
            functools.partial(inner_body, sign, coarse is not None), (subs,), specs, [rows_spec, slots_spec],
            [held_shape, jax.ShapeDtypeStruct((slots, cols), f32)],
            [pltpu.VMEM((core, 2 * cols), bf16), pltpu.VMEM((slots, 2 * cols), f32)], 2 * slot_flops, 8e6,
            (4,), (1,),
        )(*args)

    def relay(sign, sent, came):
        return call(
            functools.partial(relay_body, sign), (1,),
            [slots_spec, slots_spec, whole((slots, LANES)), whole((1, slots))], slots_spec, slots_low, [],
            slot_flops // 2, 3e6, (0, 1, 2, 3),
        )(sent, came, wanted_column, wanted_row)

    def stiffness_outer(came, part):
        return call(
            outer_body, (1,),
            [slots_spec, whole((many, LANES)), whole((1, many)), corner_spec, part_outer_spec],
            [whole((many, cols)), slots_spec], [margin_shape, slots_low], outer_scratch, slot_flops, 3e6,
            (0,),
        )(came, place_column, place_row, stiffness, part)

    field = start
    for step in range(ITERS + 1):
        came = trade(going)
        if step == 0:
            pieces, came = lax.optimization_barrier((pieces, came))
        else:
            field, part = settle(1.0, base, back, stiffness, False)
        margin, going = stiffness_outer(came, part)
        back = trade(going)
        base, sent = inner(-1.0, loads, margin, part, stiffness, None)
        if step == ITERS:
            break

        going = relay(-1.0, sent, back)
        came = trade(going)
        part, proj = settle(-1.0, base, back, local_inverse, True)
        margin, projection = call(
            project_body, (1,),
            [slots_spec, whole((many, LANES)), outer_modes_spec, whole((coarse_rows, cols))],
            [whole((many, cols)), whole((coarse_rows, cols))],
            [margin_shape, jax.ShapeDtypeStruct((coarse_rows, cols), bf16)], [], slot_flops // 2, 2e6,
            (0,),
        )(came, place_column, modes_turned, proj)
        everyone = lax.all_gather(projection, "wide", axis=0, tiled=True)
        coarse, going = call(
            functools.partial(coarse_body, side), (1,),
            [pl.BlockSpec(memory_space=pltpu.SMEM), whole((owners * coarse_rows, cols))]
            + [whole(coarse_inverse.shape)] * side
            + [
                whole((many, cols)),
                whole((1, many)),
                corner_spec,
                part_outer_spec,
                outer_modes_spec,
            ],
            [whole((coarse_rows, cols)), slots_spec],
            [jax.ShapeDtypeStruct((coarse_rows, cols), f32), slots_low], outer_scratch, slot_flops, 3e6,
            (1,),
        )(here, everyone, *pieces, margin, place_row, local_inverse, part, modes_turned)
        back = trade(going)
        base, sent = inner(1.0, field, margin, part, local_inverse, coarse)
        going = relay(1.0, sent, back)

    final = call(
        functools.partial(finish_body, -1.0), (subs,), [rows_spec, slots_spec, whole((1, slots))], rows_spec,
        held_shape, [], slot_flops, 4e6, (1, 2),
    )(base, back, wanted_row)
    return field, final


def solution(mesh):
    placed = (
        P("wide", "narrow"),
        P("wide", "narrow"),
        P("wide", None, None),
        P("wide", None, None),
        P("wide", None, None),
        P("wide", "narrow"),
        P("wide", None),
    )
    return jax.shard_map(
        shards,
        mesh=mesh,
        in_specs=placed,
        out_specs=(P("wide", "narrow"), P("wide", "narrow")),
        check_vma=False,
    )
```

profile of v0, /device:TPU:0, one launch (start us, length us, event | category | flops | bytes accessed | tf_op | source)
XLA Modules:
  0.0 200.4 jit_solution(8992581223722938373)
XLA Ops:
  0.6 0.7 copy.9
  1.3 0.5 fusion.2
  1.8 0.8 select_reduce_fusion
  2.7 0.7 sub.24
  3.4 5.2 %all-to-all-start = ((s32[8,1,192]{2,1,0:T(1,128)}), s32[8,1,192]{2,1,0:T(1,128)S(1)}, u32[]{:S(2)}, u32[]{:S(2)}) async-start(s32[8,1,192]{2,1,0:T(1,128)} %sub.24), calls=%async_computation | async-start | bytes 16384 | tf_op jit(solution)/shard_map/all_to_all | solution.py:265
  8.5 0.7 divide_bitcast_fusion
  9.2 0.9 convert_element_type.27.rest_0_
  10.1 3.1 %all-to-all-done = s32[8,1,192]{2,1,0:T(1,128)S(1)} async-done(((s32[8,1,192]{2,1,0:T(1,128)}), s32[8,1,192]{2,1,0:T(1,128)S(1)}, u32[]{:S(2)}, u32[]{:S(2)}) %all-to-all-start) | async-done | bytes 6176 | tf_op jit(solution)/shard_map/all_to_all | solution.py:265
  13.3 0.1 broadcast_in_dim_reshape.3.row_ref
  13.3 1.0 broadcast_in_dim.16.column_ref
  14.3 5.0 %shard_map.86 = (bf16[1536,128]{1,0:T(8,128)(2,1)}, s32[1536,128]{1,0:T(8,128)S(1)}) custom-call(s32[1,1536]{1,0:T(1,128)S(1)} %broadcast_in_dim_reshape.3.row_ref, f32[3072,128]{1,0:T(8,128)} %base_ref.5), custom_call_target="tpu_custom_call" | custom-call | flops 1207959552 | bytes 2000000 | tf_op jit(solution)/shard_map/pallas_call | solution.py:79
  19.4 3.5 %all-to-all-start.1 = ((bf16[8,192,128]{2,1,0:T(8,128)(2,1)}), bf16[8,192,128]{2,1,0:T(8,128)(2,1)S(1)}, u32[]{:S(2)}, u32[]{:S(2)}) async-start(bf16[8,192,128]{2,1,0:T(8,128)(2,1)} %bitcast.59), calls=%async_computation.1 | async-start | bytes 786432 | tf_op jit(solution)/shard_map/all_to_all | solution.py:265
  22.9 0.0 copy-done.4
  22.9 0.6 fusion.6.place_ref.rest_5_
  23.5 3.6 %collective-permute-start.2 = (bf16[128,256]{1,0:T(8,128)(2,1)S(1)}, bf16[128,256]{1,0:T(8,128)(2,1)S(1)}, u32[]{:S(2)}, u32[]{:S(2)}) collective-permute-start(bf16[128,256]{1,0:T(8,128)(2,1)S(1)} %convert_element_type.27.rest_0_), channel_id=1, source_target_pairs={{0,3},{1,2},{2,1},{3,0},{4,7},{5,6},{6,5},{7,4},{8,11},{9,10},{10,... | collective-permute-start | bytes 196616 | tf_op jit(solution)/shard_map/ppermute | solution.py:299
  27.2 0.0 collective-permute-start.1
  27.2 0.0 copy-done
  27.2 0.8 collective-permute-start
  27.9 6.1 %shard_map.87.part_ref = f32[4,1024,128]{2,1,0:T(8,128)} custom-call(f32[3072,128]{1,0:T(8,128)} %base_ref.5, bf16[4,1024,1024]{2,1,0:T(8,128)(2,1)} %matrix_ref.25), custom_call_target="tpu_custom_call" | custom-call | flops 805306368 | bytes 10000000 | tf_op jit(solution)/shard_map/pallas_call | solution.py:79
  34.0 0.0 collective-permute-done.2.rest_3_
  34.0 0.0 collective-permute-done.1.rest_2_
  34.0 0.0 collective-permute-done.rest_1_
  34.1 0.0 all-to-all-done.1
  34.1 4.3 %shard_map.88 = (bf16[1024,128]{1,0:T(8,128)(2,1)}, bf16[1536,128]{1,0:T(8,128)(2,1)}) custom-call(bf16[1536,128]{1,0:T(8,128)(2,1)S(1)} %bitcast.41, s32[1024,128]{1,0:T(8,128)} %broadcast_in_dim.16.column_ref, s32[1,1024]{1,0:T(1,128)} %fusion.6.place_ref.rest_5_, bf16[4,1024,1024]{2,1,0:T(8,128)(2,1)} %matrix_ref.25, f32[4,1024,128]{2,1,0:T(8,128)} %shard_map.87.part_ref), custom_call_target="tpu_custom_call" | custom-call | flops 1207959552 | bytes 3000000 | tf_op jit(solution)/shard_map/pallas_call | solution.py:79
  38.4 4.1 %all-to-all-start.2 = ((bf16[8,192,128]{2,1,0:T(8,128)(2,1)}), bf16[8,192,128]{2,1,0:T(8,128)(2,1)S(1)}, u32[]{:S(2)}, u32[]{:S(2)}) async-start(bf16[8,192,128]{2,1,0:T(8,128)(2,1)} %bitcast.62), calls=%async_computation.2 | async-start | bytes 786432 | tf_op jit(solution)/shard_map/all_to_all | solution.py:265
  42.5 6.9 %shard_map.89 = (f32[3072,128]{1,0:T(8,128)}, f32[1536,128]{1,0:T(8,128)S(1)}) custom-call(f32[4,1024,128]{2,1,0:T(8,128)} %shard_map.87.part_ref, bf16[4,1024,1024]{2,1,0:T(8,128)(2,1)} %matrix_ref.25, bf16[1024,128]{1,0:T(8,128)(2,1)} %get-tuple-element.52.margin_ref, f32[3072,128]{1,0:T(8,128)} %base_ref.7, s32[1536,128]{1,0:T(8,128)S(1)} %get-tuple-element.53.column_ref), custom_call_target="tpu_custom_call" | custom-call | flops 2415919104 | bytes 8000000 | tf_op jit(solution)/shard_map/pallas_call | solution.py:79
  49.3 1.5 all-to-all-done.2
  50.8 2.1 %shard_map.91 = bf16[1536,128]{1,0:T(8,128)(2,1)} custom-call(f32[1536,128]{1,0:T(8,128)S(1)} %get-tuple-element.57.sent_ref, bf16[1536,128]{1,0:T(8,128)(2,1)S(1)} %bitcast.33, s32[1536,128]{1,0:T(8,128)S(1)} %get-tuple-element.53.column_ref, s32[1,1536]{1,0:T(1,128)S(1)} %broadcast_in_dim_reshape.3.row_ref), custom_call_target="tpu_custom_call" | custom-call | flops 603979776 | bytes 3000000 | tf_op jit(solution)/shard_map/pallas_call | solution.py:79
  53.0 3.5 %all-to-all-start.3 = ((bf16[8,192,128]{2,1,0:T(8,128)(2,1)}), bf16[8,192,128]{2,1,0:T(8,128)(2,1)S(1)}, u32[]{:S(2)}, u32[]{:S(2)}) async-start(bf16[8,192,128]{2,1,0:T(8,128)(2,1)} %bitcast.55), calls=%async_computation.3 | async-start | bytes 786432 | tf_op jit(solution)/shard_map/all_to_all | solution.py:265
  56.4 8.3 %shard_map.90 = (f32[4,1024,128]{2,1,0:T(8,128)}, f32[128,128]{1,0:T(8,128)}) custom-call(f32[3072,128]{1,0:T(8,128)} %get-tuple-element.54.base_ref, bf16[1536,128]{1,0:T(8,128)(2,1)S(1)} %bitcast.34, s32[1,1536]{1,0:T(1,128)S(1)} %broadcast_in_dim_reshape.3.row_ref, bf16[4,1024,1024]{2,1,0:T(8,128)(2,1)} %matrix_ref.22, bf16[4,32,1024]{2,1,0:T(8,128)(2,1)} %bitcast.47), custom_call_target="tpu_custom_call" | custom-call | flops 2013265920 | bytes 14000000 | tf_op jit(solution)/shard_map/pallas_call | solution.py:79
  64.7 0.0 all-to-all-done.3
  64.7 2.8 %shard_map.92 = (bf16[1024,128]{1,0:T(8,128)(2,1)}, bf16[128,128]{1,0:T(8,128)(2,1)}) custom-call(bf16[1536,128]{1,0:T(8,128)(2,1)S(1)} %bitcast.44, s32[1024,128]{1,0:T(8,128)} %broadcast_in_dim.16.column_ref, bf16[4,32,1024]{2,1,0:T(8,128)(2,1)} %bitcast.48, f32[128,128]{1,0:T(8,128)} %get-tuple-element.58.proj_ref), custom_call_target="tpu_custom_call" | custom-call | flops 603979776 | bytes 2000000 | tf_op jit(solution)/shard_map/pallas_call | solution.py:79
  67.5 9.9 %all_gather.6.all_ref = bf16[1024,128]{1,0:T(8,128)(2,1)S(1)} all-gather(bf16[128,128]{1,0:T(8,128)(2,1)} %get-tuple-element.60), channel_id=1, replica_groups=mesh['wide'=8,'narrow'=4] {'wide'}, dimensions={0}, use_global_device_ids=true | all-gather | bytes 294912 | tf_op jit(solution)/shard_map/all_gather | solution.py:383
  77.4 3.6 %shard_map.93 = (f32[128,128]{1,0:T(8,128)}, bf16[1536,128]{1,0:T(8,128)(2,1)}) custom-call(s32[1]{0:T(128)} %bitcast.8.here_ref, bf16[1024,128]{1,0:T(8,128)(2,1)S(1)} %all_gather.6.all_ref, bf16[128,256]{1,0:T(8,128)(2,1)} %copy-done, bf16[128,256]{1,0:T(8,128)(2,1)} %copy-done.3, bf16[128,256]{1,0:T(8,128)(2,1)} %copy-done.2, bf16[128,256]{1,0:T(8,128)(2,1)} %copy-done.1, ...), custom_call_target="tpu_custom_call" | custom-call | flops 1207959552 | bytes 3000000 | tf_op jit(solution)/shard_map/pallas_call | solution.py:79
  81.1 3.6 %all-to-all-start.4 = ((bf16[8,192,128]{2,1,0:T(8,128)(2,1)}), bf16[8,192,128]{2,1,0:T(8,128)(2,1)S(1)}, u32[]{:S(2)}, u32[]{:S(2)}) async-start(bf16[8,192,128]{2,1,0:T(8,128)(2,1)} %bitcast.63), calls=%async_computation.4 | async-start | bytes 786432 | tf_op jit(solution)/shard_map/all_to_all | solution.py:265
  84.7 7.2 %shard_map.94 = (f32[3072,128]{1,0:T(8,128)}, f32[1536,128]{1,0:T(8,128)S(1)}) custom-call(f32[4,1024,128]{2,1,0:T(8,128)} %get-tuple-element.56.rest_7_.part_ref, bf16[4,1024,1024]{2,1,0:T(8,128)(2,1)} %matrix_ref.22, bf16[1024,128]{1,0:T(8,128)(2,1)} %get-tuple-element.59.rest_4_.margin_ref, f32[3072,128]{1,0:T(8,128)} %base_ref.5, ...), custom_call_target="tpu_custom_call" | custom-call | flops 2415919104 | bytes 8000000 | tf_op jit(solution)/shard_map/pallas_call | solution.py:79
  91.9 0.9 all-to-all-done.4
  92.8 2.2 %shard_map.96 = bf16[1536,128]{1,0:T(8,128)(2,1)} custom-call(f32[1536,128]{1,0:T(8,128)S(1)} %get-tuple-element.69.sent_ref, bf16[1536,128]{1,0:T(8,128)(2,1)S(1)} %bitcast.39, s32[1536,128]{1,0:T(8,128)S(1)} %get-tuple-element.53.column_ref, s32[1,1536]{1,0:T(1,128)S(1)} %broadcast_in_dim_reshape.3.row_ref), custom_call_target="tpu_custom_call" | custom-call | flops 603979776 | bytes 3000000 | tf_op jit(solution)/shard_map/pallas_call | solution.py:79
  95.0 3.5 %all-to-all-start.5 = ((bf16[8,192,128]{2,1,0:T(8,128)(2,1)}), bf16[8,192,128]{2,1,0:T(8,128)(2,1)S(1)}, u32[]{:S(2)}, u32[]{:S(2)}) async-start(bf16[8,192,128]{2,1,0:T(8,128)(2,1)} %bitcast.56), calls=%async_computation.5 | async-start | bytes 786432 | tf_op jit(solution)/shard_map/all_to_all | solution.py:265
  98.4 7.8 %shard_map.95 = (f32[3072,128]{1,0:T(8,128)}, f32[4,1024,128]{2,1,0:T(8,128)}) custom-call(f32[3072,128]{1,0:T(8,128)} %get-tuple-element.66.base_ref, bf16[1536,128]{1,0:T(8,128)(2,1)S(1)} %bitcast.40, s32[1,1536]{1,0:T(1,128)S(1)} %broadcast_in_dim_reshape.3.row_ref, bf16[4,1024,1024]{2,1,0:T(8,128)(2,1)} %matrix_ref.25), custom_call_target="tpu_custom_call" | custom-call | flops 2013265920 | bytes 14000000 | tf_op jit(solution)/shard_map/pallas_call | solution.py:79
  106.2 0.4 all-to-all-done.5
  106.7 4.3 %shard_map.97 = (bf16[1024,128]{1,0:T(8,128)(2,1)}, bf16[1536,128]{1,0:T(8,128)(2,1)}) custom-call(bf16[1536,128]{1,0:T(8,128)(2,1)S(1)} %bitcast.43, s32[1024,128]{1,0:T(8,128)} %broadcast_in_dim.16.column_ref, s32[1,1024]{1,0:T(1,128)} %fusion.6.place_ref.rest_5_, bf16[4,1024,1024]{2,1,0:T(8,128)(2,1)} %matrix_ref.25, ...), custom_call_target="tpu_custom_call" | custom-call | flops 1207959552 | bytes 3000000 | tf_op jit(solution)/shard_map/pallas_call | solution.py:79
  110.9 3.7 %all-to-all-start.6 = ((bf16[8,192,128]{2,1,0:T(8,128)(2,1)}), bf16[8,192,128]{2,1,0:T(8,128)(2,1)S(1)}, u32[]{:S(2)}, u32[]{:S(2)}) async-start(bf16[8,192,128]{2,1,0:T(8,128)(2,1)} %bitcast.64), calls=%async_computation.6 | async-start | bytes 786432 | tf_op jit(solution)/shard_map/all_to_all | solution.py:265
  114.6 6.8 %shard_map.98 = (f32[3072,128]{1,0:T(8,128)}, f32[1536,128]{1,0:T(8,128)S(1)}) custom-call(f32[4,1024,128]{2,1,0:T(8,128)} %get-tuple-element.68.part_ref, bf16[4,1024,1024]{2,1,0:T(8,128)(2,1)} %matrix_ref.25, bf16[1024,128]{1,0:T(8,128)(2,1)} %get-tuple-element.70.margin_ref, f32[3072,128]{1,0:T(8,128)} %base_ref.7, ...), custom_call_target="tpu_custom_call" | custom-call | flops 2415919104 | bytes 8000000 | tf_op jit(solution)/shard_map/pallas_call | solution.py:79
  121.5 1.5 all-to-all-done.6
  123.0 2.1 %shard_map.100 = bf16[1536,128]{1,0:T(8,128)(2,1)} custom-call(f32[1536,128]{1,0:T(8,128)S(1)} %get-tuple-element.74.sent_ref, bf16[1536,128]{1,0:T(8,128)(2,1)S(1)} %bitcast.35, s32[1536,128]{1,0:T(8,128)S(1)} %get-tuple-element.53.column_ref, s32[1,1536]{1,0:T(1,128)S(1)} %broadcast_in_dim_reshape.3.row_ref), custom_call_target="tpu_custom_call" | custom-call | flops 603979776 | bytes 3000000 | tf_op jit(solution)/shard_map/pallas_call | solution.py:79
  125.1 3.5 %all-to-all-start.7 = ((bf16[8,192,128]{2,1,0:T(8,128)(2,1)}), bf16[8,192,128]{2,1,0:T(8,128)(2,1)S(1)}, u32[]{:S(2)}, u32[]{:S(2)}) async-start(bf16[8,192,128]{2,1,0:T(8,128)(2,1)} %bitcast.57), calls=%async_computation.7 | async-start | bytes 786432 | tf_op jit(solution)/shard_map/all_to_all | solution.py:265
  128.6 8.3 %shard_map.99 = (f32[4,1024,128]{2,1,0:T(8,128)}, f32[128,128]{1,0:T(8,128)}) custom-call(f32[3072,128]{1,0:T(8,128)} %get-tuple-element.71.base_ref, bf16[1536,128]{1,0:T(8,128)(2,1)S(1)} %bitcast.36, s32[1,1536]{1,0:T(1,128)S(1)} %broadcast_in_dim_reshape.3.row_ref, bf16[4,1024,1024]{2,1,0:T(8,128)(2,1)} %matrix_ref.22, bf16[4,32,1024]{2,1,0:T(8,128)(2,1)} %bitcast.51), custom_call_target="tpu_custom_call" | custom-call | flops 2013265920 | bytes 14000000 | tf_op jit(solution)/shard_map/pallas_call | solution.py:79
  136.8 0.0 all-to-all-done.7
  136.8 2.8 %shard_map.101 = (bf16[1024,128]{1,0:T(8,128)(2,1)}, bf16[128,128]{1,0:T(8,128)(2,1)}) custom-call(bf16[1536,128]{1,0:T(8,128)(2,1)S(1)} %bitcast.46, s32[1024,128]{1,0:T(8,128)} %broadcast_in_dim.16.column_ref, bf16[4,32,1024]{2,1,0:T(8,128)(2,1)} %bitcast.52, f32[128,128]{1,0:T(8,128)} %get-tuple-element.75.proj_ref), custom_call_target="tpu_custom_call" | custom-call | flops 603979776 | bytes 2000000 | tf_op jit(solution)/shard_map/pallas_call | solution.py:79
  139.7 9.9 %all_gather.7.all_ref = bf16[1024,128]{1,0:T(8,128)(2,1)S(1)} all-gather(bf16[128,128]{1,0:T(8,128)(2,1)} %get-tuple-element.78), channel_id=1, replica_groups=mesh['wide'=8,'narrow'=4] {'wide'}, dimensions={0}, use_global_device_ids=true | all-gather | bytes 294912 | tf_op jit(solution)/shard_map/all_gather | solution.py:383
  149.6 3.6 %shard_map.102 = (f32[128,128]{1,0:T(8,128)}, bf16[1536,128]{1,0:T(8,128)(2,1)}) custom-call(s32[1]{0:T(128)} %bitcast.8.here_ref, bf16[1024,128]{1,0:T(8,128)(2,1)S(1)} %all_gather.7.all_ref, bf16[128,256]{1,0:T(8,128)(2,1)} %copy-done, bf16[128,256]{1,0:T(8,128)(2,1)} %copy-done.3, bf16[128,256]{1,0:T(8,128)(2,1)} %copy-done.2, ...), custom_call_target="tpu_custom_call" | custom-call | flops 1207959552 | bytes 3000000 | tf_op jit(solution)/shard_map/pallas_call | solution.py:79
  153.2 3.7 %all-to-all-start.8 = ((bf16[8,192,128]{2,1,0:T(8,128)(2,1)}), bf16[8,192,128]{2,1,0:T(8,128)(2,1)S(1)}, u32[]{:S(2)}, u32[]{:S(2)}) async-start(bf16[8,192,128]{2,1,0:T(8,128)(2,1)} %bitcast.60), calls=%async_computation.8 | async-start | bytes 786432 | tf_op jit(solution)/shard_map/all_to_all | solution.py:265
  156.9 7.2 %shard_map.103 = (f32[3072,128]{1,0:T(8,128)}, f32[1536,128]{1,0:T(8,128)S(1)}) custom-call(f32[4,1024,128]{2,1,0:T(8,128)} %get-tuple-element.73.rest_7_.part_ref, bf16[4,1024,1024]{2,1,0:T(8,128)(2,1)} %matrix_ref.22, bf16[1024,128]{1,0:T(8,128)(2,1)} %get-tuple-element.76.rest_4_.margin_ref, f32[3072,128]{1,0:T(8,128)} %get-tuple-element.77.base_ref, ...), custom_call_target="tpu_custom_call" | custom-call | flops 2415919104 | bytes 8000000 | tf_op jit(solution)/shard_map/pallas_call | solution.py:79
  164.1 0.8 all-to-all-done.8
  165.0 2.2 %shard_map.105 = bf16[1536,128]{1,0:T(8,128)(2,1)} custom-call(f32[1536,128]{1,0:T(8,128)S(1)} %get-tuple-element.84.sent_ref, bf16[1536,128]{1,0:T(8,128)(2,1)S(1)} %bitcast.37, s32[1536,128]{1,0:T(8,128)S(1)} %get-tuple-element.53.column_ref, s32[1,1536]{1,0:T(1,128)S(1)} %broadcast_in_dim_reshape.3.row_ref), custom_call_target="tpu_custom_call" | custom-call | flops 603979776 | bytes 3000000 | tf_op jit(solution)/shard_map/pallas_call | solution.py:79
  167.1 3.5 %all-to-all-start.9 = ((bf16[8,192,128]{2,1,0:T(8,128)(2,1)}), bf16[8,192,128]{2,1,0:T(8,128)(2,1)S(1)}, u32[]{:S(2)}, u32[]{:S(2)}) async-start(bf16[8,192,128]{2,1,0:T(8,128)(2,1)} %bitcast.58), calls=%async_computation.9 | async-start | bytes 786432 | tf_op jit(solution)/shard_map/all_to_all | solution.py:265
  170.6 7.8 %shard_map.104 = (f32[3072,128]{1,0:T(8,128)}, f32[4,1024,128]{2,1,0:T(8,128)}) custom-call(f32[3072,128]{1,0:T(8,128)} %get-tuple-element.80.base_ref, bf16[1536,128]{1,0:T(8,128)(2,1)S(1)} %bitcast.38, s32[1,1536]{1,0:T(1,128)S(1)} %broadcast_in_dim_reshape.3.row_ref, bf16[4,1024,1024]{2,1,0:T(8,128)(2,1)} %matrix_ref.25), custom_call_target="tpu_custom_call" | custom-call | flops 2013265920 | bytes 14000000 | tf_op jit(solution)/shard_map/pallas_call | solution.py:79
  178.4 0.4 all-to-all-done.9
  178.8 4.2 %shard_map.106 = (bf16[1024,128]{1,0:T(8,128)(2,1)}, bf16[1536,128]{1,0:T(8,128)(2,1)}) custom-call(bf16[1536,128]{1,0:T(8,128)(2,1)S(1)} %bitcast.42, s32[1024,128]{1,0:T(8,128)} %broadcast_in_dim.16.column_ref, s32[1,1024]{1,0:T(1,128)} %fusion.6.place_ref.rest_5_, bf16[4,1024,1024]{2,1,0:T(8,128)(2,1)} %matrix_ref.25, ...), custom_call_target="tpu_custom_call" | custom-call | flops 1207959552 | bytes 3000000 | tf_op jit(solution)/shard_map/pallas_call | solution.py:79
  183.1 3.7 %all-to-all-start.10 = ((bf16[8,192,128]{2,1,0:T(8,128)(2,1)}), bf16[8,192,128]{2,1,0:T(8,128)(2,1)S(1)}, u32[]{:S(2)}, u32[]{:S(2)}) async-start(bf16[8,192,128]{2,1,0:T(8,128)(2,1)} %bitcast.61), calls=%async_computation.10 | async-start | bytes 786432 | tf_op jit(solution)/shard_map/all_to_all | solution.py:265
  186.8 7.1 %shard_map.107 = (f32[3072,128]{1,0:T(8,128)}, f32[1536,128]{1,0:T(8,128)}) custom-call(f32[4,1024,128]{2,1,0:T(8,128)} %get-tuple-element.83.part_ref, bf16[4,1024,1024]{2,1,0:T(8,128)(2,1)} %matrix_ref.25, bf16[1024,128]{1,0:T(8,128)(2,1)} %get-tuple-element.85.margin_ref, f32[3072,128]{1,0:T(8,128)} %base_ref.7, s32[1536,128]{1,0:T(8,128)S(1)} %get-tuple-element.53.column_ref), custom_call_target="tpu_custom_call" | custom-call | flops 2415919104 | bytes 8000000 | tf_op jit(solution)/shard_map/pallas_call | solution.py:79
  193.9 1.2 all-to-all-done.10
  195.1 5.3 %shard_map.108 = f32[3072,128]{1,0:T(8,128)} custom-call(f32[3072,128]{1,0:T(8,128)} %get-tuple-element.86.base_ref, bf16[1536,128]{1,0:T(8,128)(2,1)S(1)} %bitcast.45, s32[1,1536]{1,0:T(1,128)S(1)} %broadcast_in_dim_reshape.3.row_ref), custom_call_target="tpu_custom_call" | custom-call | flops 1207959552 | bytes 4000000 | tf_op jit(solution)/shard_map/pallas_call | solution.py:79
  (16 shorter events, 0.1 us)
Async XLA Ops:
  3.4 9.9 %all-to-all-start = ((s32[8,1,192]{2,1,0:T(1,128)}), s32[8,1,192]{2,1,0:T(1,128)S(1)}, u32[]{:S(2)}, u32[]{:S(2)}) async-start(s32[8,1,192]{2,1,0:T(1,128)} %sub.24), calls=%async_computation | async-start | bytes 16384 | tf_op jit(solution)/shard_map/all_to_all | solution.py:265
  10.1 17.0 %copy-start = (bf16[128,256]{1,0:T(8,128)(2,1)}, bf16[128,256]{1,0:T(8,128)(2,1)S(1)}, u32[]{:S(2)}) copy-start(bf16[128,256]{1,0:T(8,128)(2,1)S(1)} %convert_element_type.27.rest_0_) | copy-start | bytes 196612
  14.3 8.5 %copy-start.4 = (s32[4,256]{1,0:T(4,128)S(1)}, s32[4,256]{1,0:T(4,128)}, u32[]{:S(2)}) copy-start(s32[4,256]{1,0:T(4,128)} %param.13) | copy-start | bytes 12292
  19.4 14.7 %all-to-all-start.1 = ((bf16[8,192,128]{2,1,0:T(8,128)(2,1)}), bf16[8,192,128]{2,1,0:T(8,128)(2,1)S(1)}, u32[]{:S(2)}, u32[]{:S(2)}) async-start(bf16[8,192,128]{2,1,0:T(8,128)(2,1)} %bitcast.59), calls=%async_computation.1 | async-start | bytes 786432 | tf_op jit(solution)/shard_map/all_to_all | solution.py:265
  23.5 10.5 %collective-permute-start.2 = (bf16[128,256]{1,0:T(8,128)(2,1)S(1)}, bf16[128,256]{1,0:T(8,128)(2,1)S(1)}, u32[]{:S(2)}, u32[]{:S(2)}) collective-permute-start(bf16[128,256]{1,0:T(8,128)(2,1)S(1)} %convert_element_type.27.rest_0_), channel_id=1, source_target_pairs={{0,3},{1,2},{2,1},{3,0},{4,7},{5,6},{6,5},{7,4},{8,11},{9,10},{10,... | collective-permute-start | bytes 196616 | tf_op jit(solution)/shard_map/ppermute | solution.py:299
  27.2 6.9 %collective-permute-start.1 = (bf16[128,256]{1,0:T(8,128)(2,1)S(1)}, bf16[128,256]{1,0:T(8,128)(2,1)S(1)}, u32[]{:S(2)}, u32[]{:S(2)}) collective-permute-start(bf16[128,256]{1,0:T(8,128)(2,1)S(1)} %convert_element_type.27.rest_0_), channel_id=1, source_target_pairs={{0,2},{1,3},{2,0},{3,1},{4,6},{5,7},{6,4},{7,5},{8,10},{9,11},{10,... | collective-permute-start | bytes 196616 | tf_op jit(solution)/shard_map/ppermute | solution.py:299
  27.2 6.9 %collective-permute-start = (bf16[128,256]{1,0:T(8,128)(2,1)S(1)}, bf16[128,256]{1,0:T(8,128)(2,1)S(1)}, u32[]{:S(2)}, u32[]{:S(2)}) collective-permute-start(bf16[128,256]{1,0:T(8,128)(2,1)S(1)} %convert_element_type.27.rest_0_), channel_id=1, source_target_pairs={{0,1},{1,0},{2,3},{3,2},{4,5},{5,4},{6,7},{7,6},{8,9},{9,8},{10,11... | collective-permute-start | bytes 196616 | tf_op jit(solution)/shard_map/ppermute | solution.py:299
  34.0 4.3 %copy-start.1 = (bf16[128,256]{1,0:T(8,128)(2,1)}, bf16[128,256]{1,0:T(8,128)(2,1)S(1)}, u32[]{:S(2)}) copy-start(bf16[128,256]{1,0:T(8,128)(2,1)S(1)} %collective-permute-done.2.rest_3_) | copy-start | bytes 196612
  34.0 4.3 %copy-start.2 = (bf16[128,256]{1,0:T(8,128)(2,1)}, bf16[128,256]{1,0:T(8,128)(2,1)S(1)}, u32[]{:S(2)}) copy-start(bf16[128,256]{1,0:T(8,128)(2,1)S(1)} %collective-permute-done.1.rest_2_) | copy-start | bytes 196612
  34.1 4.3 %copy-start.3 = (bf16[128,256]{1,0:T(8,128)(2,1)}, bf16[128,256]{1,0:T(8,128)(2,1)S(1)}, u32[]{:S(2)}) copy-start(bf16[128,256]{1,0:T(8,128)(2,1)S(1)} %collective-permute-done.rest_1_) | copy-start | bytes 196612
  38.4 12.5 %all-to-all-start.2 = ((bf16[8,192,128]{2,1,0:T(8,128)(2,1)}), bf16[8,192,128]{2,1,0:T(8,128)(2,1)S(1)}, u32[]{:S(2)}, u32[]{:S(2)}) async-start(bf16[8,192,128]{2,1,0:T(8,128)(2,1)} %bitcast.62), calls=%async_computation.2 | async-start | bytes 786432 | tf_op jit(solution)/shard_map/all_to_all | solution.py:265
  53.0 11.7 %all-to-all-start.3 = ((bf16[8,192,128]{2,1,0:T(8,128)(2,1)}), bf16[8,192,128]{2,1,0:T(8,128)(2,1)S(1)}, u32[]{:S(2)}, u32[]{:S(2)}) async-start(bf16[8,192,128]{2,1,0:T(8,128)(2,1)} %bitcast.55), calls=%async_computation.3 | async-start | bytes 786432 | tf_op jit(solution)/shard_map/all_to_all | solution.py:265
  81.1 11.7 %all-to-all-start.4 = ((bf16[8,192,128]{2,1,0:T(8,128)(2,1)}), bf16[8,192,128]{2,1,0:T(8,128)(2,1)S(1)}, u32[]{:S(2)}, u32[]{:S(2)}) async-start(bf16[8,192,128]{2,1,0:T(8,128)(2,1)} %bitcast.63), calls=%async_computation.4 | async-start | bytes 786432 | tf_op jit(solution)/shard_map/all_to_all | solution.py:265
  95.0 11.7 %all-to-all-start.5 = ((bf16[8,192,128]{2,1,0:T(8,128)(2,1)}), bf16[8,192,128]{2,1,0:T(8,128)(2,1)S(1)}, u32[]{:S(2)}, u32[]{:S(2)}) async-start(bf16[8,192,128]{2,1,0:T(8,128)(2,1)} %bitcast.56), calls=%async_computation.5 | async-start | bytes 786432 | tf_op jit(solution)/shard_map/all_to_all | solution.py:265
  110.9 12.0 %all-to-all-start.6 = ((bf16[8,192,128]{2,1,0:T(8,128)(2,1)}), bf16[8,192,128]{2,1,0:T(8,128)(2,1)S(1)}, u32[]{:S(2)}, u32[]{:S(2)}) async-start(bf16[8,192,128]{2,1,0:T(8,128)(2,1)} %bitcast.64), calls=%async_computation.6 | async-start | bytes 786432 | tf_op jit(solution)/shard_map/all_to_all | solution.py:265
  125.1 11.7 %all-to-all-start.7 = ((bf16[8,192,128]{2,1,0:T(8,128)(2,1)}), bf16[8,192,128]{2,1,0:T(8,128)(2,1)S(1)}, u32[]{:S(2)}, u32[]{:S(2)}) async-start(bf16[8,192,128]{2,1,0:T(8,128)(2,1)} %bitcast.57), calls=%async_computation.7 | async-start | bytes 786432 | tf_op jit(solution)/shard_map/all_to_all | solution.py:265
  153.2 11.7 %all-to-all-start.8 = ((bf16[8,192,128]{2,1,0:T(8,128)(2,1)}), bf16[8,192,128]{2,1,0:T(8,128)(2,1)S(1)}, u32[]{:S(2)}, u32[]{:S(2)}) async-start(bf16[8,192,128]{2,1,0:T(8,128)(2,1)} %bitcast.60), calls=%async_computation.8 | async-start | bytes 786432 | tf_op jit(solution)/shard_map/all_to_all | solution.py:265
  167.1 11.7 %all-to-all-start.9 = ((bf16[8,192,128]{2,1,0:T(8,128)(2,1)}), bf16[8,192,128]{2,1,0:T(8,128)(2,1)S(1)}, u32[]{:S(2)}, u32[]{:S(2)}) async-start(bf16[8,192,128]{2,1,0:T(8,128)(2,1)} %bitcast.58), calls=%async_computation.9 | async-start | bytes 786432 | tf_op jit(solution)/shard_map/all_to_all | solution.py:265
  183.1 12.0 %all-to-all-start.10 = ((bf16[8,192,128]{2,1,0:T(8,128)(2,1)}), bf16[8,192,128]{2,1,0:T(8,128)(2,1)S(1)}, u32[]{:S(2)}, u32[]{:S(2)}) async-start(bf16[8,192,128]{2,1,0:T(8,128)(2,1)} %bitcast.61), calls=%async_computation.10 | async-start | bytes 786432 | tf_op jit(solution)/shard_map/all_to_all | solution.py:265
where the time goes:
time: 203 us; the launch traced here: 200 us
  Pallas kernels  118 us (58%)
  starting transfers between devices  45.6 us (22%)
  blocking collectives  19.8 us (10%)
  waiting for transfers between devices  9.92 us (5%)
  other arithmetic  3.09 us (2%)
  local copies, waits for them, and re-layouts  2.49 us (1%)
    pallas_call x23, Pallas kernels, call(): run(*(placed(i, x, spec) for i, (x, spec) in enumerate(zip(args, in_specs...  118 us
    all_to_all x11, starting transfers between devices, trade(): lax.all_to_all(blocks, 'wide', split_axis=0, concat_axis=0, tiled=True)  41.2 us
    all_gather x2, blocking collectives, shards(): everyone = lax.all_gather(projection, 'wide', axis=0, tiled=True)  19.8 us
    all_to_all x11, waiting for transfers between devices, trade(): lax.all_to_all(blocks, 'wide', split_axis=0, concat_axis=0, tiled=True)  9.91 us
    ppermute x3, starting transfers between devices, shards(): lax.ppermute(own, 'narrow', [(i, i ^ k) for i in range(side)])  4.42 us
  transfers between devices with their start and end apart: 14, of which 8 were waited for; matrix products, arithmetic and copies ran while one was open for 1% of the time, Pallas kernels for 37%

commit v1 on v0

--- a/solution.py
+++ b/solution.py
@@ -79,6 +79,37 @@
     return lambda *args: run(*(placed(i, x, spec) for i, (x, spec) in enumerate(zip(args, in_specs))))
 
 
+def flat_call(body, near, out_shape, near_out, scratch, copies, flops, moved, scalar=()):
+    def run(*args):
+        places = [
+            pltpu.SMEM if i in scalar else pltpu.VMEM if i in near else pltpu.HBM for i in range(len(args))
+        ]
+        out_places = [pltpu.VMEM if i in near_out else pltpu.HBM for i in range(len(out_shape))]
+        return pl.pallas_call(
+            body,
+            in_specs=[pl.BlockSpec(memory_space=p) for p in places],
+            out_specs=[pl.BlockSpec(memory_space=p) for p in out_places],
+            out_shape=[p(x.shape, x.dtype) for p, x in zip(out_places, out_shape)],
+            scratch_shapes=list(scratch) + [pltpu.SemaphoreType.DMA((copies,))],
+            compiler_params=pltpu.CompilerParams(vmem_limit_bytes=VMEM_LIMIT),
+            cost_estimate=pl.CostEstimate(flops=int(flops), bytes_accessed=int(moved), transcendentals=0),
+        )(*(x if i in scalar else pltpu.with_memory_space_constraint(x, p) for i, (x, p) in enumerate(zip(args, places))))
+
+    return run
+
+
+def begin(sems, first, pairs):
+    started = [pltpu.make_async_copy(a, b, sems.at[first + i]) for i, (a, b) in enumerate(pairs)]
+    for copy in started:
+        copy.start()
+    return started
+
+
+def finish(copies):
+    for copy in copies:
+        copy.wait()
+
+
 def whole(shape):
     return pl.BlockSpec(shape, lambda s: (0,) * len(shape))
 
@@ -87,7 +118,7 @@
     product(matrix_ref, field_ref[...].astype(bf16), part_ref)
 
 
-def first_body(row_ref, field_ref, out_ref, column_ref, low):
+def turn(row_ref, column_ref):
     same = (
         lax.broadcasted_iota(i32, (LANES, LANES), 0) == lax.broadcasted_iota(i32, (LANES, LANES), 1)
     ).astype(f32)
@@ -99,12 +130,26 @@
         column = dot((same * high.astype(f32)).astype(bf16), ones) * LANES
         column += dot((same * (number - high * LANES).astype(f32)).astype(bf16), ones)
         column_ref[pl.ds(t, LANES), :] = column.astype(i32) - 2
-    low[...] = field_ref[...].astype(bf16)
-
-    def rows(at, _):
-        out_ref[at, :] = dot(hot_rows(column_ref[at, :], 0, low.shape[0]), low[...]).astype(bf16)
-
-    chunks(out_ref.shape[0], rows, 3)
+
+
+def first_body(row_ref, place_ref, field_ref, out_ref, column_ref, placed_ref, field, low, made, turned, sems):
+    parts = 3
+    size = field.shape[0] // parts
+    loads = begin(
+        sems, 0, [(field_ref.at[pl.ds(k * size, size)], field.at[pl.ds(k * size, size)]) for k in range(parts)]
+    )
+    turn(row_ref, column_ref)
+    turn(place_ref, turned)
+    stores = begin(sems, parts, [(turned, placed_ref)])
+    for k in range(parts):
+        loads[k].wait()
+        low[pl.ds(k * size, size), :] = field[pl.ds(k * size, size), :].astype(bf16)
+    size = made.shape[0] // parts
+    for k in range(parts):
+        at = pl.ds(k * size, size)
+        made[at, :] = dot(hot_rows(column_ref[at, :], 0, low.shape[0]), low[...]).astype(bf16)
+        stores += begin(sems, parts + 1 + k, [(made.at[at], out_ref.at[at])])
+    finish(stores)
 
 
 def settle_body(sign, has_modes, base_ref, in_ref, row_ref, matrix_ref, *rest):
@@ -128,7 +173,7 @@
     product(matrix_ref, low[...], part_ref)
 
 
-def finish_body(sign, base_ref, in_ref, row_ref, field_ref):
+def last_body(sign, base_ref, in_ref, row_ref, field_ref):
     core = field_ref.shape[0]
     first = pl.program_id(0) * core
 
@@ -147,29 +192,53 @@
     chunks(margin_ref.shape[0], rows, 2)
 
 
-def pack(place_ref, outer, out_ref):
-    def rows(at, c):
-        out_ref[at, :] = dot(hot_cols(place_ref[...], c, at.size), outer[...]).astype(bf16)
-
-    chunks(out_ref.shape[0], rows, 2)
-
-
-def outer_body(in_ref, column_ref, place_ref, matrix_ref, part_ref, margin_ref, out_ref, outer):
-    subs, margins, _ = matrix_ref.shape
-    take_margins(in_ref, column_ref, margin_ref)
+def pack(place_ref, outer, packed, out_ref, sems, first):
+    stores = []
+    size = packed.shape[0] // 2
+    for k in range(2):
+        at = pl.ds(k * size, size)
+        packed[at, :] = dot(hot_cols(place_ref[...], k * size, size), outer[...]).astype(bf16)
+        stores += begin(sems, first + k, [(packed.at[at], out_ref.at[at])])
+    return stores
+
+
+def outer_body(
+    in_ref, placed_ref, place_ref, matrix_ref, part_ref, margin_ref, out_ref,
+    placed, place, matrix, part, margin, outer, packed, sems,
+):
+    subs, margins, _ = matrix.shape
+    core = matrix_ref.shape[1] - margins
+    loads = begin(
+        sems, 0,
+        [
+            (placed_ref, placed),
+            (place_ref, place),
+            (matrix_ref.at[:, core:, core:], matrix),
+            (part_ref.at[:, core:, :], part),
+        ],
+    )
+    loads[0].wait()
+    take_margins(in_ref, placed, margin)
+    stores = begin(sems, 4, [(margin, margin_ref)])
+    finish(loads[1:])
     for s in range(subs):
-        taken = margin_ref[pl.ds(s * margins, margins), :]
-        outer[pl.ds(s * margins, margins), :] = (part_ref[s] + dot(matrix_ref[s], taken)).astype(bf16)
-    pack(place_ref, outer, out_ref)
-
-
-def project_body(in_ref, column_ref, modes_ref, proj_ref, margin_ref, out_ref):
-    subs, count, margins = modes_ref.shape
-    take_margins(in_ref, column_ref, margin_ref)
+        at = pl.ds(s * margins, margins)
+        outer[at, :] = (part[s] + dot(matrix[s], margin[at, :])).astype(bf16)
+    finish(stores + pack(place, outer, packed, out_ref, sems, 5))
+
+
+def project_body(in_ref, placed_ref, modes_ref, proj_ref, margin_ref, out_ref, placed, modes, proj, margin, made, sems):
+    subs, count, margins = modes.shape
+    core = modes_ref.shape[2] - margins
+    loads = begin(sems, 0, [(placed_ref, placed), (modes_ref.at[:, :, core:], modes), (proj_ref, proj)])
+    loads[0].wait()
+    take_margins(in_ref, placed, margin)
+    stores = begin(sems, 3, [(margin, margin_ref)])
+    finish(loads[1:])
     for s in range(subs):
-        taken = margin_ref[pl.ds(s * margins, margins), :]
         at = pl.ds(s * count, count)
-        out_ref[at, :] = (proj_ref[at, :] + dot(modes_ref[s], taken)).astype(bf16)
+        made[at, :] = (proj[at, :] + dot(modes[s], margin[pl.ds(s * margins, margins), :])).astype(bf16)
+    finish(stores + begin(sems, 4, [(made, out_ref)]))
 
 
 def split(x):
@@ -184,21 +253,37 @@
 
 def coarse_body(side, here_ref, all_ref, *rest):
     inverse_refs = rest[:side]
-    margin_ref, place_ref, matrix_ref, part_ref, modes_ref, coarse_ref, out_ref, outer = rest[side:]
-    subs, count, margins = modes_ref.shape
-    made = 0.0
-    for k, inverse_ref in enumerate(inverse_refs):
-        width = inverse_ref.shape[1]
-        first = pl.multiple_of((here_ref[0] ^ k) * width, width)
-        made += dot(inverse_ref[...], all_ref[pl.ds(first, width), :])
-    coarse_ref[...] = made
-    halves = split(made)
+    margin_ref, place_ref, matrix_ref, part_ref, modes_ref, coarse_ref, out_ref = rest[side : side + 7]
+    inverse, margin, place, matrix, part, modes, made, outer, packed, sems = rest[side + 7 :]
+    subs, count, margins = modes.shape
+    core = matrix_ref.shape[1] - margins
+    loads = begin(
+        sems, 0,
+        [(inverse_refs[k], inverse.at[k]) for k in range(side)]
+        + [
+            (modes_ref.at[:, :, core:], modes),
+            (margin_ref, margin),
+            (matrix_ref.at[:, core:, core:], matrix),
+            (part_ref.at[:, core:, :], part),
+            (place_ref, place),
+        ],
+    )
+    finish(loads[:side])
+    value = 0.0
+    for k in range(side):
+        width = inverse.shape[2]
+        at = pl.multiple_of((here_ref[0] ^ k) * width, width)
+        value += dot(inverse[k], all_ref[pl.ds(at, width), :])
+    made[...] = value
+    stores = begin(sems, side + 5, [(made, coarse_ref)])
+    halves = split(value)
+    finish(loads[side:])
     for s in range(subs):
         at = pl.ds(s * margins, margins)
-        solved = part_ref[s] + dot(matrix_ref[s], margin_ref[at, :])
-        lifted = both(turned_dot(modes_ref[s], halves[s * count : (s + 1) * count]))
+        solved = part[s] + dot(matrix[s], margin[at, :])
+        lifted = both(turned_dot(modes[s], halves[s * count : (s + 1) * count]))
         outer[at, :] = (damping * solved + lifted).astype(bf16)
-    pack(place_ref, outer, out_ref)
+    finish(stores + pack(place, outer, packed, out_ref, sems, side + 6))
 
 
 def inner_body(sign, has_modes, part_ref, matrix_ref, margin_ref, base_ref, column_ref, *rest):
@@ -229,12 +314,15 @@
         sent_ref[...] = both(total[...])
 
 
-def relay_body(sign, sent_ref, in_ref, column_ref, row_ref, out_ref):
-    def rows(at, _):
+def relay_body(sign, sent_ref, in_ref, column_ref, row_ref, out_ref, made, sems):
+    stores = []
+    size = made.shape[0] // 2
+    for k in range(2):
+        at = pl.ds(k * size, size)
         added = dot(hot_pairs(column_ref[at, :], row_ref[...]), in_ref[...])
-        out_ref[at, :] = (sent_ref[at, :] + sign * added).astype(bf16)
-
-    chunks(out_ref.shape[0], rows, 2)
+        made[at, :] = (sent_ref[at, :] + sign * added).astype(bf16)
+        stores += begin(sems, k, [(made.at[at], out_ref.at[at])])
+    finish(stores)
 
 
 def shards(loads, start, stiffness, local_inverse, modes, coarse_inverse, margin_rows):
@@ -268,8 +356,6 @@
     wanted = trade(asked)
     wanted_row = wanted[None, :]
     place_row = place[None, :]
-    place_column = jnp.broadcast_to(place[:, None], (many, LANES))
-    wanted_row, place_column = lax.optimization_barrier((wanted_row, place_column))
     modes_turned = jnp.swapaxes(modes, 1, 2)
 
     rows_spec = pl.BlockSpec((core, cols), lambda s: (s, 0))
@@ -283,21 +369,26 @@
     matrix_flops = 2 * subs * order * core * cols
     slot_flops = 2 * held * slots * cols
 
-    going, wanted_column = call(
-        first_body, (1,), [whole((1, slots)), whole((held, cols))], [slots_spec, whole((slots, LANES))],
-        [slots_low, jax.ShapeDtypeStruct((slots, LANES), i32)], [pltpu.VMEM((held, cols), bf16)],
-        slot_flops, 2e6, (0,), (1,),
-    )(wanted_row, start)
-    begun, own, going = lax.optimization_barrier((start, coarse_inverse.astype(bf16), going))
+    going, wanted_column, place_column = flat_call(
+        first_body, (0, 1),
+        [slots_low, jax.ShapeDtypeStruct((slots, LANES), i32), jax.ShapeDtypeStruct((many, LANES), i32)], (1,),
+        [
+            pltpu.VMEM((held, cols), f32), pltpu.VMEM((held, cols), bf16), pltpu.VMEM((slots, cols), bf16),
+            pltpu.VMEM((many, LANES), i32),
+        ],
+        7, slot_flops, 4e6,
+    )(wanted_row, place_row, start)
+    side = lax.axis_size("narrow")
+    here = lax.axis_index("narrow").reshape(1).astype(i32)
+    own = coarse_inverse.astype(bf16)
+    pieces = [own] + [
+        lax.ppermute(own, "narrow", [(i, i ^ k) for i in range(side)]) for k in range(1, side)
+    ]
+    begun, pieces, going = lax.optimization_barrier((start, pieces, going))
     part = call(
         open_body, (subs,), [rows_spec, left_spec], part_spec, part_shape, [], matrix_flops, 10e6,
     )(begun, stiffness)
 
-    side = lax.axis_size("narrow")
-    here = lax.axis_index("narrow").reshape(1).astype(i32)
-    pieces = [own] + [
-        lax.ppermute(own, "narrow", [(i, i ^ k) for i in range(side)]) for k in range(1, side)
-    ]
     core_modes_spec = pl.BlockSpec((1, count, core), lambda s: (s, 0, 0))
     outer_modes_spec = pl.BlockSpec((subs, count, margins), lambda s: (0, 0, m_at))
 
@@ -343,26 +434,31 @@
         )(*args)
 
     def relay(sign, sent, came):
-        return call(
-            functools.partial(relay_body, sign), (1,),
-            [slots_spec, slots_spec, whole((slots, LANES)), whole((1, slots))], slots_spec, slots_low, [],
-            slot_flops // 2, 3e6, (0, 1, 2, 3),
-        )(sent, came, wanted_column, wanted_row)
+        return flat_call(
+            functools.partial(relay_body, sign), (0, 1, 2, 3), [slots_low], (), [pltpu.VMEM((slots, cols), bf16)], 2,
+            slot_flops // 2, 3e6,
+        )(sent, came, wanted_column, wanted_row)[0]
+
+    column_scratch = pltpu.VMEM((many, LANES), i32)
+    corner_scratch = [
+        pltpu.VMEM((subs, margins, margins), bf16), pltpu.VMEM((subs, margins, cols), f32),
+    ]
+    margin_scratch = pltpu.VMEM((many, cols), bf16)
+    packed_scratch = pltpu.VMEM((slots, cols), bf16)
+    modes_scratch = pltpu.VMEM((subs, count, margins), bf16)
 
     def stiffness_outer(came, part):
-        return call(
-            outer_body, (1,),
-            [slots_spec, whole((many, LANES)), whole((1, many)), corner_spec, part_outer_spec],
-            [whole((many, cols)), slots_spec], [margin_shape, slots_low], outer_scratch, slot_flops, 3e6,
-            (0,),
+        return flat_call(
+            outer_body, (0,), [margin_shape, slots_low], (),
+            [column_scratch, pltpu.VMEM((1, many), i32)] + corner_scratch
+            + [margin_scratch, margin_scratch, packed_scratch],
+            7, slot_flops, 3e6,
         )(came, place_column, place_row, stiffness, part)
 
     field = start
     for step in range(ITERS + 1):
         came = trade(going)
-        if step == 0:
-            pieces, came = lax.optimization_barrier((pieces, came))
-        else:
+        if step > 0:
             field, part = settle(1.0, base, back, stiffness, False)
         margin, going = stiffness_outer(came, part)
         back = trade(going)
@@ -373,35 +469,28 @@
         going = relay(-1.0, sent, back)
         came = trade(going)
         part, proj = settle(-1.0, base, back, local_inverse, True)
-        margin, projection = call(
-            project_body, (1,),
-            [slots_spec, whole((many, LANES)), outer_modes_spec, whole((coarse_rows, cols))],
-            [whole((many, cols)), whole((coarse_rows, cols))],
-            [margin_shape, jax.ShapeDtypeStruct((coarse_rows, cols), bf16)], [], slot_flops // 2, 2e6,
-            (0,),
+        margin, projection = flat_call(
+            project_body, (0,), [margin_shape, jax.ShapeDtypeStruct((coarse_rows, cols), bf16)], (),
+            [
+                column_scratch, modes_scratch, pltpu.VMEM((coarse_rows, cols), f32), margin_scratch,
+                pltpu.VMEM((coarse_rows, cols), bf16),
+            ],
+            5, slot_flops // 2, 2e6,
         )(came, place_column, modes_turned, proj)
         everyone = lax.all_gather(projection, "wide", axis=0, tiled=True)
-        coarse, going = call(
-            functools.partial(coarse_body, side), (1,),
-            [pl.BlockSpec(memory_space=pltpu.SMEM), whole((owners * coarse_rows, cols))]
-            + [whole(coarse_inverse.shape)] * side
-            + [
-                whole((many, cols)),
-                whole((1, many)),
-                corner_spec,
-                part_outer_spec,
-                outer_modes_spec,
-            ],
-            [whole((coarse_rows, cols)), slots_spec],
-            [jax.ShapeDtypeStruct((coarse_rows, cols), f32), slots_low], outer_scratch, slot_flops, 3e6,
-            (1,),
+        coarse, going = flat_call(
+            functools.partial(coarse_body, side), (1,), [jax.ShapeDtypeStruct((coarse_rows, cols), f32), slots_low], (),
+            [pltpu.VMEM((side,) + coarse_inverse.shape, bf16), margin_scratch, pltpu.VMEM((1, many), i32)]
+            + corner_scratch
+            + [modes_scratch, pltpu.VMEM((coarse_rows, cols), f32), margin_scratch, packed_scratch],
+            side + 8, slot_flops, 3e6, (0,),
         )(here, everyone, *pieces, margin, place_row, local_inverse, part, modes_turned)
         back = trade(going)
         base, sent = inner(1.0, field, margin, part, local_inverse, coarse)
         going = relay(1.0, sent, back)
 
     final = call(
-        functools.partial(finish_body, -1.0), (subs,), [rows_spec, slots_spec, whole((1, slots))], rows_spec,
+        functools.partial(last_body, -1.0), (subs,), [rows_spec, slots_spec, whole((1, slots))], rows_spec,
         held_shape, [], slot_flops, 4e6, (1, 2),
     )(base, back, wanted_row)
     return field, final

time: 203 us -> 203 us (level)
  waiting for transfers between devices: 9.92 us -> 12.1 us
    pallas_call x23 -> x11, Pallas kernels: 118 us -> 78.9 us  [call(): run(*(placed(i, x, spec) for i, (x, spec) in enumerate(zip(args, in_specs...]
    pallas_call x0 -> x12, Pallas kernels: none -> 38.1 us  [run(): pl.pallas_call(body, in_specs=[pl.BlockSpec(memory_space=p) for p in plac...]
    all_to_all x11, waiting for transfers between devices: 9.91 us -> 12.1 us  [trade(): lax.all_to_all(blocks, 'wide', split_axis=0, concat_axis=0, tiled=True)]
  transfers between devices with their start and end apart: 14 -> 14, of which waited for: 8 -> 9; matrix products, arithmetic and copies ran while one was open for 1% -> 2% of each run, Pallas kernels for 37% -> 39%
where the time goes in v1:
time: 203 us; the launch traced here: 200 us
  Pallas kernels  117 us (58%)
  starting transfers between devices  45.1 us (22%)
  blocking collectives  19.8 us (10%)
  waiting for transfers between devices  12.1 us (6%)
  other arithmetic  3.2 us (2%)
    pallas_call x11, Pallas kernels, call(): run(*(placed(i, x, spec) for i, (x, spec) in enumerate(zip(args, in_specs...  78.9 us
    all_to_all x11, starting transfers between devices, trade(): lax.all_to_all(blocks, 'wide', split_axis=0, concat_axis=0, tiled=True)  39.3 us
    pallas_call x12, Pallas kernels, run(): pl.pallas_call(body, in_specs=[pl.BlockSpec(memory_space=p) for p in plac...  38.1 us
    all_gather x2, blocking collectives, shards(): everyone = lax.all_gather(projection, 'wide', axis=0, tiled=True)  19.8 us
    all_to_all x11, waiting for transfers between devices, trade(): lax.all_to_all(blocks, 'wide', split_axis=0, concat_axis=0, tiled=True)  12.1 us
    ppermute x3, starting transfers between devices, shards(): lax.ppermute(own, 'narrow', [(i, i ^ k) for i in range(side)])  5.76 us
  transfers between devices with their start and end apart: 14, of which 9 were waited for; matrix products, arithmetic and copies ran while one was open for 2% of the time, Pallas kernels for 39%

profile of v1, /device:TPU:0, one launch (start us, length us, event | category | flops | bytes accessed | tf_op | source)
XLA Modules:
  0.0 200.1 jit_solution(509986153197333341)
XLA Ops:
  0.6 0.9 convert_element_type.27.rest_0_
  1.5 5.1 %collective-permute-start.2 = (bf16[128,256]{1,0:T(8,128)(2,1)S(1)}, bf16[128,256]{1,0:T(8,128)(2,1)S(1)}, u32[]{:S(2)}, u32[]{:S(2)}) collective-permute-start(bf16[128,256]{1,0:T(8,128)(2,1)S(1)} %convert_element_type.27.rest_0_), channel_id=1, source_target_pairs={{0,3},{1,2},{2,1},{3,0},{4,7},{5,6},{6,5},{7,4},{8,11},{9,10},{10,... | collective-permute-start | bytes 196616 | tf_op jit(solution)/shard_map/ppermute | solution.py:385
  6.7 0.0 collective-permute-start.1
  6.7 0.6 collective-permute-start
  7.3 0.7 copy.9
  8.0 0.5 fusion.2
  8.5 0.8 select_reduce_fusion
  9.3 0.7 sub.24
  10.0 3.9 %all-to-all-start = ((s32[8,1,192]{2,1,0:T(1,128)}), s32[8,1,192]{2,1,0:T(1,128)S(1)}, u32[]{:S(2)}, u32[]{:S(2)}) async-start(s32[8,1,192]{2,1,0:T(1,128)} %sub.24), calls=%async_computation | async-start | bytes 16384 | tf_op jit(solution)/shard_map/all_to_all | solution.py:353
  13.9 0.7 fusion.9
  14.6 0.7 divide_bitcast_fusion
  15.3 0.0 copy-start
  15.4 3.2 %all-to-all-done = s32[8,1,192]{2,1,0:T(1,128)S(1)} async-done(((s32[8,1,192]{2,1,0:T(1,128)}), s32[8,1,192]{2,1,0:T(1,128)S(1)}, u32[]{:S(2)}, u32[]{:S(2)}) %all-to-all-start) | async-done | bytes 6176 | tf_op jit(solution)/shard_map/all_to_all | solution.py:353
  18.6 0.1 broadcast_in_dim_reshape.3.row_ref
  18.7 4.7 %shard_map.86 = (bf16[1536,128]{1,0:T(8,128)(2,1)}, s32[1536,128]{1,0:T(8,128)S(1)}, s32[1024,128]{1,0:T(8,128)}) custom-call(s32[1,1536]{1,0:T(1,128)S(1)} %broadcast_in_dim_reshape.3.row_ref, s32[1,1024]{1,0:T(1,128)S(1)} %fusion.6.place_ref.rest_5_, f32[3072,128]{1,0:T(8,128)} %base_ref.5), custom_call_target="tpu_custom_call" | custom-call | flops 1207959552 | bytes 4000000 | tf_op jit(solution)/shard_map/pallas_call | solution.py:88
  23.5 0.0 copy-done.1
  23.5 0.0 collective-permute-done.2.rest_3_
  23.5 0.0 collective-permute-done.1.rest_2_
  23.5 0.0 collective-permute-done.rest_1_
  23.5 0.0 copy-start.4
  23.5 3.5 %all-to-all-start.1 = ((bf16[8,192,128]{2,1,0:T(8,128)(2,1)}), bf16[8,192,128]{2,1,0:T(8,128)(2,1)S(1)}, u32[]{:S(2)}, u32[]{:S(2)}) async-start(bf16[8,192,128]{2,1,0:T(8,128)(2,1)} %bitcast.60), calls=%async_computation.1 | async-start | bytes 786432 | tf_op jit(solution)/shard_map/all_to_all | solution.py:353
  27.0 6.1 %shard_map.87.part_ref = f32[4,1024,128]{2,1,0:T(8,128)} custom-call(f32[3072,128]{1,0:T(8,128)} %base_ref.5, bf16[4,1024,1024]{2,1,0:T(8,128)(2,1)} %matrix_ref.25), custom_call_target="tpu_custom_call" | custom-call | flops 805306368 | bytes 10000000 | tf_op jit(solution)/shard_map/pallas_call | solution.py:79
  33.1 2.2 %all-to-all-done.1 = bf16[8,192,128]{2,1,0:T(8,128)(2,1)S(1)} async-done(((bf16[8,192,128]{2,1,0:T(8,128)(2,1)}), bf16[8,192,128]{2,1,0:T(8,128)(2,1)S(1)}, u32[]{:S(2)}, u32[]{:S(2)}) %all-to-all-start.1) | async-done | bytes 393248 | tf_op jit(solution)/shard_map/all_to_all | solution.py:353
  35.3 4.0 %shard_map.88 = (bf16[1024,128]{1,0:T(8,128)(2,1)}, bf16[1536,128]{1,0:T(8,128)(2,1)}) custom-call(bf16[1536,128]{1,0:T(8,128)(2,1)S(1)} %bitcast.43, s32[1024,128]{1,0:T(8,128)} %get-tuple-element.45.placed_ref, s32[1,1024]{1,0:T(1,128)} %copy-done, bf16[4,1024,1024]{2,1,0:T(8,128)(2,1)} %matrix_ref.25, f32[4,1024,128]{2,1,0:T(8,128)} %shard_map.87.part_ref), custom_call_target="tpu_custom_call" | custom-call | flops 1207959552 | bytes 3000000 | tf_op jit(solution)/shard_map/pallas_call | solution.py:88
  39.3 3.5 %all-to-all-start.2 = ((bf16[8,192,128]{2,1,0:T(8,128)(2,1)}), bf16[8,192,128]{2,1,0:T(8,128)(2,1)S(1)}, u32[]{:S(2)}, u32[]{:S(2)}) async-start(bf16[8,192,128]{2,1,0:T(8,128)(2,1)} %bitcast.62), calls=%async_computation.2 | async-start | bytes 786432 | tf_op jit(solution)/shard_map/all_to_all | solution.py:353
  42.8 6.9 %shard_map.89 = (f32[3072,128]{1,0:T(8,128)}, f32[1536,128]{1,0:T(8,128)S(1)}) custom-call(f32[4,1024,128]{2,1,0:T(8,128)} %shard_map.87.part_ref, bf16[4,1024,1024]{2,1,0:T(8,128)(2,1)} %matrix_ref.25, bf16[1024,128]{1,0:T(8,128)(2,1)} %get-tuple-element.46.margin_ref, f32[3072,128]{1,0:T(8,128)} %base_ref.7, s32[1536,128]{1,0:T(8,128)S(1)} %get-tuple-element.47.column_ref), custom_call_target="tpu_custom_call" | custom-call | flops 2415919104 | bytes 8000000 | tf_op jit(solution)/shard_map/pallas_call | solution.py:79
  49.6 1.4 all-to-all-done.2
  51.1 2.1 %shard_map.91 = bf16[1536,128]{1,0:T(8,128)(2,1)} custom-call(f32[1536,128]{1,0:T(8,128)S(1)} %get-tuple-element.51.sent_ref, bf16[1536,128]{1,0:T(8,128)(2,1)S(1)} %bitcast.33, s32[1536,128]{1,0:T(8,128)S(1)} %get-tuple-element.47.column_ref, s32[1,1536]{1,0:T(1,128)S(1)} %broadcast_in_dim_reshape.3.row_ref), custom_call_target="tpu_custom_call" | custom-call | flops 603979776 | bytes 3000000 | tf_op jit(solution)/shard_map/pallas_call | solution.py:88
  53.2 3.5 %all-to-all-start.3 = ((bf16[8,192,128]{2,1,0:T(8,128)(2,1)}), bf16[8,192,128]{2,1,0:T(8,128)(2,1)S(1)}, u32[]{:S(2)}, u32[]{:S(2)}) async-start(bf16[8,192,128]{2,1,0:T(8,128)(2,1)} %bitcast.55), calls=%async_computation.3 | async-start | bytes 786432 | tf_op jit(solution)/shard_map/all_to_all | solution.py:353
  56.7 8.3 %shard_map.90 = (f32[4,1024,128]{2,1,0:T(8,128)}, f32[128,128]{1,0:T(8,128)}) custom-call(f32[3072,128]{1,0:T(8,128)} %get-tuple-element.48.base_ref, bf16[1536,128]{1,0:T(8,128)(2,1)S(1)} %bitcast.34, s32[1,1536]{1,0:T(1,128)S(1)} %broadcast_in_dim_reshape.3.row_ref, bf16[4,1024,1024]{2,1,0:T(8,128)(2,1)} %matrix_ref.22, bf16[4,32,1024]{2,1,0:T(8,128)(2,1)} %bitcast.47), custom_call_target="tpu_custom_call" | custom-call | flops 2013265920 | bytes 14000000 | tf_op jit(solution)/shard_map/pallas_call | solution.py:79
  65.0 0.0 all-to-all-done.3
  65.0 2.8 %shard_map.92 = (bf16[1024,128]{1,0:T(8,128)(2,1)}, bf16[128,128]{1,0:T(8,128)(2,1)}) custom-call(bf16[1536,128]{1,0:T(8,128)(2,1)S(1)} %bitcast.44, s32[1024,128]{1,0:T(8,128)} %get-tuple-element.45.placed_ref, bf16[4,32,1024]{2,1,0:T(8,128)(2,1)} %bitcast.48, f32[128,128]{1,0:T(8,128)} %get-tuple-element.52.proj_ref), custom_call_target="tpu_custom_call" | custom-call | flops 603979776 | bytes 2000000 | tf_op jit(solution)/shard_map/pallas_call | solution.py:88
  67.8 9.9 %all_gather.6.all_ref = bf16[1024,128]{1,0:T(8,128)(2,1)S(1)} all-gather(bf16[128,128]{1,0:T(8,128)(2,1)} %get-tuple-element.54), channel_id=1, replica_groups=mesh['wide'=8,'narrow'=4] {'wide'}, dimensions={0}, use_global_device_ids=true | all-gather | bytes 294912 | tf_op jit(solution)/shard_map/all_gather | solution.py:480
  77.7 3.5 %shard_map.93 = (f32[128,128]{1,0:T(8,128)}, bf16[1536,128]{1,0:T(8,128)(2,1)}) custom-call(s32[1]{0:T(128)} %bitcast.8.here_ref, bf16[1024,128]{1,0:T(8,128)(2,1)S(1)} %all_gather.6.all_ref, bf16[128,256]{1,0:T(8,128)(2,1)} %copy-done.1, bf16[128,256]{1,0:T(8,128)(2,1)} %copy-done.4, bf16[128,256]{1,0:T(8,128)(2,1)} %copy-done.3, ...), custom_call_target="tpu_custom_call" | custom-call | flops 1207959552 | bytes 3000000 | tf_op jit(solution)/shard_map/pallas_call | solution.py:88
  81.3 3.6 %all-to-all-start.4 = ((bf16[8,192,128]{2,1,0:T(8,128)(2,1)}), bf16[8,192,128]{2,1,0:T(8,128)(2,1)S(1)}, u32[]{:S(2)}, u32[]{:S(2)}) async-start(bf16[8,192,128]{2,1,0:T(8,128)(2,1)} %bitcast.63), calls=%async_computation.4 | async-start | bytes 786432 | tf_op jit(solution)/shard_map/all_to_all | solution.py:353
  84.9 7.2 %shard_map.94 = (f32[3072,128]{1,0:T(8,128)}, f32[1536,128]{1,0:T(8,128)S(1)}) custom-call(f32[4,1024,128]{2,1,0:T(8,128)} %get-tuple-element.50.rest_7_.part_ref, bf16[4,1024,1024]{2,1,0:T(8,128)(2,1)} %matrix_ref.22, bf16[1024,128]{1,0:T(8,128)(2,1)} %get-tuple-element.53.rest_4_.margin_ref, f32[3072,128]{1,0:T(8,128)} %base_ref.5, ...), custom_call_target="tpu_custom_call" | custom-call | flops 2415919104 | bytes 8000000 | tf_op jit(solution)/shard_map/pallas_call | solution.py:79
  92.1 0.9 all-to-all-done.4
  93.0 2.1 %shard_map.96 = bf16[1536,128]{1,0:T(8,128)(2,1)} custom-call(f32[1536,128]{1,0:T(8,128)S(1)} %get-tuple-element.63.sent_ref, bf16[1536,128]{1,0:T(8,128)(2,1)S(1)} %bitcast.39, s32[1536,128]{1,0:T(8,128)S(1)} %get-tuple-element.47.column_ref, s32[1,1536]{1,0:T(1,128)S(1)} %broadcast_in_dim_reshape.3.row_ref), custom_call_target="tpu_custom_call" | custom-call | flops 603979776 | bytes 3000000 | tf_op jit(solution)/shard_map/pallas_call | solution.py:88
  95.1 3.5 %all-to-all-start.5 = ((bf16[8,192,128]{2,1,0:T(8,128)(2,1)}), bf16[8,192,128]{2,1,0:T(8,128)(2,1)S(1)}, u32[]{:S(2)}, u32[]{:S(2)}) async-start(bf16[8,192,128]{2,1,0:T(8,128)(2,1)} %bitcast.56), calls=%async_computation.5 | async-start | bytes 786432 | tf_op jit(solution)/shard_map/all_to_all | solution.py:353
  98.6 7.8 %shard_map.95 = (f32[3072,128]{1,0:T(8,128)}, f32[4,1024,128]{2,1,0:T(8,128)}) custom-call(f32[3072,128]{1,0:T(8,128)} %get-tuple-element.60.base_ref, bf16[1536,128]{1,0:T(8,128)(2,1)S(1)} %bitcast.40, s32[1,1536]{1,0:T(1,128)S(1)} %broadcast_in_dim_reshape.3.row_ref, bf16[4,1024,1024]{2,1,0:T(8,128)(2,1)} %matrix_ref.25), custom_call_target="tpu_custom_call" | custom-call | flops 2013265920 | bytes 14000000 | tf_op jit(solution)/shard_map/pallas_call | solution.py:79
  106.4 0.4 all-to-all-done.5
  106.9 4.0 %shard_map.97 = (bf16[1024,128]{1,0:T(8,128)(2,1)}, bf16[1536,128]{1,0:T(8,128)(2,1)}) custom-call(bf16[1536,128]{1,0:T(8,128)(2,1)S(1)} %bitcast.42, s32[1024,128]{1,0:T(8,128)} %get-tuple-element.45.placed_ref, s32[1,1024]{1,0:T(1,128)} %copy-done, bf16[4,1024,1024]{2,1,0:T(8,128)(2,1)} %matrix_ref.25, f32[4,1024,128]{2,1,0:T(8,128)} %get-tuple-element.62.part_ref), custom_call_target="tpu_custom_call" | custom-call | flops 1207959552 | bytes 3000000 | tf_op jit(solution)/shard_map/pallas_call | solution.py:88
  110.9 3.7 %all-to-all-start.6 = ((bf16[8,192,128]{2,1,0:T(8,128)(2,1)}), bf16[8,192,128]{2,1,0:T(8,128)(2,1)S(1)}, u32[]{:S(2)}, u32[]{:S(2)}) async-start(bf16[8,192,128]{2,1,0:T(8,128)(2,1)} %bitcast.64), calls=%async_computation.6 | async-start | bytes 786432 | tf_op jit(solution)/shard_map/all_to_all | solution.py:353
  114.6 6.9 %shard_map.98 = (f32[3072,128]{1,0:T(8,128)}, f32[1536,128]{1,0:T(8,128)S(1)}) custom-call(f32[4,1024,128]{2,1,0:T(8,128)} %get-tuple-element.62.part_ref, bf16[4,1024,1024]{2,1,0:T(8,128)(2,1)} %matrix_ref.25, bf16[1024,128]{1,0:T(8,128)(2,1)} %get-tuple-element.64.margin_ref, f32[3072,128]{1,0:T(8,128)} %base_ref.7, ...), custom_call_target="tpu_custom_call" | custom-call | flops 2415919104 | bytes 8000000 | tf_op jit(solution)/shard_map/pallas_call | solution.py:79
  121.5 1.5 all-to-all-done.6
  122.9 2.1 %shard_map.100 = bf16[1536,128]{1,0:T(8,128)(2,1)} custom-call(f32[1536,128]{1,0:T(8,128)S(1)} %get-tuple-element.68.sent_ref, bf16[1536,128]{1,0:T(8,128)(2,1)S(1)} %bitcast.35, s32[1536,128]{1,0:T(8,128)S(1)} %get-tuple-element.47.column_ref, s32[1,1536]{1,0:T(1,128)S(1)} %broadcast_in_dim_reshape.3.row_ref), custom_call_target="tpu_custom_call" | custom-call | flops 603979776 | bytes 3000000 | tf_op jit(solution)/shard_map/pallas_call | solution.py:88
  125.1 3.5 %all-to-all-start.7 = ((bf16[8,192,128]{2,1,0:T(8,128)(2,1)}), bf16[8,192,128]{2,1,0:T(8,128)(2,1)S(1)}, u32[]{:S(2)}, u32[]{:S(2)}) async-start(bf16[8,192,128]{2,1,0:T(8,128)(2,1)} %bitcast.57), calls=%async_computation.7 | async-start | bytes 786432 | tf_op jit(solution)/shard_map/all_to_all | solution.py:353
  128.6 8.3 %shard_map.99 = (f32[4,1024,128]{2,1,0:T(8,128)}, f32[128,128]{1,0:T(8,128)}) custom-call(f32[3072,128]{1,0:T(8,128)} %get-tuple-element.65.base_ref, bf16[1536,128]{1,0:T(8,128)(2,1)S(1)} %bitcast.36, s32[1,1536]{1,0:T(1,128)S(1)} %broadcast_in_dim_reshape.3.row_ref, bf16[4,1024,1024]{2,1,0:T(8,128)(2,1)} %matrix_ref.22, bf16[4,32,1024]{2,1,0:T(8,128)(2,1)} %bitcast.51), custom_call_target="tpu_custom_call" | custom-call | flops 2013265920 | bytes 14000000 | tf_op jit(solution)/shard_map/pallas_call | solution.py:79
  136.8 0.0 all-to-all-done.7
  136.8 2.8 %shard_map.101 = (bf16[1024,128]{1,0:T(8,128)(2,1)}, bf16[128,128]{1,0:T(8,128)(2,1)}) custom-call(bf16[1536,128]{1,0:T(8,128)(2,1)S(1)} %bitcast.46, s32[1024,128]{1,0:T(8,128)} %get-tuple-element.45.placed_ref, bf16[4,32,1024]{2,1,0:T(8,128)(2,1)} %bitcast.52, f32[128,128]{1,0:T(8,128)} %get-tuple-element.69.proj_ref), custom_call_target="tpu_custom_call" | custom-call | flops 603979776 | bytes 2000000 | tf_op jit(solution)/shard_map/pallas_call | solution.py:88
  139.7 9.9 %all_gather.7.all_ref = bf16[1024,128]{1,0:T(8,128)(2,1)S(1)} all-gather(bf16[128,128]{1,0:T(8,128)(2,1)} %get-tuple-element.72), channel_id=1, replica_groups=mesh['wide'=8,'narrow'=4] {'wide'}, dimensions={0}, use_global_device_ids=true | all-gather | bytes 294912 | tf_op jit(solution)/shard_map/all_gather | solution.py:480
  149.6 3.5 %shard_map.102 = (f32[128,128]{1,0:T(8,128)}, bf16[1536,128]{1,0:T(8,128)(2,1)}) custom-call(s32[1]{0:T(128)} %bitcast.8.here_ref, bf16[1024,128]{1,0:T(8,128)(2,1)S(1)} %all_gather.7.all_ref, bf16[128,256]{1,0:T(8,128)(2,1)} %copy-done.1, bf16[128,256]{1,0:T(8,128)(2,1)} %copy-done.4, bf16[128,256]{1,0:T(8,128)(2,1)} %copy-done.3, ...), custom_call_target="tpu_custom_call" | custom-call | flops 1207959552 | bytes 3000000 | tf_op jit(solution)/shard_map/pallas_call | solution.py:88
  153.2 3.7 %all-to-all-start.8 = ((bf16[8,192,128]{2,1,0:T(8,128)(2,1)}), bf16[8,192,128]{2,1,0:T(8,128)(2,1)S(1)}, u32[]{:S(2)}, u32[]{:S(2)}) async-start(bf16[8,192,128]{2,1,0:T(8,128)(2,1)} %bitcast.59), calls=%async_computation.8 | async-start | bytes 786432 | tf_op jit(solution)/shard_map/all_to_all | solution.py:353
  156.9 7.2 %shard_map.103 = (f32[3072,128]{1,0:T(8,128)}, f32[1536,128]{1,0:T(8,128)S(1)}) custom-call(f32[4,1024,128]{2,1,0:T(8,128)} %get-tuple-element.67.rest_7_.part_ref, bf16[4,1024,1024]{2,1,0:T(8,128)(2,1)} %matrix_ref.22, bf16[1024,128]{1,0:T(8,128)(2,1)} %get-tuple-element.70.rest_4_.margin_ref, f32[3072,128]{1,0:T(8,128)} %get-tuple-element.71.base_ref, ...), custom_call_target="tpu_custom_call" | custom-call | flops 2415919104 | bytes 8000000 | tf_op jit(solution)/shard_map/pallas_call | solution.py:79
  164.1 0.8 all-to-all-done.8
  164.9 2.1 %shard_map.105 = bf16[1536,128]{1,0:T(8,128)(2,1)} custom-call(f32[1536,128]{1,0:T(8,128)S(1)} %get-tuple-element.78.sent_ref, bf16[1536,128]{1,0:T(8,128)(2,1)S(1)} %bitcast.37, s32[1536,128]{1,0:T(8,128)S(1)} %get-tuple-element.47.column_ref, s32[1,1536]{1,0:T(1,128)S(1)} %broadcast_in_dim_reshape.3.row_ref), custom_call_target="tpu_custom_call" | custom-call | flops 603979776 | bytes 3000000 | tf_op jit(solution)/shard_map/pallas_call | solution.py:88
  167.0 3.5 %all-to-all-start.9 = ((bf16[8,192,128]{2,1,0:T(8,128)(2,1)}), bf16[8,192,128]{2,1,0:T(8,128)(2,1)S(1)}, u32[]{:S(2)}, u32[]{:S(2)}) async-start(bf16[8,192,128]{2,1,0:T(8,128)(2,1)} %bitcast.58), calls=%async_computation.9 | async-start | bytes 786432 | tf_op jit(solution)/shard_map/all_to_all | solution.py:353
  170.5 7.8 %shard_map.104 = (f32[3072,128]{1,0:T(8,128)}, f32[4,1024,128]{2,1,0:T(8,128)}) custom-call(f32[3072,128]{1,0:T(8,128)} %get-tuple-element.74.base_ref, bf16[1536,128]{1,0:T(8,128)(2,1)S(1)} %bitcast.38, s32[1,1536]{1,0:T(1,128)S(1)} %broadcast_in_dim_reshape.3.row_ref, bf16[4,1024,1024]{2,1,0:T(8,128)(2,1)} %matrix_ref.25), custom_call_target="tpu_custom_call" | custom-call | flops 2013265920 | bytes 14000000 | tf_op jit(solution)/shard_map/pallas_call | solution.py:79
  178.3 0.4 all-to-all-done.9
  178.8 4.0 %shard_map.106 = (bf16[1024,128]{1,0:T(8,128)(2,1)}, bf16[1536,128]{1,0:T(8,128)(2,1)}) custom-call(bf16[1536,128]{1,0:T(8,128)(2,1)S(1)} %bitcast.41, s32[1024,128]{1,0:T(8,128)} %get-tuple-element.45.placed_ref, s32[1,1024]{1,0:T(1,128)} %copy-done, bf16[4,1024,1024]{2,1,0:T(8,128)(2,1)} %matrix_ref.25, f32[4,1024,128]{2,1,0:T(8,128)} %get-tuple-element.77.part_ref), custom_call_target="tpu_custom_call" | custom-call | flops 1207959552 | bytes 3000000 | tf_op jit(solution)/shard_map/pallas_call | solution.py:88
  182.8 3.7 %all-to-all-start.10 = ((bf16[8,192,128]{2,1,0:T(8,128)(2,1)}), bf16[8,192,128]{2,1,0:T(8,128)(2,1)S(1)}, u32[]{:S(2)}, u32[]{:S(2)}) async-start(bf16[8,192,128]{2,1,0:T(8,128)(2,1)} %bitcast.61), calls=%async_computation.10 | async-start | bytes 786432 | tf_op jit(solution)/shard_map/all_to_all | solution.py:353
  186.5 7.1 %shard_map.107 = (f32[3072,128]{1,0:T(8,128)}, f32[1536,128]{1,0:T(8,128)}) custom-call(f32[4,1024,128]{2,1,0:T(8,128)} %get-tuple-element.77.part_ref, bf16[4,1024,1024]{2,1,0:T(8,128)(2,1)} %matrix_ref.25, bf16[1024,128]{1,0:T(8,128)(2,1)} %get-tuple-element.79.margin_ref, f32[3072,128]{1,0:T(8,128)} %base_ref.7, s32[1536,128]{1,0:T(8,128)S(1)} %get-tuple-element.47.column_ref), custom_call_target="tpu_custom_call" | custom-call | flops 2415919104 | bytes 8000000 | tf_op jit(solution)/shard_map/pallas_call | solution.py:79
  193.6 1.2 all-to-all-done.10
  194.8 5.3 %shard_map.108 = f32[3072,128]{1,0:T(8,128)} custom-call(f32[3072,128]{1,0:T(8,128)} %get-tuple-element.80.base_ref, bf16[1536,128]{1,0:T(8,128)(2,1)S(1)} %bitcast.45, s32[1,1536]{1,0:T(1,128)S(1)} %broadcast_in_dim_reshape.3.row_ref), custom_call_target="tpu_custom_call" | custom-call | flops 1207959552 | bytes 4000000 | tf_op jit(solution)/shard_map/pallas_call | solution.py:79
  (15 shorter events, 0.1 us)
Async XLA Ops:
  1.5 21.9 %copy-start.1 = (bf16[128,256]{1,0:T(8,128)(2,1)}, bf16[128,256]{1,0:T(8,128)(2,1)S(1)}, u32[]{:S(2)}) copy-start(bf16[128,256]{1,0:T(8,128)(2,1)S(1)} %convert_element_type.27.rest_0_) | copy-start | bytes 196612
  1.5 21.9 %collective-permute-start.2 = (bf16[128,256]{1,0:T(8,128)(2,1)S(1)}, bf16[128,256]{1,0:T(8,128)(2,1)S(1)}, u32[]{:S(2)}, u32[]{:S(2)}) collective-permute-start(bf16[128,256]{1,0:T(8,128)(2,1)S(1)} %convert_element_type.27.rest_0_), channel_id=1, source_target_pairs={{0,3},{1,2},{2,1},{3,0},{4,7},{5,6},{6,5},{7,4},{8,11},{9,10},{10,... | collective-permute-start | bytes 196616 | tf_op jit(solution)/shard_map/ppermute | solution.py:385
  6.7 16.8 %collective-permute-start.1 = (bf16[128,256]{1,0:T(8,128)(2,1)S(1)}, bf16[128,256]{1,0:T(8,128)(2,1)S(1)}, u32[]{:S(2)}, u32[]{:S(2)}) collective-permute-start(bf16[128,256]{1,0:T(8,128)(2,1)S(1)} %convert_element_type.27.rest_0_), channel_id=1, source_target_pairs={{0,2},{1,3},{2,0},{3,1},{4,6},{5,7},{6,4},{7,5},{8,10},{9,11},{10,... | collective-permute-start | bytes 196616 | tf_op jit(solution)/shard_map/ppermute | solution.py:385
  6.7 16.9 %collective-permute-start = (bf16[128,256]{1,0:T(8,128)(2,1)S(1)}, bf16[128,256]{1,0:T(8,128)(2,1)S(1)}, u32[]{:S(2)}, u32[]{:S(2)}) collective-permute-start(bf16[128,256]{1,0:T(8,128)(2,1)S(1)} %convert_element_type.27.rest_0_), channel_id=1, source_target_pairs={{0,1},{1,0},{2,3},{3,2},{4,5},{5,4},{6,7},{7,6},{8,9},{9,8},{10,11... | collective-permute-start | bytes 196616 | tf_op jit(solution)/shard_map/ppermute | solution.py:385
  10.0 8.6 %all-to-all-start = ((s32[8,1,192]{2,1,0:T(1,128)}), s32[8,1,192]{2,1,0:T(1,128)S(1)}, u32[]{:S(2)}, u32[]{:S(2)}) async-start(s32[8,1,192]{2,1,0:T(1,128)} %sub.24), calls=%async_computation | async-start | bytes 16384 | tf_op jit(solution)/shard_map/all_to_all | solution.py:353
  15.3 8.1 %copy-start = (s32[1,1024]{1,0:T(1,128)}, s32[1,1024]{1,0:T(1,128)S(1)}, u32[]{:S(2)}) copy-start(s32[1,1024]{1,0:T(1,128)S(1)} %fusion.6.place_ref.rest_5_) | copy-start | bytes 12292
  23.5 9.6 %copy-start.2 = (bf16[128,256]{1,0:T(8,128)(2,1)}, bf16[128,256]{1,0:T(8,128)(2,1)S(1)}, u32[]{:S(2)}) copy-start(bf16[128,256]{1,0:T(8,128)(2,1)S(1)} %collective-permute-done.2.rest_3_) | copy-start | bytes 196612
  23.5 9.6 %copy-start.3 = (bf16[128,256]{1,0:T(8,128)(2,1)}, bf16[128,256]{1,0:T(8,128)(2,1)S(1)}, u32[]{:S(2)}) copy-start(bf16[128,256]{1,0:T(8,128)(2,1)S(1)} %collective-permute-done.1.rest_2_) | copy-start | bytes 196612
  23.5 9.6 %copy-start.4 = (bf16[128,256]{1,0:T(8,128)(2,1)}, bf16[128,256]{1,0:T(8,128)(2,1)S(1)}, u32[]{:S(2)}) copy-start(bf16[128,256]{1,0:T(8,128)(2,1)S(1)} %collective-permute-done.rest_1_) | copy-start | bytes 196612
  23.5 11.7 %all-to-all-start.1 = ((bf16[8,192,128]{2,1,0:T(8,128)(2,1)}), bf16[8,192,128]{2,1,0:T(8,128)(2,1)S(1)}, u32[]{:S(2)}, u32[]{:S(2)}) async-start(bf16[8,192,128]{2,1,0:T(8,128)(2,1)} %bitcast.60), calls=%async_computation.1 | async-start | bytes 786432 | tf_op jit(solution)/shard_map/all_to_all | solution.py:353
  39.3 11.7 %all-to-all-start.2 = ((bf16[8,192,128]{2,1,0:T(8,128)(2,1)}), bf16[8,192,128]{2,1,0:T(8,128)(2,1)S(1)}, u32[]{:S(2)}, u32[]{:S(2)}) async-start(bf16[8,192,128]{2,1,0:T(8,128)(2,1)} %bitcast.62), calls=%async_computation.2 | async-start | bytes 786432 | tf_op jit(solution)/shard_map/all_to_all | solution.py:353
  53.2 11.8 %all-to-all-start.3 = ((bf16[8,192,128]{2,1,0:T(8,128)(2,1)}), bf16[8,192,128]{2,1,0:T(8,128)(2,1)S(1)}, u32[]{:S(2)}, u32[]{:S(2)}) async-start(bf16[8,192,128]{2,1,0:T(8,128)(2,1)} %bitcast.55), calls=%async_computation.3 | async-start | bytes 786432 | tf_op jit(solution)/shard_map/all_to_all | solution.py:353
  81.3 11.7 %all-to-all-start.4 = ((bf16[8,192,128]{2,1,0:T(8,128)(2,1)}), bf16[8,192,128]{2,1,0:T(8,128)(2,1)S(1)}, u32[]{:S(2)}, u32[]{:S(2)}) async-start(bf16[8,192,128]{2,1,0:T(8,128)(2,1)} %bitcast.63), calls=%async_computation.4 | async-start | bytes 786432 | tf_op jit(solution)/shard_map/all_to_all | solution.py:353
  95.1 11.7 %all-to-all-start.5 = ((bf16[8,192,128]{2,1,0:T(8,128)(2,1)}), bf16[8,192,128]{2,1,0:T(8,128)(2,1)S(1)}, u32[]{:S(2)}, u32[]{:S(2)}) async-start(bf16[8,192,128]{2,1,0:T(8,128)(2,1)} %bitcast.56), calls=%async_computation.5 | async-start | bytes 786432 | tf_op jit(solution)/shard_map/all_to_all | solution.py:353
  110.9 12.0 %all-to-all-start.6 = ((bf16[8,192,128]{2,1,0:T(8,128)(2,1)}), bf16[8,192,128]{2,1,0:T(8,128)(2,1)S(1)}, u32[]{:S(2)}, u32[]{:S(2)}) async-start(bf16[8,192,128]{2,1,0:T(8,128)(2,1)} %bitcast.64), calls=%async_computation.6 | async-start | bytes 786432 | tf_op jit(solution)/shard_map/all_to_all | solution.py:353
  125.1 11.7 %all-to-all-start.7 = ((bf16[8,192,128]{2,1,0:T(8,128)(2,1)}), bf16[8,192,128]{2,1,0:T(8,128)(2,1)S(1)}, u32[]{:S(2)}, u32[]{:S(2)}) async-start(bf16[8,192,128]{2,1,0:T(8,128)(2,1)} %bitcast.57), calls=%async_computation.7 | async-start | bytes 786432 | tf_op jit(solution)/shard_map/all_to_all | solution.py:353
  153.2 11.7 %all-to-all-start.8 = ((bf16[8,192,128]{2,1,0:T(8,128)(2,1)}), bf16[8,192,128]{2,1,0:T(8,128)(2,1)S(1)}, u32[]{:S(2)}, u32[]{:S(2)}) async-start(bf16[8,192,128]{2,1,0:T(8,128)(2,1)} %bitcast.59), calls=%async_computation.8 | async-start | bytes 786432 | tf_op jit(solution)/shard_map/all_to_all | solution.py:353
  167.0 11.7 %all-to-all-start.9 = ((bf16[8,192,128]{2,1,0:T(8,128)(2,1)}), bf16[8,192,128]{2,1,0:T(8,128)(2,1)S(1)}, u32[]{:S(2)}, u32[]{:S(2)}) async-start(bf16[8,192,128]{2,1,0:T(8,128)(2,1)} %bitcast.58), calls=%async_computation.9 | async-start | bytes 786432 | tf_op jit(solution)/shard_map/all_to_all | solution.py:353
  182.8 12.0 %all-to-all-start.10 = ((bf16[8,192,128]{2,1,0:T(8,128)(2,1)}), bf16[8,192,128]{2,1,0:T(8,128)(2,1)S(1)}, u32[]{:S(2)}, u32[]{:S(2)}) async-start(bf16[8,192,128]{2,1,0:T(8,128)(2,1)} %bitcast.61), calls=%async_computation.10 | async-start | bytes 786432 | tf_op jit(solution)/shard_map/all_to_all | solution.py:353

commit v2 on v1

--- a/solution.py
+++ b/solution.py
@@ -173,15 +173,16 @@
     product(matrix_ref, low[...], part_ref)
 
 
-def last_body(sign, base_ref, in_ref, row_ref, field_ref):
-    core = field_ref.shape[0]
-    first = pl.program_id(0) * core
-
-    def fields(at, c):
-        added = dot(hot_cols(row_ref[...], first + c, at.size), in_ref[...])
-        field_ref[at, :] = base_ref[at, :] + sign * added
-
-    chunks(core, fields, 2)
+def last_body(sign, base_ref, in_ref, row_ref, field_ref, made, sems):
+    stores = []
+    parts = sems.shape[0]
+    size = made.shape[0] // parts
+    for k in range(parts):
+        at = pl.ds(k * size, size)
+        added = dot(hot_cols(row_ref[...], k * size, size), in_ref[...])
+        made[at, :] = base_ref[at, :] + sign * added
+        stores += begin(sems, k, [(made.at[at], field_ref.at[at])])
+    finish(stores)
 
 
 def take_margins(in_ref, column_ref, margin_ref):
@@ -251,10 +252,11 @@
     return x[:, :half] + x[:, half:]
 
 
-def coarse_body(side, here_ref, all_ref, *rest):
+def coarse_body(side, place_count, here_ref, *rest):
+    pairs, rest = rest[:place_count], rest[place_count:]
     inverse_refs = rest[:side]
     margin_ref, place_ref, matrix_ref, part_ref, modes_ref, coarse_ref, out_ref = rest[side : side + 7]
-    inverse, margin, place, matrix, part, modes, made, outer, packed, sems = rest[side + 7 :]
+    inverse, everyone, margin, place, matrix, part, modes, made, outer, packed, sems = rest[side + 7 :]
     subs, count, margins = modes.shape
     core = matrix_ref.shape[1] - margins
     loads = begin(
@@ -268,12 +270,17 @@
             (place_ref, place),
         ],
     )
+    height = made.shape[0]
+    for k, pair_ref in enumerate(pairs):
+        for j in range(2):
+            at = pl.multiple_of((here_ref[1] ^ (2 * k + j)) * height, height)
+            everyone[pl.ds(at, height), :] = pair_ref[j * height : (j + 1) * height, :]
     finish(loads[:side])
     value = 0.0
     for k in range(side):
         width = inverse.shape[2]
         at = pl.multiple_of((here_ref[0] ^ k) * width, width)
-        value += dot(inverse[k], all_ref[pl.ds(at, width), :])
+        value += dot(inverse[k], everyone[pl.ds(at, width), :])
     made[...] = value
     stores = begin(sems, side + 5, [(made, coarse_ref)])
     halves = split(value)
@@ -379,12 +386,11 @@
         7, slot_flops, 4e6,
     )(wanted_row, place_row, start)
     side = lax.axis_size("narrow")
-    here = lax.axis_index("narrow").reshape(1).astype(i32)
-    own = coarse_inverse.astype(bf16)
+    here = jnp.stack([lax.axis_index("narrow"), lax.axis_index("wide")]).astype(i32)
+    begun, own, going = lax.optimization_barrier((start, coarse_inverse.astype(bf16), going))
     pieces = [own] + [
         lax.ppermute(own, "narrow", [(i, i ^ k) for i in range(side)]) for k in range(1, side)
     ]
-    begun, pieces, going = lax.optimization_barrier((start, pieces, going))
     part = call(
         open_body, (subs,), [rows_spec, left_spec], part_spec, part_shape, [], matrix_flops, 10e6,
     )(begun, stiffness)
@@ -411,7 +417,7 @@
     part_outer_spec = pl.BlockSpec((subs, margins, cols), lambda s: (0, m_at, 0))
     outer_scratch = [pltpu.VMEM((many, cols), bf16)]
 
-    def inner(sign, base, margin, part, matrices, coarse):
+    def inner(sign, base, margin, part, matrices, coarse, near_out=(1,)):
         specs = [
             pl.BlockSpec((1, core, cols), lambda s: (s, 0, 0)),
             pl.BlockSpec((1, core, margins), lambda s: (s, 0, m_at)),
@@ -430,7 +436,7 @@
             functools.partial(inner_body, sign, coarse is not None), (subs,), specs, [rows_spec, slots_spec],
             [held_shape, jax.ShapeDtypeStruct((slots, cols), f32)],
             [pltpu.VMEM((core, 2 * cols), bf16), pltpu.VMEM((slots, 2 * cols), f32)], 2 * slot_flops, 8e6,
-            (4,), (1,),
+            (4,), near_out,
         )(*args)
 
     def relay(sign, sent, came):
@@ -458,11 +464,13 @@
     field = start
     for step in range(ITERS + 1):
         came = trade(going)
-        if step > 0:
+        if step == 0:
+            pieces, came = lax.optimization_barrier((pieces, came))
+        else:
             field, part = settle(1.0, base, back, stiffness, False)
         margin, going = stiffness_outer(came, part)
         back = trade(going)
-        base, sent = inner(-1.0, loads, margin, part, stiffness, None)
+        base, sent = inner(-1.0, loads, margin, part, stiffness, None, (0,) if step == ITERS else (1,))
         if step == ITERS:
             break
 
@@ -477,22 +485,29 @@
             ],
             5, slot_flops // 2, 2e6,
         )(came, place_column, modes_turned, proj)
-        everyone = lax.all_gather(projection, "wide", axis=0, tiled=True)
+        partner = lax.ppermute(projection, "wide", [(i, i ^ 1) for i in range(owners)])
+        pair = jnp.concatenate([projection, partner], axis=0)
+        pairs = [pair] + [
+            lax.ppermute(pair, "wide", [(i, i ^ k) for i in range(owners)]) for k in range(2, owners, 2)
+        ]
         coarse, going = flat_call(
-            functools.partial(coarse_body, side), (1,), [jax.ShapeDtypeStruct((coarse_rows, cols), f32), slots_low], (),
-            [pltpu.VMEM((side,) + coarse_inverse.shape, bf16), margin_scratch, pltpu.VMEM((1, many), i32)]
+            functools.partial(coarse_body, side, len(pairs)), tuple(range(1, len(pairs) + 1)), [jax.ShapeDtypeStruct((coarse_rows, cols), f32), slots_low], (),
+            [
+                pltpu.VMEM((side,) + coarse_inverse.shape, bf16), pltpu.VMEM((owners * coarse_rows, cols), bf16),
+                margin_scratch, pltpu.VMEM((1, many), i32),
+            ]
             + corner_scratch
             + [modes_scratch, pltpu.VMEM((coarse_rows, cols), f32), margin_scratch, packed_scratch],
             side + 8, slot_flops, 3e6, (0,),
-        )(here, everyone, *pieces, margin, place_row, local_inverse, part, modes_turned)
+        )(here, *pairs, *pieces, margin, place_row, local_inverse, part, modes_turned)
         back = trade(going)
         base, sent = inner(1.0, field, margin, part, local_inverse, coarse)
         going = relay(1.0, sent, back)
 
-    final = call(
-        functools.partial(last_body, -1.0), (subs,), [rows_spec, slots_spec, whole((1, slots))], rows_spec,
-        held_shape, [], slot_flops, 4e6, (1, 2),
-    )(base, back, wanted_row)
+    final = flat_call(
+        functools.partial(last_body, -1.0), (0, 1, 2), [held_shape], (), [pltpu.VMEM((held, cols), f32)], 2 * subs,
+        slot_flops, 4e6,
+    )(base, back, wanted_row)[0]
     return field, final
 
 

time: 203 us -> 198 us (0.975)
  blocking collectives: 19.8 us -> 0 us
  starting transfers between devices: 45.1 us -> 53.6 us
  waiting for transfers between devices: 12.1 us -> 18.2 us
    all_gather x2 -> x0, blocking collectives: 19.8 us -> none  [shards(): everyone = lax.all_gather(projection, 'wide', axis=0, tiled=True)]
    ppermute x0 -> x8, waiting for transfers between devices: none -> 8.75 us  [the longest x6 8.13 us: shards(): lax.ppermute(pair, 'wide', [(i, i ^ k) for i in range(owners)])]
    ppermute x0 -> x8, starting transfers between devices: none -> 7.87 us  [the longest x6 6.98 us: shards(): lax.ppermute(pair, 'wide', [(i, i ^ k) for i in range(owners)])]
    pallas_call x11 -> x10, Pallas kernels: 78.9 us -> 73.3 us  [call(): run(*(placed(i, x, spec) for i, (x, spec) in enumerate(zip(args, in_specs...]
    pallas_call x12 -> x13, Pallas kernels: 38.1 us -> 42.7 us  [run(): pl.pallas_call(body, in_specs=[pl.BlockSpec(memory_space=p) for p in plac...]
    all_to_all x11, waiting for transfers between devices: 12.1 us -> 9.44 us  [trade(): lax.all_to_all(blocks, 'wide', split_axis=0, concat_axis=0, tiled=True)]
  transfers between devices with their start and end apart: 14 -> 22, of which waited for: 9 -> 16; matrix products, arithmetic and copies ran while one was open for 2% -> 2% of each run, Pallas kernels for 39% -> 37%
where the time goes in v2:
time: 198 us; the launch traced here: 196 us
  Pallas kernels  116 us (59%)
  starting transfers between devices  53.6 us (27%)
  waiting for transfers between devices  18.2 us (9%)
  other arithmetic  3.27 us (2%)
  local copies, waits for them, and re-layouts  3.02 us (2%)
    pallas_call x10, Pallas kernels, call(): run(*(placed(i, x, spec) for i, (x, spec) in enumerate(zip(args, in_specs...  73.3 us
    pallas_call x13, Pallas kernels, run(): pl.pallas_call(body, in_specs=[pl.BlockSpec(memory_space=p) for p in plac...  42.7 us
    all_to_all x11, starting transfers between devices, trade(): lax.all_to_all(blocks, 'wide', split_axis=0, concat_axis=0, tiled=True)  41.3 us
    all_to_all x11, waiting for transfers between devices, trade(): lax.all_to_all(blocks, 'wide', split_axis=0, concat_axis=0, tiled=True)  9.44 us
    ppermute x6, waiting for transfers between devices, shards(): lax.ppermute(pair, 'wide', [(i, i ^ k) for i in range(owners)])  8.13 us
    ppermute x6, starting transfers between devices, shards(): lax.ppermute(pair, 'wide', [(i, i ^ k) for i in range(owners)])  6.98 us
    ppermute x3, starting transfers between devices, shards(): lax.ppermute(own, 'narrow', [(i, i ^ k) for i in range(side)])  4.45 us
  transfers between devices with their start and end apart: 22, of which 16 were waited for; matrix products, arithmetic and copies ran while one was open for 2% of the time, Pallas kernels for 37%

profile of v2, /device:TPU:0, one launch (start us, length us, event | category | flops | bytes accessed | tf_op | source)
XLA Modules:
  0.0 195.6 jit_solution(17579032433628923712)
XLA Ops:
  0.6 0.7 copy.9
  1.3 0.5 fusion.2
  1.8 0.8 select_reduce_fusion
  2.7 0.7 sub.24
  3.4 5.2 %all-to-all-start = ((s32[8,1,192]{2,1,0:T(1,128)}), s32[8,1,192]{2,1,0:T(1,128)S(1)}, u32[]{:S(2)}, u32[]{:S(2)}) async-start(s32[8,1,192]{2,1,0:T(1,128)} %sub.24), calls=%async_computation | async-start | bytes 16384 | tf_op jit(solution)/shard_map/all_to_all | solution.py:360
  8.5 0.7 fusion.9
  9.2 0.7 divide_bitcast_fusion
  10.0 0.9 convert_element_type.27.rest_4_
  10.9 2.3 %all-to-all-done = s32[8,1,192]{2,1,0:T(1,128)S(1)} async-done(((s32[8,1,192]{2,1,0:T(1,128)}), s32[8,1,192]{2,1,0:T(1,128)S(1)}, u32[]{:S(2)}, u32[]{:S(2)}) %all-to-all-start) | async-done | bytes 6176 | tf_op jit(solution)/shard_map/all_to_all | solution.py:360
  13.3 4.7 %shard_map.86 = (bf16[1536,128]{1,0:T(8,128)(2,1)}, s32[1536,128]{1,0:T(8,128)S(1)}, s32[1024,128]{1,0:T(8,128)}) custom-call(s32[1,1536]{1,0:T(1,128)S(1)} %broadcast_in_dim_reshape.3.row_ref, s32[1,1024]{1,0:T(1,128)S(1)} %fusion.6.place_ref.rest_9_, f32[3072,128]{1,0:T(8,128)} %base_ref.5), custom_call_target="tpu_custom_call" | custom-call | flops 1207959552 | bytes 4000000 | tf_op jit(solution)/shard_map/pallas_call | solution.py:88
  18.1 3.5 %all-to-all-start.1 = ((bf16[8,192,128]{2,1,0:T(8,128)(2,1)}), bf16[8,192,128]{2,1,0:T(8,128)(2,1)S(1)}, u32[]{:S(2)}, u32[]{:S(2)}) async-start(bf16[8,192,128]{2,1,0:T(8,128)(2,1)} %bitcast.60), calls=%async_computation.1 | async-start | bytes 786432 | tf_op jit(solution)/shard_map/all_to_all | solution.py:360
  21.6 3.7 %collective-permute-start.2 = (bf16[128,256]{1,0:T(8,128)(2,1)S(1)}, bf16[128,256]{1,0:T(8,128)(2,1)S(1)}, u32[]{:S(2)}, u32[]{:S(2)}) collective-permute-start(bf16[128,256]{1,0:T(8,128)(2,1)S(1)} %convert_element_type.27.rest_4_), channel_id=1, source_target_pairs={{0,3},{1,2},{2,1},{3,0},{4,7},{5,6},{6,5},{7,4},{8,11},{9,10},{10,... | collective-permute-start | bytes 196616 | tf_op jit(solution)/shard_map/ppermute | solution.py:392
  25.2 0.8 collective-permute-start
  26.0 6.1 %shard_map.87.part_ref = f32[4,1024,128]{2,1,0:T(8,128)} custom-call(f32[3072,128]{1,0:T(8,128)} %base_ref.5, bf16[4,1024,1024]{2,1,0:T(8,128)(2,1)} %matrix_ref.25), custom_call_target="tpu_custom_call" | custom-call | flops 805306368 | bytes 10000000 | tf_op jit(solution)/shard_map/pallas_call | solution.py:79
  32.2 4.1 %shard_map.88 = (bf16[1024,128]{1,0:T(8,128)(2,1)}, bf16[1536,128]{1,0:T(8,128)(2,1)}) custom-call(bf16[1536,128]{1,0:T(8,128)(2,1)S(1)} %bitcast.42, s32[1024,128]{1,0:T(8,128)} %get-tuple-element.49.placed_ref, s32[1,1024]{1,0:T(1,128)} %copy-done, bf16[4,1024,1024]{2,1,0:T(8,128)(2,1)} %matrix_ref.25, f32[4,1024,128]{2,1,0:T(8,128)} %shard_map.87.part_ref), custom_call_target="tpu_custom_call" | custom-call | flops 1207959552 | bytes 3000000 | tf_op jit(solution)/shard_map/pallas_call | solution.py:88
  36.3 4.1 %all-to-all-start.2 = ((bf16[8,192,128]{2,1,0:T(8,128)(2,1)}), bf16[8,192,128]{2,1,0:T(8,128)(2,1)S(1)}, u32[]{:S(2)}, u32[]{:S(2)}) async-start(bf16[8,192,128]{2,1,0:T(8,128)(2,1)} %bitcast.64), calls=%async_computation.2 | async-start | bytes 786432 | tf_op jit(solution)/shard_map/all_to_all | solution.py:360
  40.3 6.9 %shard_map.89 = (f32[3072,128]{1,0:T(8,128)}, f32[1536,128]{1,0:T(8,128)S(1)}) custom-call(f32[4,1024,128]{2,1,0:T(8,128)} %shard_map.87.part_ref, bf16[4,1024,1024]{2,1,0:T(8,128)(2,1)} %matrix_ref.25, bf16[1024,128]{1,0:T(8,128)(2,1)} %get-tuple-element.50.margin_ref, f32[3072,128]{1,0:T(8,128)} %base_ref.7, s32[1536,128]{1,0:T(8,128)S(1)} %get-tuple-element.51.column_ref), custom_call_target="tpu_custom_call" | custom-call | flops 2415919104 | bytes 8000000 | tf_op jit(solution)/shard_map/pallas_call | solution.py:79
  47.2 1.5 all-to-all-done.2
  48.7 2.1 %shard_map.91 = bf16[1536,128]{1,0:T(8,128)(2,1)} custom-call(f32[1536,128]{1,0:T(8,128)S(1)} %get-tuple-element.55.sent_ref, bf16[1536,128]{1,0:T(8,128)(2,1)S(1)} %bitcast.34, s32[1536,128]{1,0:T(8,128)S(1)} %get-tuple-element.51.column_ref, s32[1,1536]{1,0:T(1,128)S(1)} %broadcast_in_dim_reshape.3.row_ref), custom_call_target="tpu_custom_call" | custom-call | flops 603979776 | bytes 3000000 | tf_op jit(solution)/shard_map/pallas_call | solution.py:88
  50.8 3.5 %all-to-all-start.3 = ((bf16[8,192,128]{2,1,0:T(8,128)(2,1)}), bf16[8,192,128]{2,1,0:T(8,128)(2,1)S(1)}, u32[]{:S(2)}, u32[]{:S(2)}) async-start(bf16[8,192,128]{2,1,0:T(8,128)(2,1)} %bitcast.56), calls=%async_computation.3 | async-start | bytes 786432 | tf_op jit(solution)/shard_map/all_to_all | solution.py:360
  54.3 8.3 %shard_map.90 = (f32[4,1024,128]{2,1,0:T(8,128)}, f32[128,128]{1,0:T(8,128)}) custom-call(f32[3072,128]{1,0:T(8,128)} %get-tuple-element.52.base_ref, bf16[1536,128]{1,0:T(8,128)(2,1)S(1)} %bitcast.35, s32[1,1536]{1,0:T(1,128)S(1)} %broadcast_in_dim_reshape.3.row_ref, bf16[4,1024,1024]{2,1,0:T(8,128)(2,1)} %matrix_ref.22, bf16[4,32,1024]{2,1,0:T(8,128)(2,1)} %bitcast.48), custom_call_target="tpu_custom_call" | custom-call | flops 2013265920 | bytes 14000000 | tf_op jit(solution)/shard_map/pallas_call | solution.py:79
  62.6 2.8 %shard_map.92 = (bf16[1024,128]{1,0:T(8,128)(2,1)}, bf16[128,128]{1,0:T(8,128)(2,1)}) custom-call(bf16[1536,128]{1,0:T(8,128)(2,1)S(1)} %bitcast.45, s32[1024,128]{1,0:T(8,128)} %get-tuple-element.49.placed_ref, bf16[4,32,1024]{2,1,0:T(8,128)(2,1)} %bitcast.49, f32[128,128]{1,0:T(8,128)} %get-tuple-element.56.proj_ref), custom_call_target="tpu_custom_call" | custom-call | flops 603979776 | bytes 2000000 | tf_op jit(solution)/shard_map/pallas_call | solution.py:88
  65.5 0.4 collective-permute-start.3
  65.9 0.8 constant_dynamic-update-slice_fusion.1
  67.0 2.8 %collective-permute-start.6 = (bf16[256,128]{1,0:T(8,128)(2,1)S(1)}, bf16[256,128]{1,0:T(8,128)(2,1)S(1)}, u32[]{:S(2)}, u32[]{:S(2)}) collective-permute-start(bf16[256,128]{1,0:T(8,128)(2,1)S(1)} %constant_dynamic-update-slice_fusion.rest_0_), channel_id=1, source_target_pairs={{0,24},{4,28},{8,16},{12,20},{16,8},{20,12},{24,0},{28,4},{1,25},{... | collective-permute-start | bytes 196616 | tf_op jit(solution)/shard_map/ppermute | solution.py:491
  69.8 0.5 collective-permute-start.5
  70.6 1.7 collective-permute-done.6.rest_3_
  72.2 1.8 collective-permute-done.5.rest_2_
  74.0 0.5 collective-permute-done.4.rest_1_
  74.6 4.1 %shard_map.93 = (f32[128,128]{1,0:T(8,128)}, bf16[1536,128]{1,0:T(8,128)(2,1)}) custom-call(s32[2]{0:T(128)S(1)} %pad_add_fusion.here_ref, bf16[256,128]{1,0:T(8,128)(2,1)S(1)} %constant_dynamic-update-slice_fusion.rest_0_, bf16[256,128]{1,0:T(8,128)(2,1)S(1)} %collective-permute-done.4.rest_1_, bf16[256,128]{1,0:T(8,128)(2,1)S(1)} %collective-permute-done.5.rest_2_, ...), custom_call_target="tpu_custom_call" | custom-call | flops 1207959552 | bytes 3000000 | tf_op jit(solution)/shard_map/pallas_call | solution.py:88
  78.7 3.6 %all-to-all-start.4 = ((bf16[8,192,128]{2,1,0:T(8,128)(2,1)}), bf16[8,192,128]{2,1,0:T(8,128)(2,1)S(1)}, u32[]{:S(2)}, u32[]{:S(2)}) async-start(bf16[8,192,128]{2,1,0:T(8,128)(2,1)} %bitcast.62), calls=%async_computation.4 | async-start | bytes 786432 | tf_op jit(solution)/shard_map/all_to_all | solution.py:360
  82.3 7.2 %shard_map.94 = (f32[3072,128]{1,0:T(8,128)}, f32[1536,128]{1,0:T(8,128)S(1)}) custom-call(f32[4,1024,128]{2,1,0:T(8,128)} %get-tuple-element.54.rest_11_.part_ref, bf16[4,1024,1024]{2,1,0:T(8,128)(2,1)} %matrix_ref.22, bf16[1024,128]{1,0:T(8,128)(2,1)} %get-tuple-element.57.rest_8_.margin_ref, f32[3072,128]{1,0:T(8,128)} %base_ref.5, ...), custom_call_target="tpu_custom_call" | custom-call | flops 2415919104 | bytes 8000000 | tf_op jit(solution)/shard_map/pallas_call | solution.py:79
  89.5 0.9 all-to-all-done.4
  90.4 2.1 %shard_map.96 = bf16[1536,128]{1,0:T(8,128)(2,1)} custom-call(f32[1536,128]{1,0:T(8,128)S(1)} %get-tuple-element.67.sent_ref, bf16[1536,128]{1,0:T(8,128)(2,1)S(1)} %bitcast.40, s32[1536,128]{1,0:T(8,128)S(1)} %get-tuple-element.51.column_ref, s32[1,1536]{1,0:T(1,128)S(1)} %broadcast_in_dim_reshape.3.row_ref), custom_call_target="tpu_custom_call" | custom-call | flops 603979776 | bytes 3000000 | tf_op jit(solution)/shard_map/pallas_call | solution.py:88
  92.5 3.5 %all-to-all-start.5 = ((bf16[8,192,128]{2,1,0:T(8,128)(2,1)}), bf16[8,192,128]{2,1,0:T(8,128)(2,1)S(1)}, u32[]{:S(2)}, u32[]{:S(2)}) async-start(bf16[8,192,128]{2,1,0:T(8,128)(2,1)} %bitcast.57), calls=%async_computation.5 | async-start | bytes 786432 | tf_op jit(solution)/shard_map/all_to_all | solution.py:360
  96.0 7.8 %shard_map.95 = (f32[3072,128]{1,0:T(8,128)}, f32[4,1024,128]{2,1,0:T(8,128)}) custom-call(f32[3072,128]{1,0:T(8,128)} %get-tuple-element.64.base_ref, bf16[1536,128]{1,0:T(8,128)(2,1)S(1)} %bitcast.41, s32[1,1536]{1,0:T(1,128)S(1)} %broadcast_in_dim_reshape.3.row_ref, bf16[4,1024,1024]{2,1,0:T(8,128)(2,1)} %matrix_ref.25), custom_call_target="tpu_custom_call" | custom-call | flops 2013265920 | bytes 14000000 | tf_op jit(solution)/shard_map/pallas_call | solution.py:79
  103.8 0.4 all-to-all-done.5
  104.3 4.0 %shard_map.97 = (bf16[1024,128]{1,0:T(8,128)(2,1)}, bf16[1536,128]{1,0:T(8,128)(2,1)}) custom-call(bf16[1536,128]{1,0:T(8,128)(2,1)S(1)} %bitcast.44, s32[1024,128]{1,0:T(8,128)} %get-tuple-element.49.placed_ref, s32[1,1024]{1,0:T(1,128)} %copy-done, bf16[4,1024,1024]{2,1,0:T(8,128)(2,1)} %matrix_ref.25, f32[4,1024,128]{2,1,0:T(8,128)} %get-tuple-element.66.part_ref), custom_call_target="tpu_custom_call" | custom-call | flops 1207959552 | bytes 3000000 | tf_op jit(solution)/shard_map/pallas_call | solution.py:88
  108.3 3.7 %all-to-all-start.6 = ((bf16[8,192,128]{2,1,0:T(8,128)(2,1)}), bf16[8,192,128]{2,1,0:T(8,128)(2,1)S(1)}, u32[]{:S(2)}, u32[]{:S(2)}) async-start(bf16[8,192,128]{2,1,0:T(8,128)(2,1)} %bitcast.65), calls=%async_computation.6 | async-start | bytes 786432 | tf_op jit(solution)/shard_map/all_to_all | solution.py:360
  112.0 6.9 %shard_map.98 = (f32[3072,128]{1,0:T(8,128)}, f32[1536,128]{1,0:T(8,128)S(1)}) custom-call(f32[4,1024,128]{2,1,0:T(8,128)} %get-tuple-element.66.part_ref, bf16[4,1024,1024]{2,1,0:T(8,128)(2,1)} %matrix_ref.25, bf16[1024,128]{1,0:T(8,128)(2,1)} %get-tuple-element.68.margin_ref, f32[3072,128]{1,0:T(8,128)} %base_ref.7, ...), custom_call_target="tpu_custom_call" | custom-call | flops 2415919104 | bytes 8000000 | tf_op jit(solution)/shard_map/pallas_call | solution.py:79
  118.8 1.5 all-to-all-done.6
  120.3 2.2 %shard_map.100 = bf16[1536,128]{1,0:T(8,128)(2,1)} custom-call(f32[1536,128]{1,0:T(8,128)S(1)} %get-tuple-element.72.sent_ref, bf16[1536,128]{1,0:T(8,128)(2,1)S(1)} %bitcast.36, s32[1536,128]{1,0:T(8,128)S(1)} %get-tuple-element.51.column_ref, s32[1,1536]{1,0:T(1,128)S(1)} %broadcast_in_dim_reshape.3.row_ref), custom_call_target="tpu_custom_call" | custom-call | flops 603979776 | bytes 3000000 | tf_op jit(solution)/shard_map/pallas_call | solution.py:88
  122.5 3.5 %all-to-all-start.7 = ((bf16[8,192,128]{2,1,0:T(8,128)(2,1)}), bf16[8,192,128]{2,1,0:T(8,128)(2,1)S(1)}, u32[]{:S(2)}, u32[]{:S(2)}) async-start(bf16[8,192,128]{2,1,0:T(8,128)(2,1)} %bitcast.58), calls=%async_computation.7 | async-start | bytes 786432 | tf_op jit(solution)/shard_map/all_to_all | solution.py:360
  126.0 8.3 %shard_map.99 = (f32[4,1024,128]{2,1,0:T(8,128)}, f32[128,128]{1,0:T(8,128)}) custom-call(f32[3072,128]{1,0:T(8,128)} %get-tuple-element.69.base_ref, bf16[1536,128]{1,0:T(8,128)(2,1)S(1)} %bitcast.37, s32[1,1536]{1,0:T(1,128)S(1)} %broadcast_in_dim_reshape.3.row_ref, bf16[4,1024,1024]{2,1,0:T(8,128)(2,1)} %matrix_ref.22, bf16[4,32,1024]{2,1,0:T(8,128)(2,1)} %bitcast.52), custom_call_target="tpu_custom_call" | custom-call | flops 2013265920 | bytes 14000000 | tf_op jit(solution)/shard_map/pallas_call | solution.py:79
  134.3 2.9 %shard_map.101 = (bf16[1024,128]{1,0:T(8,128)(2,1)}, bf16[128,128]{1,0:T(8,128)(2,1)}) custom-call(bf16[1536,128]{1,0:T(8,128)(2,1)S(1)} %bitcast.47, s32[1024,128]{1,0:T(8,128)} %get-tuple-element.49.placed_ref, bf16[4,32,1024]{2,1,0:T(8,128)(2,1)} %bitcast.53, f32[128,128]{1,0:T(8,128)} %get-tuple-element.73.proj_ref), custom_call_target="tpu_custom_call" | custom-call | flops 603979776 | bytes 2000000 | tf_op jit(solution)/shard_map/pallas_call | solution.py:88
  137.1 0.4 collective-permute-start.7
  137.6 0.8 constant_dynamic-update-slice_fusion.3
  138.7 2.8 %collective-permute-start.10 = (bf16[256,128]{1,0:T(8,128)(2,1)S(1)}, bf16[256,128]{1,0:T(8,128)(2,1)S(1)}, u32[]{:S(2)}, u32[]{:S(2)}) collective-permute-start(bf16[256,128]{1,0:T(8,128)(2,1)S(1)} %constant_dynamic-update-slice_fusion.2.rest_0_), channel_id=1, source_target_pairs={{0,24},{4,28},{8,16},{12,20},{16,8},{20,12},{24,0},{28,4},{1,25},{... | collective-permute-start | bytes 196616 | tf_op jit(solution)/shard_map/ppermute | solution.py:491
  141.5 0.5 collective-permute-start.9
  142.1 1.8 collective-permute-done.10.rest_3_
  143.9 1.8 collective-permute-done.9.rest_2_
  145.7 0.5 collective-permute-done.8.rest_1_
  146.2 4.1 %shard_map.102 = (f32[128,128]{1,0:T(8,128)}, bf16[1536,128]{1,0:T(8,128)(2,1)}) custom-call(s32[2]{0:T(128)S(1)} %pad_add_fusion.here_ref, bf16[256,128]{1,0:T(8,128)(2,1)S(1)} %constant_dynamic-update-slice_fusion.2.rest_0_, bf16[256,128]{1,0:T(8,128)(2,1)S(1)} %collective-permute-done.8.rest_1_, bf16[256,128]{1,0:T(8,128)(2,1)S(1)} %collective-permute-done.9.rest_2_, ...), custom_call_target="tpu_custom_call" | custom-call | flops 1207959552 | bytes 3000000 | tf_op jit(solution)/shard_map/pallas_call | solution.py:88
  150.3 3.7 %all-to-all-start.8 = ((bf16[8,192,128]{2,1,0:T(8,128)(2,1)}), bf16[8,192,128]{2,1,0:T(8,128)(2,1)S(1)}, u32[]{:S(2)}, u32[]{:S(2)}) async-start(bf16[8,192,128]{2,1,0:T(8,128)(2,1)} %bitcast.61), calls=%async_computation.8 | async-start | bytes 786432 | tf_op jit(solution)/shard_map/all_to_all | solution.py:360
  154.0 7.2 %shard_map.103 = (f32[3072,128]{1,0:T(8,128)}, f32[1536,128]{1,0:T(8,128)S(1)}) custom-call(f32[4,1024,128]{2,1,0:T(8,128)} %get-tuple-element.71.rest_11_.part_ref, bf16[4,1024,1024]{2,1,0:T(8,128)(2,1)} %matrix_ref.22, bf16[1024,128]{1,0:T(8,128)(2,1)} %get-tuple-element.74.rest_8_.margin_ref, f32[3072,128]{1,0:T(8,128)} %get-tuple-element.75.base_ref, ...), custom_call_target="tpu_custom_call" | custom-call | flops 2415919104 | bytes 8000000 | tf_op jit(solution)/shard_map/pallas_call | solution.py:79
  161.2 0.8 all-to-all-done.8
  162.1 2.1 %shard_map.105 = bf16[1536,128]{1,0:T(8,128)(2,1)} custom-call(f32[1536,128]{1,0:T(8,128)S(1)} %get-tuple-element.82.sent_ref, bf16[1536,128]{1,0:T(8,128)(2,1)S(1)} %bitcast.38, s32[1536,128]{1,0:T(8,128)S(1)} %get-tuple-element.51.column_ref, s32[1,1536]{1,0:T(1,128)S(1)} %broadcast_in_dim_reshape.3.row_ref), custom_call_target="tpu_custom_call" | custom-call | flops 603979776 | bytes 3000000 | tf_op jit(solution)/shard_map/pallas_call | solution.py:88
  164.2 3.5 %all-to-all-start.9 = ((bf16[8,192,128]{2,1,0:T(8,128)(2,1)}), bf16[8,192,128]{2,1,0:T(8,128)(2,1)S(1)}, u32[]{:S(2)}, u32[]{:S(2)}) async-start(bf16[8,192,128]{2,1,0:T(8,128)(2,1)} %bitcast.59), calls=%async_computation.9 | async-start | bytes 786432 | tf_op jit(solution)/shard_map/all_to_all | solution.py:360
  167.6 7.8 %shard_map.104 = (f32[3072,128]{1,0:T(8,128)}, f32[4,1024,128]{2,1,0:T(8,128)}) custom-call(f32[3072,128]{1,0:T(8,128)} %get-tuple-element.78.base_ref, bf16[1536,128]{1,0:T(8,128)(2,1)S(1)} %bitcast.39, s32[1,1536]{1,0:T(1,128)S(1)} %broadcast_in_dim_reshape.3.row_ref, bf16[4,1024,1024]{2,1,0:T(8,128)(2,1)} %matrix_ref.25), custom_call_target="tpu_custom_call" | custom-call | flops 2013265920 | bytes 14000000 | tf_op jit(solution)/shard_map/pallas_call | solution.py:79
  175.9 4.0 %shard_map.106 = (bf16[1024,128]{1,0:T(8,128)(2,1)}, bf16[1536,128]{1,0:T(8,128)(2,1)}) custom-call(bf16[1536,128]{1,0:T(8,128)(2,1)S(1)} %bitcast.43, s32[1024,128]{1,0:T(8,128)} %get-tuple-element.49.placed_ref, s32[1,1024]{1,0:T(1,128)} %copy-done, bf16[4,1024,1024]{2,1,0:T(8,128)(2,1)} %matrix_ref.25, f32[4,1024,128]{2,1,0:T(8,128)} %get-tuple-element.81.part_ref), custom_call_target="tpu_custom_call" | custom-call | flops 1207959552 | bytes 3000000 | tf_op jit(solution)/shard_map/pallas_call | solution.py:88
  180.0 3.7 %all-to-all-start.10 = ((bf16[8,192,128]{2,1,0:T(8,128)(2,1)}), bf16[8,192,128]{2,1,0:T(8,128)(2,1)S(1)}, u32[]{:S(2)}, u32[]{:S(2)}) async-start(bf16[8,192,128]{2,1,0:T(8,128)(2,1)} %bitcast.63), calls=%async_computation.10 | async-start | bytes 786432 | tf_op jit(solution)/shard_map/all_to_all | solution.py:360
  183.6 6.8 %shard_map.107 = (f32[3072,128]{1,0:T(8,128)S(1)}, f32[1536,128]{1,0:T(8,128)}) custom-call(f32[4,1024,128]{2,1,0:T(8,128)} %get-tuple-element.81.part_ref, bf16[4,1024,1024]{2,1,0:T(8,128)(2,1)} %matrix_ref.25, bf16[1024,128]{1,0:T(8,128)(2,1)} %get-tuple-element.83.margin_ref, f32[3072,128]{1,0:T(8,128)} %base_ref.7, ...), custom_call_target="tpu_custom_call" | custom-call | flops 2415919104 | bytes 8000000 | tf_op jit(solution)/shard_map/pallas_call | solution.py:79
  190.4 1.6 all-to-all-done.10
  192.0 3.5 %shard_map.108 = f32[3072,128]{1,0:T(8,128)} custom-call(f32[3072,128]{1,0:T(8,128)S(1)} %get-tuple-element.84.base_ref, bf16[1536,128]{1,0:T(8,128)(2,1)S(1)} %bitcast.46, s32[1,1536]{1,0:T(1,128)S(1)} %broadcast_in_dim_reshape.3.row_ref), custom_call_target="tpu_custom_call" | custom-call | flops 1207959552 | bytes 4000000 | tf_op jit(solution)/shard_map/pallas_call | solution.py:88
  (34 shorter events, 1.7 us)
Async XLA Ops:
  3.4 9.9 %all-to-all-start = ((s32[8,1,192]{2,1,0:T(1,128)}), s32[8,1,192]{2,1,0:T(1,128)S(1)}, u32[]{:S(2)}, u32[]{:S(2)}) async-start(s32[8,1,192]{2,1,0:T(1,128)} %sub.24), calls=%async_computation | async-start | bytes 16384 | tf_op jit(solution)/shard_map/all_to_all | solution.py:360
  10.0 8.1 %copy-start = (s32[1,1024]{1,0:T(1,128)}, s32[1,1024]{1,0:T(1,128)S(1)}, u32[]{:S(2)}) copy-start(s32[1,1024]{1,0:T(1,128)S(1)} %fusion.6.place_ref.rest_9_) | copy-start | bytes 12292
  10.9 14.3 %copy-start.1 = (bf16[128,256]{1,0:T(8,128)(2,1)}, bf16[128,256]{1,0:T(8,128)(2,1)S(1)}, u32[]{:S(2)}) copy-start(bf16[128,256]{1,0:T(8,128)(2,1)S(1)} %convert_element_type.27.rest_4_) | copy-start | bytes 196612
  18.1 14.1 %all-to-all-start.1 = ((bf16[8,192,128]{2,1,0:T(8,128)(2,1)}), bf16[8,192,128]{2,1,0:T(8,128)(2,1)S(1)}, u32[]{:S(2)}, u32[]{:S(2)}) async-start(bf16[8,192,128]{2,1,0:T(8,128)(2,1)} %bitcast.60), calls=%async_computation.1 | async-start | bytes 786432 | tf_op jit(solution)/shard_map/all_to_all | solution.py:360
  21.6 10.6 %collective-permute-start.2 = (bf16[128,256]{1,0:T(8,128)(2,1)S(1)}, bf16[128,256]{1,0:T(8,128)(2,1)S(1)}, u32[]{:S(2)}, u32[]{:S(2)}) collective-permute-start(bf16[128,256]{1,0:T(8,128)(2,1)S(1)} %convert_element_type.27.rest_4_), channel_id=1, source_target_pairs={{0,3},{1,2},{2,1},{3,0},{4,7},{5,6},{6,5},{7,4},{8,11},{9,10},{10,... | collective-permute-start | bytes 196616 | tf_op jit(solution)/shard_map/ppermute | solution.py:392
  25.2 6.9 %collective-permute-start.1 = (bf16[128,256]{1,0:T(8,128)(2,1)S(1)}, bf16[128,256]{1,0:T(8,128)(2,1)S(1)}, u32[]{:S(2)}, u32[]{:S(2)}) collective-permute-start(bf16[128,256]{1,0:T(8,128)(2,1)S(1)} %convert_element_type.27.rest_4_), channel_id=1, source_target_pairs={{0,2},{1,3},{2,0},{3,1},{4,6},{5,7},{6,4},{7,5},{8,10},{9,11},{10,... | collective-permute-start | bytes 196616 | tf_op jit(solution)/shard_map/ppermute | solution.py:392
  25.2 6.9 %collective-permute-start = (bf16[128,256]{1,0:T(8,128)(2,1)S(1)}, bf16[128,256]{1,0:T(8,128)(2,1)S(1)}, u32[]{:S(2)}, u32[]{:S(2)}) collective-permute-start(bf16[128,256]{1,0:T(8,128)(2,1)S(1)} %convert_element_type.27.rest_4_), channel_id=1, source_target_pairs={{0,1},{1,0},{2,3},{3,2},{4,5},{5,4},{6,7},{7,6},{8,9},{9,8},{10,11... | collective-permute-start | bytes 196616 | tf_op jit(solution)/shard_map/ppermute | solution.py:392
  32.1 4.1 %copy-start.2 = (bf16[128,256]{1,0:T(8,128)(2,1)}, bf16[128,256]{1,0:T(8,128)(2,1)S(1)}, u32[]{:S(2)}) copy-start(bf16[128,256]{1,0:T(8,128)(2,1)S(1)} %collective-permute-done.2.rest_7_) | copy-start | bytes 196612
  32.1 4.1 %copy-start.3 = (bf16[128,256]{1,0:T(8,128)(2,1)}, bf16[128,256]{1,0:T(8,128)(2,1)S(1)}, u32[]{:S(2)}) copy-start(bf16[128,256]{1,0:T(8,128)(2,1)S(1)} %collective-permute-done.1.rest_6_) | copy-start | bytes 196612
  32.2 4.1 %copy-start.4 = (bf16[128,256]{1,0:T(8,128)(2,1)}, bf16[128,256]{1,0:T(8,128)(2,1)S(1)}, u32[]{:S(2)}) copy-start(bf16[128,256]{1,0:T(8,128)(2,1)S(1)} %collective-permute-done.rest_5_) | copy-start | bytes 196612
  36.3 12.4 %all-to-all-start.2 = ((bf16[8,192,128]{2,1,0:T(8,128)(2,1)}), bf16[8,192,128]{2,1,0:T(8,128)(2,1)S(1)}, u32[]{:S(2)}, u32[]{:S(2)}) async-start(bf16[8,192,128]{2,1,0:T(8,128)(2,1)} %bitcast.64), calls=%async_computation.2 | async-start | bytes 786432 | tf_op jit(solution)/shard_map/all_to_all | solution.py:360
  50.8 11.8 %all-to-all-start.3 = ((bf16[8,192,128]{2,1,0:T(8,128)(2,1)}), bf16[8,192,128]{2,1,0:T(8,128)(2,1)S(1)}, u32[]{:S(2)}, u32[]{:S(2)}) async-start(bf16[8,192,128]{2,1,0:T(8,128)(2,1)} %bitcast.56), calls=%async_computation.3 | async-start | bytes 786432 | tf_op jit(solution)/shard_map/all_to_all | solution.py:360
  65.5 1.5 collective-permute-start.3
  67.0 5.2 %collective-permute-start.6 = (bf16[256,128]{1,0:T(8,128)(2,1)S(1)}, bf16[256,128]{1,0:T(8,128)(2,1)S(1)}, u32[]{:S(2)}, u32[]{:S(2)}) collective-permute-start(bf16[256,128]{1,0:T(8,128)(2,1)S(1)} %constant_dynamic-update-slice_fusion.rest_0_), channel_id=1, source_target_pairs={{0,24},{4,28},{8,16},{12,20},{16,8},{20,12},{24,0},{28,4},{1,25},{... | collective-permute-start | bytes 196616 | tf_op jit(solution)/shard_map/ppermute | solution.py:491
  69.8 4.3 %collective-permute-start.5 = (bf16[256,128]{1,0:T(8,128)(2,1)S(1)}, bf16[256,128]{1,0:T(8,128)(2,1)S(1)}, u32[]{:S(2)}, u32[]{:S(2)}) collective-permute-start(bf16[256,128]{1,0:T(8,128)(2,1)S(1)} %constant_dynamic-update-slice_fusion.rest_0_), channel_id=1, source_target_pairs={{0,16},{4,20},{8,24},{12,28},{16,0},{20,4},{24,8},{28,12},{1,17},{... | collective-permute-start | bytes 196616 | tf_op jit(solution)/shard_map/ppermute | solution.py:491
  70.3 4.3 %collective-permute-start.4 = (bf16[256,128]{1,0:T(8,128)(2,1)S(1)}, bf16[256,128]{1,0:T(8,128)(2,1)S(1)}, u32[]{:S(2)}, u32[]{:S(2)}) collective-permute-start(bf16[256,128]{1,0:T(8,128)(2,1)S(1)} %constant_dynamic-update-slice_fusion.rest_0_), channel_id=1, source_target_pairs={{0,8},{4,12},{8,0},{12,4},{16,24},{20,28},{24,16},{28,20},{1,9},{5... | collective-permute-start | bytes 196616 | tf_op jit(solution)/shard_map/ppermute | solution.py:491
  78.7 11.7 %all-to-all-start.4 = ((bf16[8,192,128]{2,1,0:T(8,128)(2,1)}), bf16[8,192,128]{2,1,0:T(8,128)(2,1)S(1)}, u32[]{:S(2)}, u32[]{:S(2)}) async-start(bf16[8,192,128]{2,1,0:T(8,128)(2,1)} %bitcast.62), calls=%async_computation.4 | async-start | bytes 786432 | tf_op jit(solution)/shard_map/all_to_all | solution.py:360
  92.5 11.7 %all-to-all-start.5 = ((bf16[8,192,128]{2,1,0:T(8,128)(2,1)}), bf16[8,192,128]{2,1,0:T(8,128)(2,1)S(1)}, u32[]{:S(2)}, u32[]{:S(2)}) async-start(bf16[8,192,128]{2,1,0:T(8,128)(2,1)} %bitcast.57), calls=%async_computation.5 | async-start | bytes 786432 | tf_op jit(solution)/shard_map/all_to_all | solution.py:360
  108.3 12.0 %all-to-all-start.6 = ((bf16[8,192,128]{2,1,0:T(8,128)(2,1)}), bf16[8,192,128]{2,1,0:T(8,128)(2,1)S(1)}, u32[]{:S(2)}, u32[]{:S(2)}) async-start(bf16[8,192,128]{2,1,0:T(8,128)(2,1)} %bitcast.65), calls=%async_computation.6 | async-start | bytes 786432 | tf_op jit(solution)/shard_map/all_to_all | solution.py:360
  122.5 11.8 %all-to-all-start.7 = ((bf16[8,192,128]{2,1,0:T(8,128)(2,1)}), bf16[8,192,128]{2,1,0:T(8,128)(2,1)S(1)}, u32[]{:S(2)}, u32[]{:S(2)}) async-start(bf16[8,192,128]{2,1,0:T(8,128)(2,1)} %bitcast.58), calls=%async_computation.7 | async-start | bytes 786432 | tf_op jit(solution)/shard_map/all_to_all | solution.py:360
  137.1 1.5 collective-permute-start.7
  138.7 5.2 %collective-permute-start.10 = (bf16[256,128]{1,0:T(8,128)(2,1)S(1)}, bf16[256,128]{1,0:T(8,128)(2,1)S(1)}, u32[]{:S(2)}, u32[]{:S(2)}) collective-permute-start(bf16[256,128]{1,0:T(8,128)(2,1)S(1)} %constant_dynamic-update-slice_fusion.2.rest_0_), channel_id=1, source_target_pairs={{0,24},{4,28},{8,16},{12,20},{16,8},{20,12},{24,0},{28,4},{1,25},{... | collective-permute-start | bytes 196616 | tf_op jit(solution)/shard_map/ppermute | solution.py:491
  141.5 4.3 %collective-permute-start.9 = (bf16[256,128]{1,0:T(8,128)(2,1)S(1)}, bf16[256,128]{1,0:T(8,128)(2,1)S(1)}, u32[]{:S(2)}, u32[]{:S(2)}) collective-permute-start(bf16[256,128]{1,0:T(8,128)(2,1)S(1)} %constant_dynamic-update-slice_fusion.2.rest_0_), channel_id=1, source_target_pairs={{0,16},{4,20},{8,24},{12,28},{16,0},{20,4},{24,8},{28,12},{1,17},{... | collective-permute-start | bytes 196616 | tf_op jit(solution)/shard_map/ppermute | solution.py:491
  142.0 4.3 %collective-permute-start.8 = (bf16[256,128]{1,0:T(8,128)(2,1)S(1)}, bf16[256,128]{1,0:T(8,128)(2,1)S(1)}, u32[]{:S(2)}, u32[]{:S(2)}) collective-permute-start(bf16[256,128]{1,0:T(8,128)(2,1)S(1)} %constant_dynamic-update-slice_fusion.2.rest_0_), channel_id=1, source_target_pairs={{0,8},{4,12},{8,0},{12,4},{16,24},{20,28},{24,16},{28,20},{1,9},{5... | collective-permute-start | bytes 196616 | tf_op jit(solution)/shard_map/ppermute | solution.py:491
  150.3 11.7 %all-to-all-start.8 = ((bf16[8,192,128]{2,1,0:T(8,128)(2,1)}), bf16[8,192,128]{2,1,0:T(8,128)(2,1)S(1)}, u32[]{:S(2)}, u32[]{:S(2)}) async-start(bf16[8,192,128]{2,1,0:T(8,128)(2,1)} %bitcast.61), calls=%async_computation.8 | async-start | bytes 786432 | tf_op jit(solution)/shard_map/all_to_all | solution.py:360
  164.2 11.7 %all-to-all-start.9 = ((bf16[8,192,128]{2,1,0:T(8,128)(2,1)}), bf16[8,192,128]{2,1,0:T(8,128)(2,1)S(1)}, u32[]{:S(2)}, u32[]{:S(2)}) async-start(bf16[8,192,128]{2,1,0:T(8,128)(2,1)} %bitcast.59), calls=%async_computation.9 | async-start | bytes 786432 | tf_op jit(solution)/shard_map/all_to_all | solution.py:360
  180.0 12.0 %all-to-all-start.10 = ((bf16[8,192,128]{2,1,0:T(8,128)(2,1)}), bf16[8,192,128]{2,1,0:T(8,128)(2,1)S(1)}, u32[]{:S(2)}, u32[]{:S(2)}) async-start(bf16[8,192,128]{2,1,0:T(8,128)(2,1)} %bitcast.63), calls=%async_computation.10 | async-start | bytes 786432 | tf_op jit(solution)/shard_map/all_to_all | solution.py:360

commit v3 on v2

--- a/solution.py
+++ b/solution.py
@@ -144,8 +144,8 @@
     for k in range(parts):
         loads[k].wait()
         low[pl.ds(k * size, size), :] = field[pl.ds(k * size, size), :].astype(bf16)
-    size = made.shape[0] // parts
-    for k in range(parts):
+    size = made.shape[0] // 2
+    for k in range(2):
         at = pl.ds(k * size, size)
         made[at, :] = dot(hot_rows(column_ref[at, :], 0, low.shape[0]), low[...]).astype(bf16)
         stores += begin(sems, parts + 1 + k, [(made.at[at], out_ref.at[at])])
@@ -252,23 +252,54 @@
     return x[:, :half] + x[:, half:]
 
 
-def coarse_body(side, place_count, here_ref, *rest):
-    pairs, rest = rest[:place_count], rest[place_count:]
-    inverse_refs = rest[:side]
-    margin_ref, place_ref, matrix_ref, part_ref, modes_ref, coarse_ref, out_ref = rest[side : side + 7]
-    inverse, everyone, margin, place, matrix, part, modes, made, outer, packed, sems = rest[side + 7 :]
+def ready_body(
+    margin_ref, place_ref, matrix_ref, part_ref, modes_ref, solved_ref, lift_ref,
+    margin, place, matrix, part, modes, outer, solved, lift, sems,
+):
     subs, count, margins = modes.shape
     core = matrix_ref.shape[1] - margins
+    cols = part.shape[2]
+    finish(
+        begin(
+            sems, 0,
+            [
+                (margin_ref, margin),
+                (matrix_ref.at[:, core:, core:], matrix),
+                (part_ref.at[:, core:, :], part),
+                (modes_ref.at[:, :, core:], modes),
+                (place_ref, place),
+            ],
+        )
+    )
+    width = lift.shape[1]
+    rows = lax.broadcasted_iota(i32, (count, width), 0)
+    lanes = lax.broadcasted_iota(i32, (count, width), 1)
+    for s in range(subs):
+        at = pl.ds(s * margins, margins)
+        outer[at, : 2 * cols] = split(damping * (part[s] + dot(matrix[s], margin[at, :])))
+        own = (rows + s * count == lanes).astype(f32).astype(bf16)
+        outer[at, 2 * cols :] = turned_dot(modes[s], own).astype(bf16)
+    stores = []
+    size = solved.shape[0] // 2
+    for k in range(2):
+        at = pl.ds(k * size, size)
+        packed = dot(hot_cols(place[...], k * size, size), outer[...])
+        solved[at, :] = both(packed[:, : 2 * cols])
+        lift[at, :] = packed[:, 2 * cols :].astype(bf16)
+        stores += begin(
+            sems, 5 + 2 * k, [(solved.at[at], solved_ref.at[at]), (lift.at[at], lift_ref.at[at])]
+        )
+    finish(stores)
+
+
+def coarse_body(side, pair_count, here_ref, *rest):
+    pairs, rest = rest[:pair_count], rest[pair_count:]
+    inverse_refs = rest[:side]
+    solved_ref, lift_ref, coarse_ref, out_ref = rest[side : side + 4]
+    inverse, everyone, solved, lift, made, packed, sems = rest[side + 4 :]
     loads = begin(
         sems, 0,
-        [(inverse_refs[k], inverse.at[k]) for k in range(side)]
-        + [
-            (modes_ref.at[:, :, core:], modes),
-            (margin_ref, margin),
-            (matrix_ref.at[:, core:, core:], matrix),
-            (part_ref.at[:, core:, :], part),
-            (place_ref, place),
-        ],
+        [(inverse_refs[k], inverse.at[k]) for k in range(side)] + [(lift_ref, lift), (solved_ref, solved)],
     )
     height = made.shape[0]
     for k, pair_ref in enumerate(pairs):
@@ -282,15 +313,15 @@
         at = pl.multiple_of((here_ref[0] ^ k) * width, width)
         value += dot(inverse[k], everyone[pl.ds(at, width), :])
     made[...] = value
-    stores = begin(sems, side + 5, [(made, coarse_ref)])
+    stores = begin(sems, side + 2, [(made, coarse_ref)])
     halves = split(value)
     finish(loads[side:])
-    for s in range(subs):
-        at = pl.ds(s * margins, margins)
-        solved = part[s] + dot(matrix[s], margin[at, :])
-        lifted = both(turned_dot(modes[s], halves[s * count : (s + 1) * count]))
-        outer[at, :] = (damping * solved + lifted).astype(bf16)
-    finish(stores + pack(place, outer, packed, out_ref, sems, side + 6))
+    size = packed.shape[0] // 2
+    for k in range(2):
+        at = pl.ds(k * size, size)
+        packed[at, :] = (solved[at, :] + both(dot(lift[at, :], halves))).astype(bf16)
+        stores += begin(sems, side + 3 + k, [(packed.at[at], out_ref.at[at])])
+    finish(stores)
 
 
 def inner_body(sign, has_modes, part_ref, matrix_ref, margin_ref, base_ref, column_ref, *rest):
@@ -383,7 +414,7 @@
             pltpu.VMEM((held, cols), f32), pltpu.VMEM((held, cols), bf16), pltpu.VMEM((slots, cols), bf16),
             pltpu.VMEM((many, LANES), i32),
         ],
-        7, slot_flops, 4e6,
+        6, slot_flops, 4e6,
     )(wanted_row, place_row, start)
     side = lax.axis_size("narrow")
     here = jnp.stack([lax.axis_index("narrow"), lax.axis_index("wide")]).astype(i32)
@@ -490,16 +521,26 @@
         pairs = [pair] + [
             lax.ppermute(pair, "wide", [(i, i ^ k) for i in range(owners)]) for k in range(2, owners, 2)
         ]
+        solved, lift = flat_call(
+            ready_body, (),
+            [jax.ShapeDtypeStruct((slots, cols), f32), jax.ShapeDtypeStruct((slots, coarse_rows), bf16)], (),
+            [margin_scratch, pltpu.VMEM((1, many), i32)] + corner_scratch
+            + [
+                modes_scratch, pltpu.VMEM((many, 2 * cols + coarse_rows), bf16), pltpu.VMEM((slots, cols), f32),
+                pltpu.VMEM((slots, coarse_rows), bf16),
+            ],
+            9, slot_flops, 3e6,
+        )(margin, place_row, local_inverse, part, modes_turned)
         coarse, going = flat_call(
-            functools.partial(coarse_body, side, len(pairs)), tuple(range(1, len(pairs) + 1)), [jax.ShapeDtypeStruct((coarse_rows, cols), f32), slots_low], (),
+            functools.partial(coarse_body, side, len(pairs)), tuple(range(1, len(pairs) + 1)),
+            [jax.ShapeDtypeStruct((coarse_rows, cols), f32), slots_low], (),
             [
                 pltpu.VMEM((side,) + coarse_inverse.shape, bf16), pltpu.VMEM((owners * coarse_rows, cols), bf16),
-                margin_scratch, pltpu.VMEM((1, many), i32),
-            ]
-            + corner_scratch
-            + [modes_scratch, pltpu.VMEM((coarse_rows, cols), f32), margin_scratch, packed_scratch],
-            side + 8, slot_flops, 3e6, (0,),
-        )(here, *pairs, *pieces, margin, place_row, local_inverse, part, modes_turned)
+                pltpu.VMEM((slots, cols), f32), pltpu.VMEM((slots, coarse_rows), bf16),
+                pltpu.VMEM((coarse_rows, cols), f32), packed_scratch,
+            ],
+            side + 5, slot_flops // 4, 3e6, (0,),
+        )(here, *pairs, *pieces, solved, lift)
         back = trade(going)
         base, sent = inner(1.0, field, margin, part, local_inverse, coarse)
         going = relay(1.0, sent, back)

time: 198 us -> 198 us (level)
  waiting for transfers between devices: 18.2 us -> 10.9 us
  Pallas kernels: 116 us -> 123 us
    ppermute x6, waiting for transfers between devices: 8.13 us -> 0.02 us  [shards(): lax.ppermute(pair, 'wide', [(i, i ^ k) for i in range(owners)])]
    pallas_call x13 -> x15, Pallas kernels: 42.7 us -> 49.3 us  [run(): pl.pallas_call(body, in_specs=[pl.BlockSpec(memory_space=p) for p in plac...]
  transfers between devices with their start and end apart: 22 -> 22, of which waited for: 16 -> 10; matrix products, arithmetic and copies ran while one was open for 2% -> 2% of each run, Pallas kernels for 37% -> 42%
where the time goes in v3:
time: 198 us; the launch traced here: 196 us
  Pallas kernels  123 us (62%)
  starting transfers between devices  54.2 us (27%)
  waiting for transfers between devices  10.9 us (6%)
  other arithmetic  3.27 us (2%)
  local copies, waits for them, and re-layouts  3.02 us (2%)
    pallas_call x10, Pallas kernels, call(): run(*(placed(i, x, spec) for i, (x, spec) in enumerate(zip(args, in_specs...  73.3 us
    pallas_call x15, Pallas kernels, run(): pl.pallas_call(body, in_specs=[pl.BlockSpec(memory_space=p) for p in plac...  49.3 us
    all_to_all x11, starting transfers between devices, trade(): lax.all_to_all(blocks, 'wide', split_axis=0, concat_axis=0, tiled=True)  42.3 us
    all_to_all x11, waiting for transfers between devices, trade(): lax.all_to_all(blocks, 'wide', split_axis=0, concat_axis=0, tiled=True)  9.95 us
    ppermute x6, starting transfers between devices, shards(): lax.ppermute(pair, 'wide', [(i, i ^ k) for i in range(owners)])  6.98 us
    ppermute x3, starting transfers between devices, shards(): lax.ppermute(own, 'narrow', [(i, i ^ k) for i in range(side)])  4.45 us
  transfers between devices with their start and end apart: 22, of which 10 were waited for; matrix products, arithmetic and copies ran while one was open for 2% of the time, Pallas kernels for 42%

profile of v3, /device:TPU:0, one launch (start us, length us, event | category | flops | bytes accessed | tf_op | source)
XLA Modules:
  0.0 195.7 jit_solution(2682128545525444032)
XLA Ops:
  0.6 0.7 copy.9
  1.3 0.5 fusion.2
  1.8 0.8 select_reduce_fusion
  2.7 0.7 sub.24
  3.4 5.2 %all-to-all-start = ((s32[8,1,192]{2,1,0:T(1,128)}), s32[8,1,192]{2,1,0:T(1,128)S(1)}, u32[]{:S(2)}, u32[]{:S(2)}) async-start(s32[8,1,192]{2,1,0:T(1,128)} %sub.24), calls=%async_computation | async-start | bytes 16384 | tf_op jit(solution)/shard_map/all_to_all | solution.py:391
  8.5 0.7 fusion.9
  9.2 0.7 divide_bitcast_fusion
  10.0 0.9 convert_element_type.27.rest_4_
  10.9 2.3 %all-to-all-done = s32[8,1,192]{2,1,0:T(1,128)S(1)} async-done(((s32[8,1,192]{2,1,0:T(1,128)}), s32[8,1,192]{2,1,0:T(1,128)S(1)}, u32[]{:S(2)}, u32[]{:S(2)}) %all-to-all-start) | async-done | bytes 6176 | tf_op jit(solution)/shard_map/all_to_all | solution.py:391
  13.3 4.8 %shard_map.86 = (bf16[1536,128]{1,0:T(8,128)(2,1)}, s32[1536,128]{1,0:T(8,128)S(1)}, s32[1024,128]{1,0:T(8,128)}) custom-call(s32[1,1536]{1,0:T(1,128)S(1)} %broadcast_in_dim_reshape.3.row_ref, s32[1,1024]{1,0:T(1,128)S(1)} %fusion.6.place_ref, f32[3072,128]{1,0:T(8,128)} %base_ref.5), custom_call_target="tpu_custom_call" | custom-call | flops 1207959552 | bytes 4000000 | tf_op jit(solution)/shard_map/pallas_call | solution.py:88
  18.1 3.5 %all-to-all-start.1 = ((bf16[8,192,128]{2,1,0:T(8,128)(2,1)}), bf16[8,192,128]{2,1,0:T(8,128)(2,1)S(1)}, u32[]{:S(2)}, u32[]{:S(2)}) async-start(bf16[8,192,128]{2,1,0:T(8,128)(2,1)} %bitcast.60), calls=%async_computation.1 | async-start | bytes 786432 | tf_op jit(solution)/shard_map/all_to_all | solution.py:391
  21.6 3.7 %collective-permute-start.2 = (bf16[128,256]{1,0:T(8,128)(2,1)S(1)}, bf16[128,256]{1,0:T(8,128)(2,1)S(1)}, u32[]{:S(2)}, u32[]{:S(2)}) collective-permute-start(bf16[128,256]{1,0:T(8,128)(2,1)S(1)} %convert_element_type.27.rest_4_), channel_id=1, source_target_pairs={{0,3},{1,2},{2,1},{3,0},{4,7},{5,6},{6,5},{7,4},{8,11},{9,10},{10,... | collective-permute-start | bytes 196616 | tf_op jit(solution)/shard_map/ppermute | solution.py:423
  25.3 0.8 collective-permute-start
  26.1 6.1 %shard_map.87.part_ref = f32[4,1024,128]{2,1,0:T(8,128)} custom-call(f32[3072,128]{1,0:T(8,128)} %base_ref.5, bf16[4,1024,1024]{2,1,0:T(8,128)(2,1)} %matrix_ref.29), custom_call_target="tpu_custom_call" | custom-call | flops 805306368 | bytes 10000000 | tf_op jit(solution)/shard_map/pallas_call | solution.py:79
  32.2 4.1 %shard_map.88 = (bf16[1024,128]{1,0:T(8,128)(2,1)}, bf16[1536,128]{1,0:T(8,128)(2,1)}) custom-call(bf16[1536,128]{1,0:T(8,128)(2,1)S(1)} %bitcast.42, s32[1024,128]{1,0:T(8,128)} %get-tuple-element.53.placed_ref, s32[1,1024]{1,0:T(1,128)} %copy-done, bf16[4,1024,1024]{2,1,0:T(8,128)(2,1)} %matrix_ref.29, f32[4,1024,128]{2,1,0:T(8,128)} %shard_map.87.part_ref), custom_call_target="tpu_custom_call" | custom-call | flops 1207959552 | bytes 3000000 | tf_op jit(solution)/shard_map/pallas_call | solution.py:88
  36.3 4.1 %all-to-all-start.2 = ((bf16[8,192,128]{2,1,0:T(8,128)(2,1)}), bf16[8,192,128]{2,1,0:T(8,128)(2,1)S(1)}, u32[]{:S(2)}, u32[]{:S(2)}) async-start(bf16[8,192,128]{2,1,0:T(8,128)(2,1)} %bitcast.64), calls=%async_computation.2 | async-start | bytes 786432 | tf_op jit(solution)/shard_map/all_to_all | solution.py:391
  40.4 6.9 %shard_map.89 = (f32[3072,128]{1,0:T(8,128)}, f32[1536,128]{1,0:T(8,128)S(1)}) custom-call(f32[4,1024,128]{2,1,0:T(8,128)} %shard_map.87.part_ref, bf16[4,1024,1024]{2,1,0:T(8,128)(2,1)} %matrix_ref.29, bf16[1024,128]{1,0:T(8,128)(2,1)} %get-tuple-element.54.margin_ref, f32[3072,128]{1,0:T(8,128)} %base_ref.7, s32[1536,128]{1,0:T(8,128)S(1)} %get-tuple-element.55.column_ref), custom_call_target="tpu_custom_call" | custom-call | flops 2415919104 | bytes 8000000 | tf_op jit(solution)/shard_map/pallas_call | solution.py:79
  47.2 1.5 all-to-all-done.2
  48.7 2.2 %shard_map.91 = bf16[1536,128]{1,0:T(8,128)(2,1)} custom-call(f32[1536,128]{1,0:T(8,128)S(1)} %get-tuple-element.59.sent_ref, bf16[1536,128]{1,0:T(8,128)(2,1)S(1)} %bitcast.34, s32[1536,128]{1,0:T(8,128)S(1)} %get-tuple-element.55.column_ref, s32[1,1536]{1,0:T(1,128)S(1)} %broadcast_in_dim_reshape.3.row_ref), custom_call_target="tpu_custom_call" | custom-call | flops 603979776 | bytes 3000000 | tf_op jit(solution)/shard_map/pallas_call | solution.py:88
  50.9 3.6 %all-to-all-start.3 = ((bf16[8,192,128]{2,1,0:T(8,128)(2,1)}), bf16[8,192,128]{2,1,0:T(8,128)(2,1)S(1)}, u32[]{:S(2)}, u32[]{:S(2)}) async-start(bf16[8,192,128]{2,1,0:T(8,128)(2,1)} %bitcast.56), calls=%async_computation.3 | async-start | bytes 786432 | tf_op jit(solution)/shard_map/all_to_all | solution.py:391
  54.6 8.3 %shard_map.90 = (f32[4,1024,128]{2,1,0:T(8,128)}, f32[128,128]{1,0:T(8,128)}) custom-call(f32[3072,128]{1,0:T(8,128)} %get-tuple-element.56.base_ref, bf16[1536,128]{1,0:T(8,128)(2,1)S(1)} %bitcast.35, s32[1,1536]{1,0:T(1,128)S(1)} %broadcast_in_dim_reshape.3.row_ref, bf16[4,1024,1024]{2,1,0:T(8,128)(2,1)} %matrix_ref.26, bf16[4,32,1024]{2,1,0:T(8,128)(2,1)} %bitcast.48), custom_call_target="tpu_custom_call" | custom-call | flops 2013265920 | bytes 14000000 | tf_op jit(solution)/shard_map/pallas_call | solution.py:79
  62.9 2.9 %shard_map.92 = (bf16[1024,128]{1,0:T(8,128)(2,1)}, bf16[128,128]{1,0:T(8,128)(2,1)}) custom-call(bf16[1536,128]{1,0:T(8,128)(2,1)S(1)} %bitcast.45, s32[1024,128]{1,0:T(8,128)} %get-tuple-element.53.placed_ref, bf16[4,32,1024]{2,1,0:T(8,128)(2,1)} %bitcast.49, f32[128,128]{1,0:T(8,128)} %get-tuple-element.60.proj_ref), custom_call_target="tpu_custom_call" | custom-call | flops 603979776 | bytes 2000000 | tf_op jit(solution)/shard_map/pallas_call | solution.py:88
  65.8 0.3 collective-permute-start.3
  66.0 0.8 constant_dynamic-update-slice_fusion.1
  66.8 0.4 collective-permute-done.3
  67.3 2.7 %collective-permute-start.6 = (bf16[256,128]{1,0:T(8,128)(2,1)S(1)}, bf16[256,128]{1,0:T(8,128)(2,1)S(1)}, u32[]{:S(2)}, u32[]{:S(2)}) collective-permute-start(bf16[256,128]{1,0:T(8,128)(2,1)S(1)} %constant_dynamic-update-slice_fusion.rest_0_), channel_id=1, source_target_pairs={{0,24},{4,28},{8,16},{12,20},{16,8},{20,12},{24,0},{28,4},{1,25},{... | collective-permute-start | bytes 196616 | tf_op jit(solution)/shard_map/ppermute | solution.py:522
  69.9 0.5 collective-permute-start.5
  70.5 0.3 collective-permute-start.4
  70.7 4.2 %shard_map.93 = (f32[1536,128]{1,0:T(8,128)}, bf16[1536,128]{1,0:T(8,128)(2,1)}) custom-call(bf16[1024,128]{1,0:T(8,128)(2,1)} %get-tuple-element.61.margin_ref, s32[1,1024]{1,0:T(1,128)} %copy-done, bf16[4,1024,1024]{2,1,0:T(8,128)(2,1)} %matrix_ref.26, f32[4,1024,128]{2,1,0:T(8,128)} %get-tuple-element.58.part_ref, bf16[4,32,1024]{2,1,0:T(8,128)(2,1)} %bitcast.50), custom_call_target="tpu_custom_call" | custom-call | flops 1207959552 | bytes 3000000 | tf_op jit(solution)/shard_map/pallas_call | solution.py:88
  75.0 3.1 %shard_map.94 = (f32[128,128]{1,0:T(8,128)}, bf16[1536,128]{1,0:T(8,128)(2,1)}) custom-call(s32[2]{0:T(128)S(1)} %pad_add_fusion.here_ref, bf16[256,128]{1,0:T(8,128)(2,1)S(1)} %constant_dynamic-update-slice_fusion.rest_0_, bf16[256,128]{1,0:T(8,128)(2,1)S(1)} %collective-permute-done.4.rest_1_, bf16[256,128]{1,0:T(8,128)(2,1)S(1)} %collective-permute-done.5.rest_2_, ...), custom_call_target="tpu_custom_call" | custom-call | flops 301989888 | bytes 3000000 | tf_op jit(solution)/shard_map/pallas_call | solution.py:88
  78.2 4.0 %all-to-all-start.4 = ((bf16[8,192,128]{2,1,0:T(8,128)(2,1)}), bf16[8,192,128]{2,1,0:T(8,128)(2,1)S(1)}, u32[]{:S(2)}, u32[]{:S(2)}) async-start(bf16[8,192,128]{2,1,0:T(8,128)(2,1)} %bitcast.62), calls=%async_computation.4 | async-start | bytes 786432 | tf_op jit(solution)/shard_map/all_to_all | solution.py:391
  82.1 7.2 %shard_map.95 = (f32[3072,128]{1,0:T(8,128)}, f32[1536,128]{1,0:T(8,128)S(1)}) custom-call(f32[4,1024,128]{2,1,0:T(8,128)} %get-tuple-element.58.part_ref, bf16[4,1024,1024]{2,1,0:T(8,128)(2,1)} %matrix_ref.26, bf16[1024,128]{1,0:T(8,128)(2,1)} %get-tuple-element.61.margin_ref, f32[3072,128]{1,0:T(8,128)} %base_ref.5, ...), custom_call_target="tpu_custom_call" | custom-call | flops 2415919104 | bytes 8000000 | tf_op jit(solution)/shard_map/pallas_call | solution.py:79
  89.3 1.1 all-to-all-done.4
  90.5 2.1 %shard_map.97 = bf16[1536,128]{1,0:T(8,128)(2,1)} custom-call(f32[1536,128]{1,0:T(8,128)S(1)} %get-tuple-element.73.sent_ref, bf16[1536,128]{1,0:T(8,128)(2,1)S(1)} %bitcast.40, s32[1536,128]{1,0:T(8,128)S(1)} %get-tuple-element.55.column_ref, s32[1,1536]{1,0:T(1,128)S(1)} %broadcast_in_dim_reshape.3.row_ref), custom_call_target="tpu_custom_call" | custom-call | flops 603979776 | bytes 3000000 | tf_op jit(solution)/shard_map/pallas_call | solution.py:88
  92.6 3.5 %all-to-all-start.5 = ((bf16[8,192,128]{2,1,0:T(8,128)(2,1)}), bf16[8,192,128]{2,1,0:T(8,128)(2,1)S(1)}, u32[]{:S(2)}, u32[]{:S(2)}) async-start(bf16[8,192,128]{2,1,0:T(8,128)(2,1)} %bitcast.57), calls=%async_computation.5 | async-start | bytes 786432 | tf_op jit(solution)/shard_map/all_to_all | solution.py:391
  96.0 7.8 %shard_map.96 = (f32[3072,128]{1,0:T(8,128)}, f32[4,1024,128]{2,1,0:T(8,128)}) custom-call(f32[3072,128]{1,0:T(8,128)} %get-tuple-element.70.base_ref, bf16[1536,128]{1,0:T(8,128)(2,1)S(1)} %bitcast.41, s32[1,1536]{1,0:T(1,128)S(1)} %broadcast_in_dim_reshape.3.row_ref, bf16[4,1024,1024]{2,1,0:T(8,128)(2,1)} %matrix_ref.29), custom_call_target="tpu_custom_call" | custom-call | flops 2013265920 | bytes 14000000 | tf_op jit(solution)/shard_map/pallas_call | solution.py:79
  103.9 0.4 all-to-all-done.5
  104.3 4.0 %shard_map.98 = (bf16[1024,128]{1,0:T(8,128)(2,1)}, bf16[1536,128]{1,0:T(8,128)(2,1)}) custom-call(bf16[1536,128]{1,0:T(8,128)(2,1)S(1)} %bitcast.44, s32[1024,128]{1,0:T(8,128)} %get-tuple-element.53.placed_ref, s32[1,1024]{1,0:T(1,128)} %copy-done, bf16[4,1024,1024]{2,1,0:T(8,128)(2,1)} %matrix_ref.29, f32[4,1024,128]{2,1,0:T(8,128)} %get-tuple-element.72.part_ref), custom_call_target="tpu_custom_call" | custom-call | flops 1207959552 | bytes 3000000 | tf_op jit(solution)/shard_map/pallas_call | solution.py:88
  108.3 3.7 %all-to-all-start.6 = ((bf16[8,192,128]{2,1,0:T(8,128)(2,1)}), bf16[8,192,128]{2,1,0:T(8,128)(2,1)S(1)}, u32[]{:S(2)}, u32[]{:S(2)}) async-start(bf16[8,192,128]{2,1,0:T(8,128)(2,1)} %bitcast.65), calls=%async_computation.6 | async-start | bytes 786432 | tf_op jit(solution)/shard_map/all_to_all | solution.py:391
  112.1 6.9 %shard_map.99 = (f32[3072,128]{1,0:T(8,128)}, f32[1536,128]{1,0:T(8,128)S(1)}) custom-call(f32[4,1024,128]{2,1,0:T(8,128)} %get-tuple-element.72.part_ref, bf16[4,1024,1024]{2,1,0:T(8,128)(2,1)} %matrix_ref.29, bf16[1024,128]{1,0:T(8,128)(2,1)} %get-tuple-element.74.margin_ref, f32[3072,128]{1,0:T(8,128)} %base_ref.7, ...), custom_call_target="tpu_custom_call" | custom-call | flops 2415919104 | bytes 8000000 | tf_op jit(solution)/shard_map/pallas_call | solution.py:79
  118.9 1.5 all-to-all-done.6
  120.4 2.2 %shard_map.101 = bf16[1536,128]{1,0:T(8,128)(2,1)} custom-call(f32[1536,128]{1,0:T(8,128)S(1)} %get-tuple-element.78.sent_ref, bf16[1536,128]{1,0:T(8,128)(2,1)S(1)} %bitcast.36, s32[1536,128]{1,0:T(8,128)S(1)} %get-tuple-element.55.column_ref, s32[1,1536]{1,0:T(1,128)S(1)} %broadcast_in_dim_reshape.3.row_ref), custom_call_target="tpu_custom_call" | custom-call | flops 603979776 | bytes 3000000 | tf_op jit(solution)/shard_map/pallas_call | solution.py:88
  122.6 3.7 %all-to-all-start.7 = ((bf16[8,192,128]{2,1,0:T(8,128)(2,1)}), bf16[8,192,128]{2,1,0:T(8,128)(2,1)S(1)}, u32[]{:S(2)}, u32[]{:S(2)}) async-start(bf16[8,192,128]{2,1,0:T(8,128)(2,1)} %bitcast.58), calls=%async_computation.7 | async-start | bytes 786432 | tf_op jit(solution)/shard_map/all_to_all | solution.py:391
  126.3 8.3 %shard_map.100 = (f32[4,1024,128]{2,1,0:T(8,128)}, f32[128,128]{1,0:T(8,128)}) custom-call(f32[3072,128]{1,0:T(8,128)} %get-tuple-element.75.base_ref, bf16[1536,128]{1,0:T(8,128)(2,1)S(1)} %bitcast.37, s32[1,1536]{1,0:T(1,128)S(1)} %broadcast_in_dim_reshape.3.row_ref, bf16[4,1024,1024]{2,1,0:T(8,128)(2,1)} %matrix_ref.26, bf16[4,32,1024]{2,1,0:T(8,128)(2,1)} %bitcast.52), custom_call_target="tpu_custom_call" | custom-call | flops 2013265920 | bytes 14000000 | tf_op jit(solution)/shard_map/pallas_call | solution.py:79
  134.6 2.9 %shard_map.102 = (bf16[1024,128]{1,0:T(8,128)(2,1)}, bf16[128,128]{1,0:T(8,128)(2,1)}) custom-call(bf16[1536,128]{1,0:T(8,128)(2,1)S(1)} %bitcast.47, s32[1024,128]{1,0:T(8,128)} %get-tuple-element.53.placed_ref, bf16[4,32,1024]{2,1,0:T(8,128)(2,1)} %bitcast.53, f32[128,128]{1,0:T(8,128)} %get-tuple-element.79.proj_ref), custom_call_target="tpu_custom_call" | custom-call | flops 603979776 | bytes 2000000 | tf_op jit(solution)/shard_map/pallas_call | solution.py:88
  137.7 0.8 constant_dynamic-update-slice_fusion.3
  138.4 0.5 collective-permute-done.7
  138.9 2.6 %collective-permute-start.10 = (bf16[256,128]{1,0:T(8,128)(2,1)S(1)}, bf16[256,128]{1,0:T(8,128)(2,1)S(1)}, u32[]{:S(2)}, u32[]{:S(2)}) collective-permute-start(bf16[256,128]{1,0:T(8,128)(2,1)S(1)} %constant_dynamic-update-slice_fusion.2.rest_0_), channel_id=1, source_target_pairs={{0,24},{4,28},{8,16},{12,20},{16,8},{20,12},{24,0},{28,4},{1,25},{... | collective-permute-start | bytes 196616 | tf_op jit(solution)/shard_map/ppermute | solution.py:522
  141.5 0.5 collective-permute-start.9
  142.1 0.3 collective-permute-start.8
  142.4 4.2 %shard_map.103 = (f32[1536,128]{1,0:T(8,128)}, bf16[1536,128]{1,0:T(8,128)(2,1)}) custom-call(bf16[1024,128]{1,0:T(8,128)(2,1)} %get-tuple-element.80.margin_ref, s32[1,1024]{1,0:T(1,128)} %copy-done, bf16[4,1024,1024]{2,1,0:T(8,128)(2,1)} %matrix_ref.26, f32[4,1024,128]{2,1,0:T(8,128)} %get-tuple-element.77.part_ref, bf16[4,32,1024]{2,1,0:T(8,128)(2,1)} %bitcast.54), custom_call_target="tpu_custom_call" | custom-call | flops 1207959552 | bytes 3000000 | tf_op jit(solution)/shard_map/pallas_call | solution.py:88
  146.7 3.1 %shard_map.104 = (f32[128,128]{1,0:T(8,128)}, bf16[1536,128]{1,0:T(8,128)(2,1)}) custom-call(s32[2]{0:T(128)S(1)} %pad_add_fusion.here_ref, bf16[256,128]{1,0:T(8,128)(2,1)S(1)} %constant_dynamic-update-slice_fusion.2.rest_0_, bf16[256,128]{1,0:T(8,128)(2,1)S(1)} %collective-permute-done.8.rest_1_, bf16[256,128]{1,0:T(8,128)(2,1)S(1)} %collective-permute-done.9.rest_2_, ...), custom_call_target="tpu_custom_call" | custom-call | flops 301989888 | bytes 3000000 | tf_op jit(solution)/shard_map/pallas_call | solution.py:88
  149.8 3.9 %all-to-all-start.8 = ((bf16[8,192,128]{2,1,0:T(8,128)(2,1)}), bf16[8,192,128]{2,1,0:T(8,128)(2,1)S(1)}, u32[]{:S(2)}, u32[]{:S(2)}) async-start(bf16[8,192,128]{2,1,0:T(8,128)(2,1)} %bitcast.61), calls=%async_computation.8 | async-start | bytes 786432 | tf_op jit(solution)/shard_map/all_to_all | solution.py:391
  153.7 7.2 %shard_map.105 = (f32[3072,128]{1,0:T(8,128)}, f32[1536,128]{1,0:T(8,128)S(1)}) custom-call(f32[4,1024,128]{2,1,0:T(8,128)} %get-tuple-element.77.part_ref, bf16[4,1024,1024]{2,1,0:T(8,128)(2,1)} %matrix_ref.26, bf16[1024,128]{1,0:T(8,128)(2,1)} %get-tuple-element.80.margin_ref, f32[3072,128]{1,0:T(8,128)} %get-tuple-element.81.base_ref, ...), custom_call_target="tpu_custom_call" | custom-call | flops 2415919104 | bytes 8000000 | tf_op jit(solution)/shard_map/pallas_call | solution.py:79
  160.9 1.2 all-to-all-done.8
  162.1 2.1 %shard_map.107 = bf16[1536,128]{1,0:T(8,128)(2,1)} custom-call(f32[1536,128]{1,0:T(8,128)S(1)} %get-tuple-element.90.sent_ref, bf16[1536,128]{1,0:T(8,128)(2,1)S(1)} %bitcast.38, s32[1536,128]{1,0:T(8,128)S(1)} %get-tuple-element.55.column_ref, s32[1,1536]{1,0:T(1,128)S(1)} %broadcast_in_dim_reshape.3.row_ref), custom_call_target="tpu_custom_call" | custom-call | flops 603979776 | bytes 3000000 | tf_op jit(solution)/shard_map/pallas_call | solution.py:88
  164.2 3.5 %all-to-all-start.9 = ((bf16[8,192,128]{2,1,0:T(8,128)(2,1)}), bf16[8,192,128]{2,1,0:T(8,128)(2,1)S(1)}, u32[]{:S(2)}, u32[]{:S(2)}) async-start(bf16[8,192,128]{2,1,0:T(8,128)(2,1)} %bitcast.59), calls=%async_computation.9 | async-start | bytes 786432 | tf_op jit(solution)/shard_map/all_to_all | solution.py:391
  167.6 7.8 %shard_map.106 = (f32[3072,128]{1,0:T(8,128)}, f32[4,1024,128]{2,1,0:T(8,128)}) custom-call(f32[3072,128]{1,0:T(8,128)} %get-tuple-element.86.base_ref, bf16[1536,128]{1,0:T(8,128)(2,1)S(1)} %bitcast.39, s32[1,1536]{1,0:T(1,128)S(1)} %broadcast_in_dim_reshape.3.row_ref, bf16[4,1024,1024]{2,1,0:T(8,128)(2,1)} %matrix_ref.29), custom_call_target="tpu_custom_call" | custom-call | flops 2013265920 | bytes 14000000 | tf_op jit(solution)/shard_map/pallas_call | solution.py:79
  175.5 0.4 all-to-all-done.9
  175.9 4.0 %shard_map.108 = (bf16[1024,128]{1,0:T(8,128)(2,1)}, bf16[1536,128]{1,0:T(8,128)(2,1)}) custom-call(bf16[1536,128]{1,0:T(8,128)(2,1)S(1)} %bitcast.43, s32[1024,128]{1,0:T(8,128)} %get-tuple-element.53.placed_ref, s32[1,1024]{1,0:T(1,128)} %copy-done, bf16[4,1024,1024]{2,1,0:T(8,128)(2,1)} %matrix_ref.29, f32[4,1024,128]{2,1,0:T(8,128)} %get-tuple-element.89.part_ref), custom_call_target="tpu_custom_call" | custom-call | flops 1207959552 | bytes 3000000 | tf_op jit(solution)/shard_map/pallas_call | solution.py:88
  179.9 3.7 %all-to-all-start.10 = ((bf16[8,192,128]{2,1,0:T(8,128)(2,1)}), bf16[8,192,128]{2,1,0:T(8,128)(2,1)S(1)}, u32[]{:S(2)}, u32[]{:S(2)}) async-start(bf16[8,192,128]{2,1,0:T(8,128)(2,1)} %bitcast.63), calls=%async_computation.10 | async-start | bytes 786432 | tf_op jit(solution)/shard_map/all_to_all | solution.py:391
  183.7 6.8 %shard_map.109 = (f32[3072,128]{1,0:T(8,128)S(1)}, f32[1536,128]{1,0:T(8,128)}) custom-call(f32[4,1024,128]{2,1,0:T(8,128)} %get-tuple-element.89.part_ref, bf16[4,1024,1024]{2,1,0:T(8,128)(2,1)} %matrix_ref.29, bf16[1024,128]{1,0:T(8,128)(2,1)} %get-tuple-element.91.margin_ref, f32[3072,128]{1,0:T(8,128)} %base_ref.7, ...), custom_call_target="tpu_custom_call" | custom-call | flops 2415919104 | bytes 8000000 | tf_op jit(solution)/shard_map/pallas_call | solution.py:79
  190.5 1.5 all-to-all-done.10
  192.0 3.5 %shard_map.110 = f32[3072,128]{1,0:T(8,128)} custom-call(f32[3072,128]{1,0:T(8,128)S(1)} %get-tuple-element.92.base_ref, bf16[1536,128]{1,0:T(8,128)(2,1)S(1)} %bitcast.46, s32[1,1536]{1,0:T(1,128)S(1)} %broadcast_in_dim_reshape.3.row_ref), custom_call_target="tpu_custom_call" | custom-call | flops 1207959552 | bytes 4000000 | tf_op jit(solution)/shard_map/pallas_call | solution.py:88
  (36 shorter events, 0.6 us)
Async XLA Ops:
  3.4 9.9 %all-to-all-start = ((s32[8,1,192]{2,1,0:T(1,128)}), s32[8,1,192]{2,1,0:T(1,128)S(1)}, u32[]{:S(2)}, u32[]{:S(2)}) async-start(s32[8,1,192]{2,1,0:T(1,128)} %sub.24), calls=%async_computation | async-start | bytes 16384 | tf_op jit(solution)/shard_map/all_to_all | solution.py:391
  10.0 8.1 %copy-start = (s32[1,1024]{1,0:T(1,128)}, s32[1,1024]{1,0:T(1,128)S(1)}, u32[]{:S(2)}) copy-start(s32[1,1024]{1,0:T(1,128)S(1)} %fusion.6.place_ref) | copy-start | bytes 12292
  10.9 14.4 %copy-start.1 = (bf16[128,256]{1,0:T(8,128)(2,1)}, bf16[128,256]{1,0:T(8,128)(2,1)S(1)}, u32[]{:S(2)}) copy-start(bf16[128,256]{1,0:T(8,128)(2,1)S(1)} %convert_element_type.27.rest_4_) | copy-start | bytes 196612
  18.1 14.1 %all-to-all-start.1 = ((bf16[8,192,128]{2,1,0:T(8,128)(2,1)}), bf16[8,192,128]{2,1,0:T(8,128)(2,1)S(1)}, u32[]{:S(2)}, u32[]{:S(2)}) async-start(bf16[8,192,128]{2,1,0:T(8,128)(2,1)} %bitcast.60), calls=%async_computation.1 | async-start | bytes 786432 | tf_op jit(solution)/shard_map/all_to_all | solution.py:391
  21.6 10.6 %collective-permute-start.2 = (bf16[128,256]{1,0:T(8,128)(2,1)S(1)}, bf16[128,256]{1,0:T(8,128)(2,1)S(1)}, u32[]{:S(2)}, u32[]{:S(2)}) collective-permute-start(bf16[128,256]{1,0:T(8,128)(2,1)S(1)} %convert_element_type.27.rest_4_), channel_id=1, source_target_pairs={{0,3},{1,2},{2,1},{3,0},{4,7},{5,6},{6,5},{7,4},{8,11},{9,10},{10,... | collective-permute-start | bytes 196616 | tf_op jit(solution)/shard_map/ppermute | solution.py:423
  25.3 6.9 %collective-permute-start.1 = (bf16[128,256]{1,0:T(8,128)(2,1)S(1)}, bf16[128,256]{1,0:T(8,128)(2,1)S(1)}, u32[]{:S(2)}, u32[]{:S(2)}) collective-permute-start(bf16[128,256]{1,0:T(8,128)(2,1)S(1)} %convert_element_type.27.rest_4_), channel_id=1, source_target_pairs={{0,2},{1,3},{2,0},{3,1},{4,6},{5,7},{6,4},{7,5},{8,10},{9,11},{10,... | collective-permute-start | bytes 196616 | tf_op jit(solution)/shard_map/ppermute | solution.py:423
  25.3 6.9 %collective-permute-start = (bf16[128,256]{1,0:T(8,128)(2,1)S(1)}, bf16[128,256]{1,0:T(8,128)(2,1)S(1)}, u32[]{:S(2)}, u32[]{:S(2)}) collective-permute-start(bf16[128,256]{1,0:T(8,128)(2,1)S(1)} %convert_element_type.27.rest_4_), channel_id=1, source_target_pairs={{0,1},{1,0},{2,3},{3,2},{4,5},{5,4},{6,7},{7,6},{8,9},{9,8},{10,11... | collective-permute-start | bytes 196616 | tf_op jit(solution)/shard_map/ppermute | solution.py:423
  32.2 4.1 %copy-start.2 = (bf16[128,256]{1,0:T(8,128)(2,1)}, bf16[128,256]{1,0:T(8,128)(2,1)S(1)}, u32[]{:S(2)}) copy-start(bf16[128,256]{1,0:T(8,128)(2,1)S(1)} %collective-permute-done.2.rest_7_) | copy-start | bytes 196612
  32.2 4.1 %copy-start.3 = (bf16[128,256]{1,0:T(8,128)(2,1)}, bf16[128,256]{1,0:T(8,128)(2,1)S(1)}, u32[]{:S(2)}) copy-start(bf16[128,256]{1,0:T(8,128)(2,1)S(1)} %collective-permute-done.1.rest_6_) | copy-start | bytes 196612
  32.2 4.1 %copy-start.4 = (bf16[128,256]{1,0:T(8,128)(2,1)}, bf16[128,256]{1,0:T(8,128)(2,1)S(1)}, u32[]{:S(2)}) copy-start(bf16[128,256]{1,0:T(8,128)(2,1)S(1)} %collective-permute-done.rest_5_) | copy-start | bytes 196612
  36.3 12.4 %all-to-all-start.2 = ((bf16[8,192,128]{2,1,0:T(8,128)(2,1)}), bf16[8,192,128]{2,1,0:T(8,128)(2,1)S(1)}, u32[]{:S(2)}, u32[]{:S(2)}) async-start(bf16[8,192,128]{2,1,0:T(8,128)(2,1)} %bitcast.64), calls=%async_computation.2 | async-start | bytes 786432 | tf_op jit(solution)/shard_map/all_to_all | solution.py:391
  50.9 12.0 %all-to-all-start.3 = ((bf16[8,192,128]{2,1,0:T(8,128)(2,1)}), bf16[8,192,128]{2,1,0:T(8,128)(2,1)S(1)}, u32[]{:S(2)}, u32[]{:S(2)}) async-start(bf16[8,192,128]{2,1,0:T(8,128)(2,1)} %bitcast.56), calls=%async_computation.3 | async-start | bytes 786432 | tf_op jit(solution)/shard_map/all_to_all | solution.py:391
  65.8 1.5 collective-permute-start.3
  67.3 7.7 %collective-permute-start.6 = (bf16[256,128]{1,0:T(8,128)(2,1)S(1)}, bf16[256,128]{1,0:T(8,128)(2,1)S(1)}, u32[]{:S(2)}, u32[]{:S(2)}) collective-permute-start(bf16[256,128]{1,0:T(8,128)(2,1)S(1)} %constant_dynamic-update-slice_fusion.rest_0_), channel_id=1, source_target_pairs={{0,24},{4,28},{8,16},{12,20},{16,8},{20,12},{24,0},{28,4},{1,25},{... | collective-permute-start | bytes 196616 | tf_op jit(solution)/shard_map/ppermute | solution.py:522
  69.9 5.1 %collective-permute-start.5 = (bf16[256,128]{1,0:T(8,128)(2,1)S(1)}, bf16[256,128]{1,0:T(8,128)(2,1)S(1)}, u32[]{:S(2)}, u32[]{:S(2)}) collective-permute-start(bf16[256,128]{1,0:T(8,128)(2,1)S(1)} %constant_dynamic-update-slice_fusion.rest_0_), channel_id=1, source_target_pairs={{0,16},{4,20},{8,24},{12,28},{16,0},{20,4},{24,8},{28,12},{1,17},{... | collective-permute-start | bytes 196616 | tf_op jit(solution)/shard_map/ppermute | solution.py:522
  70.5 4.6 %collective-permute-start.4 = (bf16[256,128]{1,0:T(8,128)(2,1)S(1)}, bf16[256,128]{1,0:T(8,128)(2,1)S(1)}, u32[]{:S(2)}, u32[]{:S(2)}) collective-permute-start(bf16[256,128]{1,0:T(8,128)(2,1)S(1)} %constant_dynamic-update-slice_fusion.rest_0_), channel_id=1, source_target_pairs={{0,8},{4,12},{8,0},{12,4},{16,24},{20,28},{24,16},{28,20},{1,9},{5... | collective-permute-start | bytes 196616 | tf_op jit(solution)/shard_map/ppermute | solution.py:522
  78.2 12.3 %all-to-all-start.4 = ((bf16[8,192,128]{2,1,0:T(8,128)(2,1)}), bf16[8,192,128]{2,1,0:T(8,128)(2,1)S(1)}, u32[]{:S(2)}, u32[]{:S(2)}) async-start(bf16[8,192,128]{2,1,0:T(8,128)(2,1)} %bitcast.62), calls=%async_computation.4 | async-start | bytes 786432 | tf_op jit(solution)/shard_map/all_to_all | solution.py:391
  92.6 11.7 %all-to-all-start.5 = ((bf16[8,192,128]{2,1,0:T(8,128)(2,1)}), bf16[8,192,128]{2,1,0:T(8,128)(2,1)S(1)}, u32[]{:S(2)}, u32[]{:S(2)}) async-start(bf16[8,192,128]{2,1,0:T(8,128)(2,1)} %bitcast.57), calls=%async_computation.5 | async-start | bytes 786432 | tf_op jit(solution)/shard_map/all_to_all | solution.py:391
  108.3 12.0 %all-to-all-start.6 = ((bf16[8,192,128]{2,1,0:T(8,128)(2,1)}), bf16[8,192,128]{2,1,0:T(8,128)(2,1)S(1)}, u32[]{:S(2)}, u32[]{:S(2)}) async-start(bf16[8,192,128]{2,1,0:T(8,128)(2,1)} %bitcast.65), calls=%async_computation.6 | async-start | bytes 786432 | tf_op jit(solution)/shard_map/all_to_all | solution.py:391
  122.6 12.0 %all-to-all-start.7 = ((bf16[8,192,128]{2,1,0:T(8,128)(2,1)}), bf16[8,192,128]{2,1,0:T(8,128)(2,1)S(1)}, u32[]{:S(2)}, u32[]{:S(2)}) async-start(bf16[8,192,128]{2,1,0:T(8,128)(2,1)} %bitcast.58), calls=%async_computation.7 | async-start | bytes 786432 | tf_op jit(solution)/shard_map/all_to_all | solution.py:391
  137.4 1.5 collective-permute-start.7
  138.9 7.7 %collective-permute-start.10 = (bf16[256,128]{1,0:T(8,128)(2,1)S(1)}, bf16[256,128]{1,0:T(8,128)(2,1)S(1)}, u32[]{:S(2)}, u32[]{:S(2)}) collective-permute-start(bf16[256,128]{1,0:T(8,128)(2,1)S(1)} %constant_dynamic-update-slice_fusion.2.rest_0_), channel_id=1, source_target_pairs={{0,24},{4,28},{8,16},{12,20},{16,8},{20,12},{24,0},{28,4},{1,25},{... | collective-permute-start | bytes 196616 | tf_op jit(solution)/shard_map/ppermute | solution.py:522
  141.5 5.1 %collective-permute-start.9 = (bf16[256,128]{1,0:T(8,128)(2,1)S(1)}, bf16[256,128]{1,0:T(8,128)(2,1)S(1)}, u32[]{:S(2)}, u32[]{:S(2)}) collective-permute-start(bf16[256,128]{1,0:T(8,128)(2,1)S(1)} %constant_dynamic-update-slice_fusion.2.rest_0_), channel_id=1, source_target_pairs={{0,16},{4,20},{8,24},{12,28},{16,0},{20,4},{24,8},{28,12},{1,17},{... | collective-permute-start | bytes 196616 | tf_op jit(solution)/shard_map/ppermute | solution.py:522
  142.1 4.6 %collective-permute-start.8 = (bf16[256,128]{1,0:T(8,128)(2,1)S(1)}, bf16[256,128]{1,0:T(8,128)(2,1)S(1)}, u32[]{:S(2)}, u32[]{:S(2)}) collective-permute-start(bf16[256,128]{1,0:T(8,128)(2,1)S(1)} %constant_dynamic-update-slice_fusion.2.rest_0_), channel_id=1, source_target_pairs={{0,8},{4,12},{8,0},{12,4},{16,24},{20,28},{24,16},{28,20},{1,9},{5... | collective-permute-start | bytes 196616 | tf_op jit(solution)/shard_map/ppermute | solution.py:522
  149.8 12.2 %all-to-all-start.8 = ((bf16[8,192,128]{2,1,0:T(8,128)(2,1)}), bf16[8,192,128]{2,1,0:T(8,128)(2,1)S(1)}, u32[]{:S(2)}, u32[]{:S(2)}) async-start(bf16[8,192,128]{2,1,0:T(8,128)(2,1)} %bitcast.61), calls=%async_computation.8 | async-start | bytes 786432 | tf_op jit(solution)/shard_map/all_to_all | solution.py:391
  164.2 11.7 %all-to-all-start.9 = ((bf16[8,192,128]{2,1,0:T(8,128)(2,1)}), bf16[8,192,128]{2,1,0:T(8,128)(2,1)S(1)}, u32[]{:S(2)}, u32[]{:S(2)}) async-start(bf16[8,192,128]{2,1,0:T(8,128)(2,1)} %bitcast.59), calls=%async_computation.9 | async-start | bytes 786432 | tf_op jit(solution)/shard_map/all_to_all | solution.py:391
  179.9 12.0 %all-to-all-start.10 = ((bf16[8,192,128]{2,1,0:T(8,128)(2,1)}), bf16[8,192,128]{2,1,0:T(8,128)(2,1)S(1)}, u32[]{:S(2)}, u32[]{:S(2)}) async-start(bf16[8,192,128]{2,1,0:T(8,128)(2,1)} %bitcast.63), calls=%async_computation.10 | async-start | bytes 786432 | tf_op jit(solution)/shard_map/all_to_all | solution.py:391

commit v4 on v3

--- a/solution.py
+++ b/solution.py
@@ -254,7 +254,7 @@
 
 def ready_body(
     margin_ref, place_ref, matrix_ref, part_ref, modes_ref, solved_ref, lift_ref,
-    margin, place, matrix, part, modes, outer, solved, lift, sems,
+    margin, place, matrix, part, modes, outer, sems,
 ):
     subs, count, margins = modes.shape
     core = matrix_ref.shape[1] - margins
@@ -271,7 +271,7 @@
             ],
         )
     )
-    width = lift.shape[1]
+    width = lift_ref.shape[1]
     rows = lax.broadcasted_iota(i32, (count, width), 0)
     lanes = lax.broadcasted_iota(i32, (count, width), 1)
     for s in range(subs):
@@ -279,48 +279,39 @@
         outer[at, : 2 * cols] = split(damping * (part[s] + dot(matrix[s], margin[at, :])))
         own = (rows + s * count == lanes).astype(f32).astype(bf16)
         outer[at, 2 * cols :] = turned_dot(modes[s], own).astype(bf16)
-    stores = []
-    size = solved.shape[0] // 2
+    size = solved_ref.shape[0] // 2
     for k in range(2):
         at = pl.ds(k * size, size)
         packed = dot(hot_cols(place[...], k * size, size), outer[...])
-        solved[at, :] = both(packed[:, : 2 * cols])
-        lift[at, :] = packed[:, 2 * cols :].astype(bf16)
-        stores += begin(
-            sems, 5 + 2 * k, [(solved.at[at], solved_ref.at[at]), (lift.at[at], lift_ref.at[at])]
-        )
-    finish(stores)
+        solved_ref[at, :] = both(packed[:, : 2 * cols])
+        lift_ref[at, :] = packed[:, 2 * cols :].astype(bf16)
 
 
 def coarse_body(side, pair_count, here_ref, *rest):
     pairs, rest = rest[:pair_count], rest[pair_count:]
     inverse_refs = rest[:side]
     solved_ref, lift_ref, coarse_ref, out_ref = rest[side : side + 4]
-    inverse, everyone, solved, lift, made, packed, sems = rest[side + 4 :]
-    loads = begin(
-        sems, 0,
-        [(inverse_refs[k], inverse.at[k]) for k in range(side)] + [(lift_ref, lift), (solved_ref, solved)],
-    )
+    inverse, everyone, made, packed, sems = rest[side + 4 :]
+    loads = begin(sems, 0, [(inverse_refs[k], inverse.at[k]) for k in range(side)])
     height = made.shape[0]
     for k, pair_ref in enumerate(pairs):
         for j in range(2):
             at = pl.multiple_of((here_ref[1] ^ (2 * k + j)) * height, height)
             everyone[pl.ds(at, height), :] = pair_ref[j * height : (j + 1) * height, :]
-    finish(loads[:side])
+    finish(loads)
     value = 0.0
     for k in range(side):
         width = inverse.shape[2]
         at = pl.multiple_of((here_ref[0] ^ k) * width, width)
         value += dot(inverse[k], everyone[pl.ds(at, width), :])
     made[...] = value
-    stores = begin(sems, side + 2, [(made, coarse_ref)])
+    stores = begin(sems, side, [(made, coarse_ref)])
     halves = split(value)
-    finish(loads[side:])
     size = packed.shape[0] // 2
     for k in range(2):
         at = pl.ds(k * size, size)
-        packed[at, :] = (solved[at, :] + both(dot(lift[at, :], halves))).astype(bf16)
-        stores += begin(sems, side + 3 + k, [(packed.at[at], out_ref.at[at])])
+        packed[at, :] = (solved_ref[at, :] + both(dot(lift_ref[at, :], halves))).astype(bf16)
+        stores += begin(sems, side + 1 + k, [(packed.at[at], out_ref.at[at])])
     finish(stores)
 
 
@@ -523,23 +514,20 @@
         ]
         solved, lift = flat_call(
             ready_body, (),
-            [jax.ShapeDtypeStruct((slots, cols), f32), jax.ShapeDtypeStruct((slots, coarse_rows), bf16)], (),
+            [jax.ShapeDtypeStruct((slots, cols), f32), jax.ShapeDtypeStruct((slots, coarse_rows), bf16)], (0, 1),
             [margin_scratch, pltpu.VMEM((1, many), i32)] + corner_scratch
-            + [
-                modes_scratch, pltpu.VMEM((many, 2 * cols + coarse_rows), bf16), pltpu.VMEM((slots, cols), f32),
-                pltpu.VMEM((slots, coarse_rows), bf16),
-            ],
-            9, slot_flops, 3e6,
+            + [modes_scratch, pltpu.VMEM((many, 2 * cols + coarse_rows), bf16)],
+            5, slot_flops, 3e6,
         )(margin, place_row, local_inverse, part, modes_turned)
         coarse, going = flat_call(
-            functools.partial(coarse_body, side, len(pairs)), tuple(range(1, len(pairs) + 1)),
+            functools.partial(coarse_body, side, len(pairs)),
+            tuple(range(1, len(pairs) + 1)) + (len(pairs) + side + 1, len(pairs) + side + 2),
             [jax.ShapeDtypeStruct((coarse_rows, cols), f32), slots_low], (),
             [
                 pltpu.VMEM((side,) + coarse_inverse.shape, bf16), pltpu.VMEM((owners * coarse_rows, cols), bf16),
-                pltpu.VMEM((slots, cols), f32), pltpu.VMEM((slots, coarse_rows), bf16),
                 pltpu.VMEM((coarse_rows, cols), f32), packed_scratch,
             ],
-            side + 5, slot_flops // 4, 3e6, (0,),
+            side + 3, slot_flops // 4, 3e6, (0,),
         )(here, *pairs, *pieces, solved, lift)
         back = trade(going)
         base, sent = inner(1.0, field, margin, part, local_inverse, coarse)

time: 198 us -> 196 us (0.990)
  Pallas kernels: 123 us -> 120 us
    pallas_call x15, Pallas kernels: 49.3 us -> 47.1 us  [run(): pl.pallas_call(body, in_specs=[pl.BlockSpec(memory_space=p) for p in plac...]
  transfers between devices with their start and end apart: 22 -> 22, of which waited for: 10 -> 12; matrix products, arithmetic and copies ran while one was open for 2% -> 2% of each run, Pallas kernels for 42% -> 41%
where the time goes in v4:
time: 196 us; the launch traced here: 193 us
  Pallas kernels  120 us (61%)
  starting transfers between devices  53.3 us (27%)
  waiting for transfers between devices  11.8 us (6%)
  other arithmetic  3.27 us (2%)
  local copies, waits for them, and re-layouts  3.02 us (2%)
    pallas_call x10, Pallas kernels, call(): run(*(placed(i, x, spec) for i, (x, spec) in enumerate(zip(args, in_specs...  73.3 us
    pallas_call x15, Pallas kernels, run(): pl.pallas_call(body, in_specs=[pl.BlockSpec(memory_space=p) for p in plac...  47.1 us
    all_to_all x11, starting transfers between devices, trade(): lax.all_to_all(blocks, 'wide', split_axis=0, concat_axis=0, tiled=True)  41.3 us
    all_to_all x11, waiting for transfers between devices, trade(): lax.all_to_all(blocks, 'wide', split_axis=0, concat_axis=0, tiled=True)  9.77 us
    ppermute x6, starting transfers between devices, shards(): lax.ppermute(pair, 'wide', [(i, i ^ k) for i in range(owners)])  6.98 us
    ppermute x3, starting transfers between devices, shards(): lax.ppermute(own, 'narrow', [(i, i ^ k) for i in range(side)])  4.45 us
  transfers between devices with their start and end apart: 22, of which 12 were waited for; matrix products, arithmetic and copies ran while one was open for 2% of the time, Pallas kernels for 41%

profile of v4, /device:TPU:0, one launch (start us, length us, event | category | flops | bytes accessed | tf_op | source)
XLA Modules:
  0.0 193.4 jit_solution(9220660093854325935)
XLA Ops:
  0.6 0.7 copy.9
  1.3 0.5 fusion.2
  1.8 0.8 select_reduce_fusion
  2.7 0.7 sub.24
  3.4 5.2 %all-to-all-start = ((s32[8,1,192]{2,1,0:T(1,128)}), s32[8,1,192]{2,1,0:T(1,128)S(1)}, u32[]{:S(2)}, u32[]{:S(2)}) async-start(s32[8,1,192]{2,1,0:T(1,128)} %sub.24), calls=%async_computation | async-start | bytes 16384 | tf_op jit(solution)/shard_map/all_to_all | solution.py:382
  8.5 0.7 fusion.9
  9.2 0.7 divide_bitcast_fusion
  10.0 0.9 convert_element_type.27.rest_4_
  10.9 2.3 %all-to-all-done = s32[8,1,192]{2,1,0:T(1,128)S(1)} async-done(((s32[8,1,192]{2,1,0:T(1,128)}), s32[8,1,192]{2,1,0:T(1,128)S(1)}, u32[]{:S(2)}, u32[]{:S(2)}) %all-to-all-start) | async-done | bytes 6176 | tf_op jit(solution)/shard_map/all_to_all | solution.py:382
  13.3 4.8 %shard_map.86 = (bf16[1536,128]{1,0:T(8,128)(2,1)}, s32[1536,128]{1,0:T(8,128)S(1)}, s32[1024,128]{1,0:T(8,128)}) custom-call(s32[1,1536]{1,0:T(1,128)S(1)} %broadcast_in_dim_reshape.3.row_ref, s32[1,1024]{1,0:T(1,128)S(1)} %fusion.6.place_ref, f32[3072,128]{1,0:T(8,128)} %base_ref.5), custom_call_target="tpu_custom_call" | custom-call | flops 1207959552 | bytes 4000000 | tf_op jit(solution)/shard_map/pallas_call | solution.py:88
  18.1 3.5 %all-to-all-start.1 = ((bf16[8,192,128]{2,1,0:T(8,128)(2,1)}), bf16[8,192,128]{2,1,0:T(8,128)(2,1)S(1)}, u32[]{:S(2)}, u32[]{:S(2)}) async-start(bf16[8,192,128]{2,1,0:T(8,128)(2,1)} %bitcast.60), calls=%async_computation.1 | async-start | bytes 786432 | tf_op jit(solution)/shard_map/all_to_all | solution.py:382
  21.6 3.7 %collective-permute-start.2 = (bf16[128,256]{1,0:T(8,128)(2,1)S(1)}, bf16[128,256]{1,0:T(8,128)(2,1)S(1)}, u32[]{:S(2)}, u32[]{:S(2)}) collective-permute-start(bf16[128,256]{1,0:T(8,128)(2,1)S(1)} %convert_element_type.27.rest_4_), channel_id=1, source_target_pairs={{0,3},{1,2},{2,1},{3,0},{4,7},{5,6},{6,5},{7,4},{8,11},{9,10},{10,... | collective-permute-start | bytes 196616 | tf_op jit(solution)/shard_map/ppermute | solution.py:414
  25.3 0.8 collective-permute-start
  26.1 6.1 %shard_map.87.part_ref = f32[4,1024,128]{2,1,0:T(8,128)} custom-call(f32[3072,128]{1,0:T(8,128)} %base_ref.5, bf16[4,1024,1024]{2,1,0:T(8,128)(2,1)} %matrix_ref.29), custom_call_target="tpu_custom_call" | custom-call | flops 805306368 | bytes 10000000 | tf_op jit(solution)/shard_map/pallas_call | solution.py:79
  32.2 4.1 %shard_map.88 = (bf16[1024,128]{1,0:T(8,128)(2,1)}, bf16[1536,128]{1,0:T(8,128)(2,1)}) custom-call(bf16[1536,128]{1,0:T(8,128)(2,1)S(1)} %bitcast.42, s32[1024,128]{1,0:T(8,128)} %get-tuple-element.53.placed_ref, s32[1,1024]{1,0:T(1,128)} %copy-done, bf16[4,1024,1024]{2,1,0:T(8,128)(2,1)} %matrix_ref.29, f32[4,1024,128]{2,1,0:T(8,128)} %shard_map.87.part_ref), custom_call_target="tpu_custom_call" | custom-call | flops 1207959552 | bytes 3000000 | tf_op jit(solution)/shard_map/pallas_call | solution.py:88
  36.3 4.1 %all-to-all-start.2 = ((bf16[8,192,128]{2,1,0:T(8,128)(2,1)}), bf16[8,192,128]{2,1,0:T(8,128)(2,1)S(1)}, u32[]{:S(2)}, u32[]{:S(2)}) async-start(bf16[8,192,128]{2,1,0:T(8,128)(2,1)} %bitcast.64), calls=%async_computation.2 | async-start | bytes 786432 | tf_op jit(solution)/shard_map/all_to_all | solution.py:382
  40.4 6.9 %shard_map.89 = (f32[3072,128]{1,0:T(8,128)}, f32[1536,128]{1,0:T(8,128)S(1)}) custom-call(f32[4,1024,128]{2,1,0:T(8,128)} %shard_map.87.part_ref, bf16[4,1024,1024]{2,1,0:T(8,128)(2,1)} %matrix_ref.29, bf16[1024,128]{1,0:T(8,128)(2,1)} %get-tuple-element.54.margin_ref, f32[3072,128]{1,0:T(8,128)} %base_ref.7, s32[1536,128]{1,0:T(8,128)S(1)} %get-tuple-element.55.column_ref), custom_call_target="tpu_custom_call" | custom-call | flops 2415919104 | bytes 8000000 | tf_op jit(solution)/shard_map/pallas_call | solution.py:79
  47.2 1.5 all-to-all-done.2
  48.7 2.2 %shard_map.91 = bf16[1536,128]{1,0:T(8,128)(2,1)} custom-call(f32[1536,128]{1,0:T(8,128)S(1)} %get-tuple-element.59.sent_ref, bf16[1536,128]{1,0:T(8,128)(2,1)S(1)} %bitcast.34, s32[1536,128]{1,0:T(8,128)S(1)} %get-tuple-element.55.column_ref, s32[1,1536]{1,0:T(1,128)S(1)} %broadcast_in_dim_reshape.3.row_ref), custom_call_target="tpu_custom_call" | custom-call | flops 603979776 | bytes 3000000 | tf_op jit(solution)/shard_map/pallas_call | solution.py:88
  50.9 3.6 %all-to-all-start.3 = ((bf16[8,192,128]{2,1,0:T(8,128)(2,1)}), bf16[8,192,128]{2,1,0:T(8,128)(2,1)S(1)}, u32[]{:S(2)}, u32[]{:S(2)}) async-start(bf16[8,192,128]{2,1,0:T(8,128)(2,1)} %bitcast.56), calls=%async_computation.3 | async-start | bytes 786432 | tf_op jit(solution)/shard_map/all_to_all | solution.py:382
  54.6 8.3 %shard_map.90 = (f32[4,1024,128]{2,1,0:T(8,128)}, f32[128,128]{1,0:T(8,128)}) custom-call(f32[3072,128]{1,0:T(8,128)} %get-tuple-element.56.base_ref, bf16[1536,128]{1,0:T(8,128)(2,1)S(1)} %bitcast.35, s32[1,1536]{1,0:T(1,128)S(1)} %broadcast_in_dim_reshape.3.row_ref, bf16[4,1024,1024]{2,1,0:T(8,128)(2,1)} %matrix_ref.26, bf16[4,32,1024]{2,1,0:T(8,128)(2,1)} %bitcast.48), custom_call_target="tpu_custom_call" | custom-call | flops 2013265920 | bytes 14000000 | tf_op jit(solution)/shard_map/pallas_call | solution.py:79
  62.9 2.9 %shard_map.92 = (bf16[1024,128]{1,0:T(8,128)(2,1)}, bf16[128,128]{1,0:T(8,128)(2,1)}) custom-call(bf16[1536,128]{1,0:T(8,128)(2,1)S(1)} %bitcast.45, s32[1024,128]{1,0:T(8,128)} %get-tuple-element.53.placed_ref, bf16[4,32,1024]{2,1,0:T(8,128)(2,1)} %bitcast.49, f32[128,128]{1,0:T(8,128)} %get-tuple-element.60.proj_ref), custom_call_target="tpu_custom_call" | custom-call | flops 603979776 | bytes 2000000 | tf_op jit(solution)/shard_map/pallas_call | solution.py:88
  66.0 0.8 constant_dynamic-update-slice_fusion.1
  66.8 0.4 collective-permute-done.3
  67.3 2.7 %collective-permute-start.6 = (bf16[256,128]{1,0:T(8,128)(2,1)S(1)}, bf16[256,128]{1,0:T(8,128)(2,1)S(1)}, u32[]{:S(2)}, u32[]{:S(2)}) collective-permute-start(bf16[256,128]{1,0:T(8,128)(2,1)S(1)} %constant_dynamic-update-slice_fusion.rest_0_), channel_id=1, source_target_pairs={{0,24},{4,28},{8,16},{12,20},{16,8},{20,12},{24,0},{28,4},{1,25},{... | collective-permute-start | bytes 196616 | tf_op jit(solution)/shard_map/ppermute | solution.py:513
  69.9 0.5 collective-permute-start.5
  70.7 3.4 %shard_map.93 = (f32[1536,128]{1,0:T(8,128)S(1)}, bf16[1536,128]{1,0:T(8,128)(2,1)S(1)}) custom-call(bf16[1024,128]{1,0:T(8,128)(2,1)} %get-tuple-element.61.margin_ref, s32[1,1024]{1,0:T(1,128)} %copy-done, bf16[4,1024,1024]{2,1,0:T(8,128)(2,1)} %matrix_ref.26, f32[4,1024,128]{2,1,0:T(8,128)} %get-tuple-element.58.part_ref, bf16[4,32,1024]{2,1,0:T(8,128)(2,1)} %bitcast.50), custom_call_target="tpu_custom_call" | custom-call | flops 1207959552 | bytes 3000000 | tf_op jit(solution)/shard_map/pallas_call | solution.py:88
  74.2 0.5 collective-permute-done.4.rest_1_
  74.7 2.8 %shard_map.94 = (f32[128,128]{1,0:T(8,128)}, bf16[1536,128]{1,0:T(8,128)(2,1)}) custom-call(s32[2]{0:T(128)S(1)} %pad_add_fusion.here_ref, bf16[256,128]{1,0:T(8,128)(2,1)S(1)} %constant_dynamic-update-slice_fusion.rest_0_, bf16[256,128]{1,0:T(8,128)(2,1)S(1)} %collective-permute-done.4.rest_1_, bf16[256,128]{1,0:T(8,128)(2,1)S(1)} %collective-permute-done.5.rest_2_, ...), custom_call_target="tpu_custom_call" | custom-call | flops 301989888 | bytes 3000000 | tf_op jit(solution)/shard_map/pallas_call | solution.py:88
  77.6 3.5 %all-to-all-start.4 = ((bf16[8,192,128]{2,1,0:T(8,128)(2,1)}), bf16[8,192,128]{2,1,0:T(8,128)(2,1)S(1)}, u32[]{:S(2)}, u32[]{:S(2)}) async-start(bf16[8,192,128]{2,1,0:T(8,128)(2,1)} %bitcast.62), calls=%async_computation.4 | async-start | bytes 786432 | tf_op jit(solution)/shard_map/all_to_all | solution.py:382
  81.0 7.2 %shard_map.95 = (f32[3072,128]{1,0:T(8,128)}, f32[1536,128]{1,0:T(8,128)S(1)}) custom-call(f32[4,1024,128]{2,1,0:T(8,128)} %get-tuple-element.58.part_ref, bf16[4,1024,1024]{2,1,0:T(8,128)(2,1)} %matrix_ref.26, bf16[1024,128]{1,0:T(8,128)(2,1)} %get-tuple-element.61.margin_ref, f32[3072,128]{1,0:T(8,128)} %base_ref.5, ...), custom_call_target="tpu_custom_call" | custom-call | flops 2415919104 | bytes 8000000 | tf_op jit(solution)/shard_map/pallas_call | solution.py:79
  88.2 1.1 all-to-all-done.4
  89.3 2.1 %shard_map.97 = bf16[1536,128]{1,0:T(8,128)(2,1)} custom-call(f32[1536,128]{1,0:T(8,128)S(1)} %get-tuple-element.73.sent_ref, bf16[1536,128]{1,0:T(8,128)(2,1)S(1)} %bitcast.40, s32[1536,128]{1,0:T(8,128)S(1)} %get-tuple-element.55.column_ref, s32[1,1536]{1,0:T(1,128)S(1)} %broadcast_in_dim_reshape.3.row_ref), custom_call_target="tpu_custom_call" | custom-call | flops 603979776 | bytes 3000000 | tf_op jit(solution)/shard_map/pallas_call | solution.py:88
  91.4 3.5 %all-to-all-start.5 = ((bf16[8,192,128]{2,1,0:T(8,128)(2,1)}), bf16[8,192,128]{2,1,0:T(8,128)(2,1)S(1)}, u32[]{:S(2)}, u32[]{:S(2)}) async-start(bf16[8,192,128]{2,1,0:T(8,128)(2,1)} %bitcast.57), calls=%async_computation.5 | async-start | bytes 786432 | tf_op jit(solution)/shard_map/all_to_all | solution.py:382
  94.9 7.8 %shard_map.96 = (f32[3072,128]{1,0:T(8,128)}, f32[4,1024,128]{2,1,0:T(8,128)}) custom-call(f32[3072,128]{1,0:T(8,128)} %get-tuple-element.70.base_ref, bf16[1536,128]{1,0:T(8,128)(2,1)S(1)} %bitcast.41, s32[1,1536]{1,0:T(1,128)S(1)} %broadcast_in_dim_reshape.3.row_ref, bf16[4,1024,1024]{2,1,0:T(8,128)(2,1)} %matrix_ref.29), custom_call_target="tpu_custom_call" | custom-call | flops 2013265920 | bytes 14000000 | tf_op jit(solution)/shard_map/pallas_call | solution.py:79
  102.7 0.4 all-to-all-done.5
  103.2 4.0 %shard_map.98 = (bf16[1024,128]{1,0:T(8,128)(2,1)}, bf16[1536,128]{1,0:T(8,128)(2,1)}) custom-call(bf16[1536,128]{1,0:T(8,128)(2,1)S(1)} %bitcast.44, s32[1024,128]{1,0:T(8,128)} %get-tuple-element.53.placed_ref, s32[1,1024]{1,0:T(1,128)} %copy-done, bf16[4,1024,1024]{2,1,0:T(8,128)(2,1)} %matrix_ref.29, f32[4,1024,128]{2,1,0:T(8,128)} %get-tuple-element.72.part_ref), custom_call_target="tpu_custom_call" | custom-call | flops 1207959552 | bytes 3000000 | tf_op jit(solution)/shard_map/pallas_call | solution.py:88
  107.2 3.7 %all-to-all-start.6 = ((bf16[8,192,128]{2,1,0:T(8,128)(2,1)}), bf16[8,192,128]{2,1,0:T(8,128)(2,1)S(1)}, u32[]{:S(2)}, u32[]{:S(2)}) async-start(bf16[8,192,128]{2,1,0:T(8,128)(2,1)} %bitcast.65), calls=%async_computation.6 | async-start | bytes 786432 | tf_op jit(solution)/shard_map/all_to_all | solution.py:382
  110.9 6.9 %shard_map.99 = (f32[3072,128]{1,0:T(8,128)}, f32[1536,128]{1,0:T(8,128)S(1)}) custom-call(f32[4,1024,128]{2,1,0:T(8,128)} %get-tuple-element.72.part_ref, bf16[4,1024,1024]{2,1,0:T(8,128)(2,1)} %matrix_ref.29, bf16[1024,128]{1,0:T(8,128)(2,1)} %get-tuple-element.74.margin_ref, f32[3072,128]{1,0:T(8,128)} %base_ref.7, ...), custom_call_target="tpu_custom_call" | custom-call | flops 2415919104 | bytes 8000000 | tf_op jit(solution)/shard_map/pallas_call | solution.py:79
  117.8 1.5 all-to-all-done.6
  119.3 2.2 %shard_map.101 = bf16[1536,128]{1,0:T(8,128)(2,1)} custom-call(f32[1536,128]{1,0:T(8,128)S(1)} %get-tuple-element.78.sent_ref, bf16[1536,128]{1,0:T(8,128)(2,1)S(1)} %bitcast.36, s32[1536,128]{1,0:T(8,128)S(1)} %get-tuple-element.55.column_ref, s32[1,1536]{1,0:T(1,128)S(1)} %broadcast_in_dim_reshape.3.row_ref), custom_call_target="tpu_custom_call" | custom-call | flops 603979776 | bytes 3000000 | tf_op jit(solution)/shard_map/pallas_call | solution.py:88
  121.4 3.7 %all-to-all-start.7 = ((bf16[8,192,128]{2,1,0:T(8,128)(2,1)}), bf16[8,192,128]{2,1,0:T(8,128)(2,1)S(1)}, u32[]{:S(2)}, u32[]{:S(2)}) async-start(bf16[8,192,128]{2,1,0:T(8,128)(2,1)} %bitcast.58), calls=%async_computation.7 | async-start | bytes 786432 | tf_op jit(solution)/shard_map/all_to_all | solution.py:382
  125.1 8.3 %shard_map.100 = (f32[4,1024,128]{2,1,0:T(8,128)}, f32[128,128]{1,0:T(8,128)}) custom-call(f32[3072,128]{1,0:T(8,128)} %get-tuple-element.75.base_ref, bf16[1536,128]{1,0:T(8,128)(2,1)S(1)} %bitcast.37, s32[1,1536]{1,0:T(1,128)S(1)} %broadcast_in_dim_reshape.3.row_ref, bf16[4,1024,1024]{2,1,0:T(8,128)(2,1)} %matrix_ref.26, bf16[4,32,1024]{2,1,0:T(8,128)(2,1)} %bitcast.52), custom_call_target="tpu_custom_call" | custom-call | flops 2013265920 | bytes 14000000 | tf_op jit(solution)/shard_map/pallas_call | solution.py:79
  133.4 2.9 %shard_map.102 = (bf16[1024,128]{1,0:T(8,128)(2,1)}, bf16[128,128]{1,0:T(8,128)(2,1)}) custom-call(bf16[1536,128]{1,0:T(8,128)(2,1)S(1)} %bitcast.47, s32[1024,128]{1,0:T(8,128)} %get-tuple-element.53.placed_ref, bf16[4,32,1024]{2,1,0:T(8,128)(2,1)} %bitcast.53, f32[128,128]{1,0:T(8,128)} %get-tuple-element.79.proj_ref), custom_call_target="tpu_custom_call" | custom-call | flops 603979776 | bytes 2000000 | tf_op jit(solution)/shard_map/pallas_call | solution.py:88
  136.5 0.8 constant_dynamic-update-slice_fusion.3
  137.3 0.5 collective-permute-done.7
  137.8 2.6 %collective-permute-start.10 = (bf16[256,128]{1,0:T(8,128)(2,1)S(1)}, bf16[256,128]{1,0:T(8,128)(2,1)S(1)}, u32[]{:S(2)}, u32[]{:S(2)}) collective-permute-start(bf16[256,128]{1,0:T(8,128)(2,1)S(1)} %constant_dynamic-update-slice_fusion.2.rest_0_), channel_id=1, source_target_pairs={{0,24},{4,28},{8,16},{12,20},{16,8},{20,12},{24,0},{28,4},{1,25},{... | collective-permute-start | bytes 196616 | tf_op jit(solution)/shard_map/ppermute | solution.py:513
  140.4 0.5 collective-permute-start.9
  140.9 0.3 collective-permute-start.8
  141.3 3.4 %shard_map.103 = (f32[1536,128]{1,0:T(8,128)S(1)}, bf16[1536,128]{1,0:T(8,128)(2,1)S(1)}) custom-call(bf16[1024,128]{1,0:T(8,128)(2,1)} %get-tuple-element.80.margin_ref, s32[1,1024]{1,0:T(1,128)} %copy-done, bf16[4,1024,1024]{2,1,0:T(8,128)(2,1)} %matrix_ref.26, f32[4,1024,128]{2,1,0:T(8,128)} %get-tuple-element.77.part_ref, bf16[4,32,1024]{2,1,0:T(8,128)(2,1)} %bitcast.54), custom_call_target="tpu_custom_call" | custom-call | flops 1207959552 | bytes 3000000 | tf_op jit(solution)/shard_map/pallas_call | solution.py:88
  144.7 0.5 collective-permute-done.8.rest_1_
  145.2 2.9 %shard_map.104 = (f32[128,128]{1,0:T(8,128)}, bf16[1536,128]{1,0:T(8,128)(2,1)}) custom-call(s32[2]{0:T(128)S(1)} %pad_add_fusion.here_ref, bf16[256,128]{1,0:T(8,128)(2,1)S(1)} %constant_dynamic-update-slice_fusion.2.rest_0_, bf16[256,128]{1,0:T(8,128)(2,1)S(1)} %collective-permute-done.8.rest_1_, bf16[256,128]{1,0:T(8,128)(2,1)S(1)} %collective-permute-done.9.rest_2_, ...), custom_call_target="tpu_custom_call" | custom-call | flops 301989888 | bytes 3000000 | tf_op jit(solution)/shard_map/pallas_call | solution.py:88
  148.1 3.5 %all-to-all-start.8 = ((bf16[8,192,128]{2,1,0:T(8,128)(2,1)}), bf16[8,192,128]{2,1,0:T(8,128)(2,1)S(1)}, u32[]{:S(2)}, u32[]{:S(2)}) async-start(bf16[8,192,128]{2,1,0:T(8,128)(2,1)} %bitcast.61), calls=%async_computation.8 | async-start | bytes 786432 | tf_op jit(solution)/shard_map/all_to_all | solution.py:382
  151.5 7.2 %shard_map.105 = (f32[3072,128]{1,0:T(8,128)}, f32[1536,128]{1,0:T(8,128)S(1)}) custom-call(f32[4,1024,128]{2,1,0:T(8,128)} %get-tuple-element.77.part_ref, bf16[4,1024,1024]{2,1,0:T(8,128)(2,1)} %matrix_ref.26, bf16[1024,128]{1,0:T(8,128)(2,1)} %get-tuple-element.80.margin_ref, f32[3072,128]{1,0:T(8,128)} %get-tuple-element.81.base_ref, ...), custom_call_target="tpu_custom_call" | custom-call | flops 2415919104 | bytes 8000000 | tf_op jit(solution)/shard_map/pallas_call | solution.py:79
  158.8 1.1 all-to-all-done.8
  159.8 2.1 %shard_map.107 = bf16[1536,128]{1,0:T(8,128)(2,1)} custom-call(f32[1536,128]{1,0:T(8,128)S(1)} %get-tuple-element.90.sent_ref, bf16[1536,128]{1,0:T(8,128)(2,1)S(1)} %bitcast.38, s32[1536,128]{1,0:T(8,128)S(1)} %get-tuple-element.55.column_ref, s32[1,1536]{1,0:T(1,128)S(1)} %broadcast_in_dim_reshape.3.row_ref), custom_call_target="tpu_custom_call" | custom-call | flops 603979776 | bytes 3000000 | tf_op jit(solution)/shard_map/pallas_call | solution.py:88
  161.9 3.5 %all-to-all-start.9 = ((bf16[8,192,128]{2,1,0:T(8,128)(2,1)}), bf16[8,192,128]{2,1,0:T(8,128)(2,1)S(1)}, u32[]{:S(2)}, u32[]{:S(2)}) async-start(bf16[8,192,128]{2,1,0:T(8,128)(2,1)} %bitcast.59), calls=%async_computation.9 | async-start | bytes 786432 | tf_op jit(solution)/shard_map/all_to_all | solution.py:382
  165.4 7.8 %shard_map.106 = (f32[3072,128]{1,0:T(8,128)}, f32[4,1024,128]{2,1,0:T(8,128)}) custom-call(f32[3072,128]{1,0:T(8,128)} %get-tuple-element.86.base_ref, bf16[1536,128]{1,0:T(8,128)(2,1)S(1)} %bitcast.39, s32[1,1536]{1,0:T(1,128)S(1)} %broadcast_in_dim_reshape.3.row_ref, bf16[4,1024,1024]{2,1,0:T(8,128)(2,1)} %matrix_ref.29), custom_call_target="tpu_custom_call" | custom-call | flops 2013265920 | bytes 14000000 | tf_op jit(solution)/shard_map/pallas_call | solution.py:79
  173.2 0.4 all-to-all-done.9
  173.7 4.0 %shard_map.108 = (bf16[1024,128]{1,0:T(8,128)(2,1)}, bf16[1536,128]{1,0:T(8,128)(2,1)}) custom-call(bf16[1536,128]{1,0:T(8,128)(2,1)S(1)} %bitcast.43, s32[1024,128]{1,0:T(8,128)} %get-tuple-element.53.placed_ref, s32[1,1024]{1,0:T(1,128)} %copy-done, bf16[4,1024,1024]{2,1,0:T(8,128)(2,1)} %matrix_ref.29, f32[4,1024,128]{2,1,0:T(8,128)} %get-tuple-element.89.part_ref), custom_call_target="tpu_custom_call" | custom-call | flops 1207959552 | bytes 3000000 | tf_op jit(solution)/shard_map/pallas_call | solution.py:88
  177.7 3.7 %all-to-all-start.10 = ((bf16[8,192,128]{2,1,0:T(8,128)(2,1)}), bf16[8,192,128]{2,1,0:T(8,128)(2,1)S(1)}, u32[]{:S(2)}, u32[]{:S(2)}) async-start(bf16[8,192,128]{2,1,0:T(8,128)(2,1)} %bitcast.63), calls=%async_computation.10 | async-start | bytes 786432 | tf_op jit(solution)/shard_map/all_to_all | solution.py:382
  181.4 6.8 %shard_map.109 = (f32[3072,128]{1,0:T(8,128)S(1)}, f32[1536,128]{1,0:T(8,128)}) custom-call(f32[4,1024,128]{2,1,0:T(8,128)} %get-tuple-element.89.part_ref, bf16[4,1024,1024]{2,1,0:T(8,128)(2,1)} %matrix_ref.29, bf16[1024,128]{1,0:T(8,128)(2,1)} %get-tuple-element.91.margin_ref, f32[3072,128]{1,0:T(8,128)} %base_ref.7, ...), custom_call_target="tpu_custom_call" | custom-call | flops 2415919104 | bytes 8000000 | tf_op jit(solution)/shard_map/pallas_call | solution.py:79
  188.2 1.5 all-to-all-done.10
  189.8 3.5 %shard_map.110 = f32[3072,128]{1,0:T(8,128)} custom-call(f32[3072,128]{1,0:T(8,128)S(1)} %get-tuple-element.92.base_ref, bf16[1536,128]{1,0:T(8,128)(2,1)S(1)} %bitcast.46, s32[1,1536]{1,0:T(1,128)S(1)} %broadcast_in_dim_reshape.3.row_ref), custom_call_target="tpu_custom_call" | custom-call | flops 1207959552 | bytes 4000000 | tf_op jit(solution)/shard_map/pallas_call | solution.py:88
  (36 shorter events, 1.1 us)
Async XLA Ops:
  3.4 9.9 %all-to-all-start = ((s32[8,1,192]{2,1,0:T(1,128)}), s32[8,1,192]{2,1,0:T(1,128)S(1)}, u32[]{:S(2)}, u32[]{:S(2)}) async-start(s32[8,1,192]{2,1,0:T(1,128)} %sub.24), calls=%async_computation | async-start | bytes 16384 | tf_op jit(solution)/shard_map/all_to_all | solution.py:382
  10.0 8.1 %copy-start = (s32[1,1024]{1,0:T(1,128)}, s32[1,1024]{1,0:T(1,128)S(1)}, u32[]{:S(2)}) copy-start(s32[1,1024]{1,0:T(1,128)S(1)} %fusion.6.place_ref) | copy-start | bytes 12292
  10.9 14.4 %copy-start.1 = (bf16[128,256]{1,0:T(8,128)(2,1)}, bf16[128,256]{1,0:T(8,128)(2,1)S(1)}, u32[]{:S(2)}) copy-start(bf16[128,256]{1,0:T(8,128)(2,1)S(1)} %convert_element_type.27.rest_4_) | copy-start | bytes 196612
  18.1 14.1 %all-to-all-start.1 = ((bf16[8,192,128]{2,1,0:T(8,128)(2,1)}), bf16[8,192,128]{2,1,0:T(8,128)(2,1)S(1)}, u32[]{:S(2)}, u32[]{:S(2)}) async-start(bf16[8,192,128]{2,1,0:T(8,128)(2,1)} %bitcast.60), calls=%async_computation.1 | async-start | bytes 786432 | tf_op jit(solution)/shard_map/all_to_all | solution.py:382
  21.6 10.6 %collective-permute-start.2 = (bf16[128,256]{1,0:T(8,128)(2,1)S(1)}, bf16[128,256]{1,0:T(8,128)(2,1)S(1)}, u32[]{:S(2)}, u32[]{:S(2)}) collective-permute-start(bf16[128,256]{1,0:T(8,128)(2,1)S(1)} %convert_element_type.27.rest_4_), channel_id=1, source_target_pairs={{0,3},{1,2},{2,1},{3,0},{4,7},{5,6},{6,5},{7,4},{8,11},{9,10},{10,... | collective-permute-start | bytes 196616 | tf_op jit(solution)/shard_map/ppermute | solution.py:414
  25.3 6.9 %collective-permute-start.1 = (bf16[128,256]{1,0:T(8,128)(2,1)S(1)}, bf16[128,256]{1,0:T(8,128)(2,1)S(1)}, u32[]{:S(2)}, u32[]{:S(2)}) collective-permute-start(bf16[128,256]{1,0:T(8,128)(2,1)S(1)} %convert_element_type.27.rest_4_), channel_id=1, source_target_pairs={{0,2},{1,3},{2,0},{3,1},{4,6},{5,7},{6,4},{7,5},{8,10},{9,11},{10,... | collective-permute-start | bytes 196616 | tf_op jit(solution)/shard_map/ppermute | solution.py:414
  25.3 6.9 %collective-permute-start = (bf16[128,256]{1,0:T(8,128)(2,1)S(1)}, bf16[128,256]{1,0:T(8,128)(2,1)S(1)}, u32[]{:S(2)}, u32[]{:S(2)}) collective-permute-start(bf16[128,256]{1,0:T(8,128)(2,1)S(1)} %convert_element_type.27.rest_4_), channel_id=1, source_target_pairs={{0,1},{1,0},{2,3},{3,2},{4,5},{5,4},{6,7},{7,6},{8,9},{9,8},{10,11... | collective-permute-start | bytes 196616 | tf_op jit(solution)/shard_map/ppermute | solution.py:414
  32.2 4.1 %copy-start.2 = (bf16[128,256]{1,0:T(8,128)(2,1)}, bf16[128,256]{1,0:T(8,128)(2,1)S(1)}, u32[]{:S(2)}) copy-start(bf16[128,256]{1,0:T(8,128)(2,1)S(1)} %collective-permute-done.2.rest_7_) | copy-start | bytes 196612
  32.2 4.1 %copy-start.3 = (bf16[128,256]{1,0:T(8,128)(2,1)}, bf16[128,256]{1,0:T(8,128)(2,1)S(1)}, u32[]{:S(2)}) copy-start(bf16[128,256]{1,0:T(8,128)(2,1)S(1)} %collective-permute-done.1.rest_6_) | copy-start | bytes 196612
  32.2 4.1 %copy-start.4 = (bf16[128,256]{1,0:T(8,128)(2,1)}, bf16[128,256]{1,0:T(8,128)(2,1)S(1)}, u32[]{:S(2)}) copy-start(bf16[128,256]{1,0:T(8,128)(2,1)S(1)} %collective-permute-done.rest_5_) | copy-start | bytes 196612
  36.3 12.4 %all-to-all-start.2 = ((bf16[8,192,128]{2,1,0:T(8,128)(2,1)}), bf16[8,192,128]{2,1,0:T(8,128)(2,1)S(1)}, u32[]{:S(2)}, u32[]{:S(2)}) async-start(bf16[8,192,128]{2,1,0:T(8,128)(2,1)} %bitcast.64), calls=%async_computation.2 | async-start | bytes 786432 | tf_op jit(solution)/shard_map/all_to_all | solution.py:382
  50.9 12.0 %all-to-all-start.3 = ((bf16[8,192,128]{2,1,0:T(8,128)(2,1)}), bf16[8,192,128]{2,1,0:T(8,128)(2,1)S(1)}, u32[]{:S(2)}, u32[]{:S(2)}) async-start(bf16[8,192,128]{2,1,0:T(8,128)(2,1)} %bitcast.56), calls=%async_computation.3 | async-start | bytes 786432 | tf_op jit(solution)/shard_map/all_to_all | solution.py:382
  65.8 1.5 collective-permute-start.3
  67.3 6.9 %collective-permute-start.6 = (bf16[256,128]{1,0:T(8,128)(2,1)S(1)}, bf16[256,128]{1,0:T(8,128)(2,1)S(1)}, u32[]{:S(2)}, u32[]{:S(2)}) collective-permute-start(bf16[256,128]{1,0:T(8,128)(2,1)S(1)} %constant_dynamic-update-slice_fusion.rest_0_), channel_id=1, source_target_pairs={{0,24},{4,28},{8,16},{12,20},{16,8},{20,12},{24,0},{28,4},{1,25},{... | collective-permute-start | bytes 196616 | tf_op jit(solution)/shard_map/ppermute | solution.py:513
  69.9 4.3 %collective-permute-start.5 = (bf16[256,128]{1,0:T(8,128)(2,1)S(1)}, bf16[256,128]{1,0:T(8,128)(2,1)S(1)}, u32[]{:S(2)}, u32[]{:S(2)}) collective-permute-start(bf16[256,128]{1,0:T(8,128)(2,1)S(1)} %constant_dynamic-update-slice_fusion.rest_0_), channel_id=1, source_target_pairs={{0,16},{4,20},{8,24},{12,28},{16,0},{20,4},{24,8},{28,12},{1,17},{... | collective-permute-start | bytes 196616 | tf_op jit(solution)/shard_map/ppermute | solution.py:513
  70.5 4.3 %collective-permute-start.4 = (bf16[256,128]{1,0:T(8,128)(2,1)S(1)}, bf16[256,128]{1,0:T(8,128)(2,1)S(1)}, u32[]{:S(2)}, u32[]{:S(2)}) collective-permute-start(bf16[256,128]{1,0:T(8,128)(2,1)S(1)} %constant_dynamic-update-slice_fusion.rest_0_), channel_id=1, source_target_pairs={{0,8},{4,12},{8,0},{12,4},{16,24},{20,28},{24,16},{28,20},{1,9},{5... | collective-permute-start | bytes 196616 | tf_op jit(solution)/shard_map/ppermute | solution.py:513
  77.6 11.8 %all-to-all-start.4 = ((bf16[8,192,128]{2,1,0:T(8,128)(2,1)}), bf16[8,192,128]{2,1,0:T(8,128)(2,1)S(1)}, u32[]{:S(2)}, u32[]{:S(2)}) async-start(bf16[8,192,128]{2,1,0:T(8,128)(2,1)} %bitcast.62), calls=%async_computation.4 | async-start | bytes 786432 | tf_op jit(solution)/shard_map/all_to_all | solution.py:382
  91.4 11.7 %all-to-all-start.5 = ((bf16[8,192,128]{2,1,0:T(8,128)(2,1)}), bf16[8,192,128]{2,1,0:T(8,128)(2,1)S(1)}, u32[]{:S(2)}, u32[]{:S(2)}) async-start(bf16[8,192,128]{2,1,0:T(8,128)(2,1)} %bitcast.57), calls=%async_computation.5 | async-start | bytes 786432 | tf_op jit(solution)/shard_map/all_to_all | solution.py:382
  107.2 12.0 %all-to-all-start.6 = ((bf16[8,192,128]{2,1,0:T(8,128)(2,1)}), bf16[8,192,128]{2,1,0:T(8,128)(2,1)S(1)}, u32[]{:S(2)}, u32[]{:S(2)}) async-start(bf16[8,192,128]{2,1,0:T(8,128)(2,1)} %bitcast.65), calls=%async_computation.6 | async-start | bytes 786432 | tf_op jit(solution)/shard_map/all_to_all | solution.py:382
  121.4 12.0 %all-to-all-start.7 = ((bf16[8,192,128]{2,1,0:T(8,128)(2,1)}), bf16[8,192,128]{2,1,0:T(8,128)(2,1)S(1)}, u32[]{:S(2)}, u32[]{:S(2)}) async-start(bf16[8,192,128]{2,1,0:T(8,128)(2,1)} %bitcast.58), calls=%async_computation.7 | async-start | bytes 786432 | tf_op jit(solution)/shard_map/all_to_all | solution.py:382
  136.3 1.5 collective-permute-start.7
  137.8 6.9 %collective-permute-start.10 = (bf16[256,128]{1,0:T(8,128)(2,1)S(1)}, bf16[256,128]{1,0:T(8,128)(2,1)S(1)}, u32[]{:S(2)}, u32[]{:S(2)}) collective-permute-start(bf16[256,128]{1,0:T(8,128)(2,1)S(1)} %constant_dynamic-update-slice_fusion.2.rest_0_), channel_id=1, source_target_pairs={{0,24},{4,28},{8,16},{12,20},{16,8},{20,12},{24,0},{28,4},{1,25},{... | collective-permute-start | bytes 196616 | tf_op jit(solution)/shard_map/ppermute | solution.py:513
  140.4 4.3 %collective-permute-start.9 = (bf16[256,128]{1,0:T(8,128)(2,1)S(1)}, bf16[256,128]{1,0:T(8,128)(2,1)S(1)}, u32[]{:S(2)}, u32[]{:S(2)}) collective-permute-start(bf16[256,128]{1,0:T(8,128)(2,1)S(1)} %constant_dynamic-update-slice_fusion.2.rest_0_), channel_id=1, source_target_pairs={{0,16},{4,20},{8,24},{12,28},{16,0},{20,4},{24,8},{28,12},{1,17},{... | collective-permute-start | bytes 196616 | tf_op jit(solution)/shard_map/ppermute | solution.py:513
  140.9 4.3 %collective-permute-start.8 = (bf16[256,128]{1,0:T(8,128)(2,1)S(1)}, bf16[256,128]{1,0:T(8,128)(2,1)S(1)}, u32[]{:S(2)}, u32[]{:S(2)}) collective-permute-start(bf16[256,128]{1,0:T(8,128)(2,1)S(1)} %constant_dynamic-update-slice_fusion.2.rest_0_), channel_id=1, source_target_pairs={{0,8},{4,12},{8,0},{12,4},{16,24},{20,28},{24,16},{28,20},{1,9},{5... | collective-permute-start | bytes 196616 | tf_op jit(solution)/shard_map/ppermute | solution.py:513
  148.1 11.7 %all-to-all-start.8 = ((bf16[8,192,128]{2,1,0:T(8,128)(2,1)}), bf16[8,192,128]{2,1,0:T(8,128)(2,1)S(1)}, u32[]{:S(2)}, u32[]{:S(2)}) async-start(bf16[8,192,128]{2,1,0:T(8,128)(2,1)} %bitcast.61), calls=%async_computation.8 | async-start | bytes 786432 | tf_op jit(solution)/shard_map/all_to_all | solution.py:382
  161.9 11.7 %all-to-all-start.9 = ((bf16[8,192,128]{2,1,0:T(8,128)(2,1)}), bf16[8,192,128]{2,1,0:T(8,128)(2,1)S(1)}, u32[]{:S(2)}, u32[]{:S(2)}) async-start(bf16[8,192,128]{2,1,0:T(8,128)(2,1)} %bitcast.59), calls=%async_computation.9 | async-start | bytes 786432 | tf_op jit(solution)/shard_map/all_to_all | solution.py:382
  177.7 12.0 %all-to-all-start.10 = ((bf16[8,192,128]{2,1,0:T(8,128)(2,1)}), bf16[8,192,128]{2,1,0:T(8,128)(2,1)S(1)}, u32[]{:S(2)}, u32[]{:S(2)}) async-start(bf16[8,192,128]{2,1,0:T(8,128)(2,1)} %bitcast.63), calls=%async_computation.10 | async-start | bytes 786432 | tf_op jit(solution)/shard_map/all_to_all | solution.py:382

commit v5 on v4

--- a/solution.py
+++ b/solution.py
@@ -287,17 +287,16 @@
         lift_ref[at, :] = packed[:, 2 * cols :].astype(bf16)
 
 
-def coarse_body(side, pair_count, here_ref, *rest):
-    pairs, rest = rest[:pair_count], rest[pair_count:]
+def coarse_body(side, share_count, here_ref, *rest):
+    shares, rest = rest[:share_count], rest[share_count:]
     inverse_refs = rest[:side]
     solved_ref, lift_ref, coarse_ref, out_ref = rest[side : side + 4]
     inverse, everyone, made, packed, sems = rest[side + 4 :]
     loads = begin(sems, 0, [(inverse_refs[k], inverse.at[k]) for k in range(side)])
     height = made.shape[0]
-    for k, pair_ref in enumerate(pairs):
-        for j in range(2):
-            at = pl.multiple_of((here_ref[1] ^ (2 * k + j)) * height, height)
-            everyone[pl.ds(at, height), :] = pair_ref[j * height : (j + 1) * height, :]
+    for k, share_ref in enumerate(shares):
+        at = pl.multiple_of((here_ref[1] ^ k) * height, height)
+        everyone[pl.ds(at, height), :] = share_ref[...]
     finish(loads)
     value = 0.0
     for k in range(side):
@@ -374,15 +373,16 @@
     earlier = (jnp.arange(many)[:, None] > jnp.arange(many)[None, :]).astype(bf16)
     rank = jnp.sum(dot(earlier, onehot) * onehot.astype(f32), axis=1).astype(i32)
     place = source * capacity + rank
-    hit = place[:, None] == jnp.arange(slots, dtype=i32)[None, :]
-    asked = jnp.sum(jnp.where(hit, row[:, None] + 1, 0), axis=0) - 1
+    slot = jnp.arange(slots, dtype=i32).reshape(1, owners, 1, capacity)
+    here_hit = place[:, None, None, None] == slot
+    asked = jnp.sum(jnp.where(here_hit, row[:, None, None, None] + 1, 0), axis=0)
 
     def trade(x):
         blocks = x.reshape((owners, x.shape[0] // owners) + x.shape[1:])
         got = lax.all_to_all(blocks, "wide", split_axis=0, concat_axis=0, tiled=True)
         return got.reshape(x.shape)
 
-    wanted = trade(asked)
+    wanted = lax.all_to_all(asked, "wide", split_axis=0, concat_axis=0, tiled=True).reshape(slots) - 1
     wanted_row = wanted[None, :]
     place_row = place[None, :]
     modes_turned = jnp.swapaxes(modes, 1, 2)
@@ -508,10 +508,10 @@
             5, slot_flops // 2, 2e6,
         )(came, place_column, modes_turned, proj)
         partner = lax.ppermute(projection, "wide", [(i, i ^ 1) for i in range(owners)])
-        pair = jnp.concatenate([projection, partner], axis=0)
-        pairs = [pair] + [
-            lax.ppermute(pair, "wide", [(i, i ^ k) for i in range(owners)]) for k in range(2, owners, 2)
-        ]
+        shares = []
+        for k in range(0, owners, 2):
+            for x in (projection, partner):
+                shares.append(lax.ppermute(x, "wide", [(i, i ^ k) for i in range(owners)]) if k > 0 else x)
         solved, lift = flat_call(
             ready_body, (),
             [jax.ShapeDtypeStruct((slots, cols), f32), jax.ShapeDtypeStruct((slots, coarse_rows), bf16)], (0, 1),
@@ -520,15 +520,15 @@
             5, slot_flops, 3e6,
         )(margin, place_row, local_inverse, part, modes_turned)
         coarse, going = flat_call(
-            functools.partial(coarse_body, side, len(pairs)),
-            tuple(range(1, len(pairs) + 1)) + (len(pairs) + side + 1, len(pairs) + side + 2),
+            functools.partial(coarse_body, side, len(shares)),
+            tuple(range(1, len(shares) + 1)) + (len(shares) + side + 1, len(shares) + side + 2),
             [jax.ShapeDtypeStruct((coarse_rows, cols), f32), slots_low], (),
             [
                 pltpu.VMEM((side,) + coarse_inverse.shape, bf16), pltpu.VMEM((owners * coarse_rows, cols), bf16),
                 pltpu.VMEM((coarse_rows, cols), f32), packed_scratch,
             ],
             side + 3, slot_flops // 4, 3e6, (0,),
-        )(here, *pairs, *pieces, solved, lift)
+        )(here, *shares, *pieces, solved, lift)
         back = trade(going)
         base, sent = inner(1.0, field, margin, part, local_inverse, coarse)
         going = relay(1.0, sent, back)

time: 196 us -> 200 us (1.020)
  starting transfers between devices: 53.3 us -> 60.6 us
    ppermute x6 -> x12, starting transfers between devices: 6.98 us -> 14 us  [shards(): lax.ppermute(x, 'wide', [(i, i ^ k) for i in range(owners)])]
    all_to_all x0 -> x1, starting transfers between devices: none -> 5.17 us  [shards(): lax.all_to_all(asked, 'wide', split_axis=0, concat_axis=0, tiled=True)]
    all_to_all x11 -> x10, starting transfers between devices: 41.3 us -> 36.5 us  [trade(): lax.all_to_all(blocks, 'wide', split_axis=0, concat_axis=0, tiled=True)]
    all_to_all x0 -> x1, waiting for transfers between devices: none -> 2.32 us  [shards(): lax.all_to_all(asked, 'wide', split_axis=0, concat_axis=0, tiled=True)]
    all_to_all x11 -> x10, waiting for transfers between devices: 9.77 us -> 7.58 us  [trade(): lax.all_to_all(blocks, 'wide', split_axis=0, concat_axis=0, tiled=True)]
  transfers between devices with their start and end apart: 22 -> 28, of which waited for: 12 -> 10; matrix products, arithmetic and copies ran while one was open for 2% -> 1% of each run, Pallas kernels for 41% -> 40%
where the time goes in v5:
time: 200 us; the launch traced here: 198 us
  Pallas kernels  120 us (60%)
  starting transfers between devices  60.6 us (30%)
  waiting for transfers between devices  10.6 us (5%)
  other arithmetic  3.42 us (2%)
    pallas_call x10, Pallas kernels, call(): run(*(placed(i, x, spec) for i, (x, spec) in enumerate(zip(args, in_specs...  73.2 us
    pallas_call x15, Pallas kernels, run(): pl.pallas_call(body, in_specs=[pl.BlockSpec(memory_space=p) for p in plac...  47 us
    all_to_all x10, starting transfers between devices, trade(): lax.all_to_all(blocks, 'wide', split_axis=0, concat_axis=0, tiled=True)  36.5 us
    ppermute x12, starting transfers between devices, shards(): lax.ppermute(x, 'wide', [(i, i ^ k) for i in range(owners)])  14 us
    all_to_all x10, waiting for transfers between devices, trade(): lax.all_to_all(blocks, 'wide', split_axis=0, concat_axis=0, tiled=True)  7.58 us
    all_to_all x1, starting transfers between devices, shards(): lax.all_to_all(asked, 'wide', split_axis=0, concat_axis=0, tiled=True)  5.17 us
    ppermute x3, starting transfers between devices, shards(): lax.ppermute(own, 'narrow', [(i, i ^ k) for i in range(side)])  4.45 us
  transfers between devices with their start and end apart: 28, of which 10 were waited for; matrix products, arithmetic and copies ran while one was open for 1% of the time, Pallas kernels for 40%

profile of v5, /device:TPU:0, one launch (start us, length us, event | category | flops | bytes accessed | tf_op | source)
XLA Modules:
  0.0 197.9 jit_solution(13294072540008876561)
XLA Ops:
  0.6 0.7 copy.10
  1.3 0.5 fusion.2
  1.9 1.0 select_reduce_fusion
  2.8 0.6 copy.9
  3.4 5.2 %all-to-all-start = ((s32[8,1,192]{2,1,0:T(1,128)}), s32[8,1,192]{2,1,0:T(1,128)S(1)}, u32[]{:S(2)}, u32[]{:S(2)}) async-start(s32[8,1,192]{2,1,0:T(1,128)} %copy.9), calls=%async_computation | async-start | bytes 16384 | tf_op jit(solution)/shard_map/all_to_all | solution.py:385
  8.6 0.7 fusion.9
  9.3 0.7 divide_bitcast_fusion
  10.1 0.9 convert_element_type.27.rest_8_
  11.0 2.3 %all-to-all-done = s32[8,1,192]{2,1,0:T(1,128)S(1)} async-done(((s32[8,1,192]{2,1,0:T(1,128)}), s32[8,1,192]{2,1,0:T(1,128)S(1)}, u32[]{:S(2)}, u32[]{:S(2)}) %all-to-all-start) | async-done | bytes 6176 | tf_op jit(solution)/shard_map/all_to_all | solution.py:385
  13.4 4.8 %shard_map.86 = (bf16[1536,128]{1,0:T(8,128)(2,1)}, s32[1536,128]{1,0:T(8,128)S(1)}, s32[1024,128]{1,0:T(8,128)}) custom-call(s32[1,1536]{1,0:T(1,128)S(1)} %sub.24.row_ref, s32[1,1024]{1,0:T(1,128)S(1)} %fusion.6.place_ref, f32[3072,128]{1,0:T(8,128)} %base_ref.5), custom_call_target="tpu_custom_call" | custom-call | flops 1207959552 | bytes 4000000 | tf_op jit(solution)/shard_map/pallas_call | solution.py:88
  18.2 3.5 %all-to-all-start.1 = ((bf16[8,192,128]{2,1,0:T(8,128)(2,1)}), bf16[8,192,128]{2,1,0:T(8,128)(2,1)S(1)}, u32[]{:S(2)}, u32[]{:S(2)}) async-start(bf16[8,192,128]{2,1,0:T(8,128)(2,1)} %bitcast.61), calls=%async_computation.1 | async-start | bytes 786432 | tf_op jit(solution)/shard_map/all_to_all | solution.py:382
  21.7 3.7 %collective-permute-start.2 = (bf16[128,256]{1,0:T(8,128)(2,1)S(1)}, bf16[128,256]{1,0:T(8,128)(2,1)S(1)}, u32[]{:S(2)}, u32[]{:S(2)}) collective-permute-start(bf16[128,256]{1,0:T(8,128)(2,1)S(1)} %convert_element_type.27.rest_8_), channel_id=1, source_target_pairs={{0,3},{1,2},{2,1},{3,0},{4,7},{5,6},{6,5},{7,4},{8,11},{9,10},{10,... | collective-permute-start | bytes 196616 | tf_op jit(solution)/shard_map/ppermute | solution.py:414
  25.3 0.8 collective-permute-start
  26.1 6.1 %shard_map.87.part_ref = f32[4,1024,128]{2,1,0:T(8,128)} custom-call(f32[3072,128]{1,0:T(8,128)} %base_ref.5, bf16[4,1024,1024]{2,1,0:T(8,128)(2,1)} %matrix_ref.29), custom_call_target="tpu_custom_call" | custom-call | flops 805306368 | bytes 10000000 | tf_op jit(solution)/shard_map/pallas_call | solution.py:79
  32.3 4.1 %shard_map.88 = (bf16[1024,128]{1,0:T(8,128)(2,1)}, bf16[1536,128]{1,0:T(8,128)(2,1)}) custom-call(bf16[1536,128]{1,0:T(8,128)(2,1)S(1)} %bitcast.43, s32[1024,128]{1,0:T(8,128)} %get-tuple-element.53.placed_ref, s32[1,1024]{1,0:T(1,128)} %copy-done, bf16[4,1024,1024]{2,1,0:T(8,128)(2,1)} %matrix_ref.29, f32[4,1024,128]{2,1,0:T(8,128)} %shard_map.87.part_ref), custom_call_target="tpu_custom_call" | custom-call | flops 1207959552 | bytes 3000000 | tf_op jit(solution)/shard_map/pallas_call | solution.py:88
  36.4 4.1 %all-to-all-start.2 = ((bf16[8,192,128]{2,1,0:T(8,128)(2,1)}), bf16[8,192,128]{2,1,0:T(8,128)(2,1)S(1)}, u32[]{:S(2)}, u32[]{:S(2)}) async-start(bf16[8,192,128]{2,1,0:T(8,128)(2,1)} %bitcast.65), calls=%async_computation.2 | async-start | bytes 786432 | tf_op jit(solution)/shard_map/all_to_all | solution.py:382
  40.4 6.9 %shard_map.89 = (f32[3072,128]{1,0:T(8,128)}, f32[1536,128]{1,0:T(8,128)S(1)}) custom-call(f32[4,1024,128]{2,1,0:T(8,128)} %shard_map.87.part_ref, bf16[4,1024,1024]{2,1,0:T(8,128)(2,1)} %matrix_ref.29, bf16[1024,128]{1,0:T(8,128)(2,1)} %get-tuple-element.54.margin_ref, f32[3072,128]{1,0:T(8,128)} %base_ref.7, s32[1536,128]{1,0:T(8,128)S(1)} %get-tuple-element.55.column_ref), custom_call_target="tpu_custom_call" | custom-call | flops 2415919104 | bytes 8000000 | tf_op jit(solution)/shard_map/pallas_call | solution.py:79
  47.3 1.5 all-to-all-done.2
  48.8 2.1 %shard_map.91 = bf16[1536,128]{1,0:T(8,128)(2,1)} custom-call(f32[1536,128]{1,0:T(8,128)S(1)} %get-tuple-element.59.sent_ref, bf16[1536,128]{1,0:T(8,128)(2,1)S(1)} %bitcast.35, s32[1536,128]{1,0:T(8,128)S(1)} %get-tuple-element.55.column_ref, s32[1,1536]{1,0:T(1,128)S(1)} %sub.24.row_ref), custom_call_target="tpu_custom_call" | custom-call | flops 603979776 | bytes 3000000 | tf_op jit(solution)/shard_map/pallas_call | solution.py:88
  50.9 3.6 %all-to-all-start.3 = ((bf16[8,192,128]{2,1,0:T(8,128)(2,1)}), bf16[8,192,128]{2,1,0:T(8,128)(2,1)S(1)}, u32[]{:S(2)}, u32[]{:S(2)}) async-start(bf16[8,192,128]{2,1,0:T(8,128)(2,1)} %bitcast.57), calls=%async_computation.3 | async-start | bytes 786432 | tf_op jit(solution)/shard_map/all_to_all | solution.py:382
  54.6 8.3 %shard_map.90 = (f32[4,1024,128]{2,1,0:T(8,128)}, f32[128,128]{1,0:T(8,128)}) custom-call(f32[3072,128]{1,0:T(8,128)} %get-tuple-element.56.base_ref, bf16[1536,128]{1,0:T(8,128)(2,1)S(1)} %bitcast.36, s32[1,1536]{1,0:T(1,128)S(1)} %sub.24.row_ref, bf16[4,1024,1024]{2,1,0:T(8,128)(2,1)} %matrix_ref.26, bf16[4,32,1024]{2,1,0:T(8,128)(2,1)} %bitcast.49), custom_call_target="tpu_custom_call" | custom-call | flops 2013265920 | bytes 14000000 | tf_op jit(solution)/shard_map/pallas_call | solution.py:79
  62.9 2.9 %shard_map.92 = (bf16[1024,128]{1,0:T(8,128)(2,1)}, bf16[128,128]{1,0:T(8,128)(2,1)}) custom-call(bf16[1536,128]{1,0:T(8,128)(2,1)S(1)} %bitcast.46, s32[1024,128]{1,0:T(8,128)} %get-tuple-element.53.placed_ref, bf16[4,32,1024]{2,1,0:T(8,128)(2,1)} %bitcast.50, f32[128,128]{1,0:T(8,128)} %get-tuple-element.60.proj_ref), custom_call_target="tpu_custom_call" | custom-call | flops 603979776 | bytes 2000000 | tf_op jit(solution)/shard_map/pallas_call | solution.py:88
  65.7 2.7 %collective-permute-start.8 = (bf16[128,128]{1,0:T(8,128)(2,1)}, bf16[128,128]{1,0:T(8,128)(2,1)S(1)}, u32[]{:S(2)}, u32[]{:S(2)}) collective-permute-start(bf16[128,128]{1,0:T(8,128)(2,1)} %get-tuple-element.62.rest_0_), channel_id=1, source_target_pairs={{0,24},{4,28},{8,16},{12,20},{16,8},{20,12},{24,0},{28,4},{1,25},{... | collective-permute-start | bytes 98312 | tf_op jit(solution)/shard_map/ppermute | solution.py:514
  68.5 0.6 collective-permute-start.6
  69.4 0.5 collective-permute-done.3.rest_1_
  69.9 2.2 %collective-permute-start.9 = (bf16[128,128]{1,0:T(8,128)(2,1)S(1)}, bf16[128,128]{1,0:T(8,128)(2,1)S(1)}, u32[]{:S(2)}, u32[]{:S(2)}) collective-permute-start(bf16[128,128]{1,0:T(8,128)(2,1)S(1)} %collective-permute-done.3.rest_1_), channel_id=1, source_target_pairs={{0,24},{4,28},{8,16},{12,20},{16,8},{20,12},{24,0},{28,4},{1,25},{... | collective-permute-start | bytes 98312 | tf_op jit(solution)/shard_map/ppermute | solution.py:514
  72.0 0.6 collective-permute-start.7
  72.6 0.8 collective-permute-start.5
  73.4 3.4 %shard_map.93 = (f32[1536,128]{1,0:T(8,128)S(1)}, bf16[1536,128]{1,0:T(8,128)(2,1)S(1)}) custom-call(bf16[1024,128]{1,0:T(8,128)(2,1)} %get-tuple-element.61.margin_ref, s32[1,1024]{1,0:T(1,128)} %copy-done, bf16[4,1024,1024]{2,1,0:T(8,128)(2,1)} %matrix_ref.26, f32[4,1024,128]{2,1,0:T(8,128)} %get-tuple-element.58.part_ref, bf16[4,32,1024]{2,1,0:T(8,128)(2,1)} %bitcast.51), custom_call_target="tpu_custom_call" | custom-call | flops 1207959552 | bytes 3000000 | tf_op jit(solution)/shard_map/pallas_call | solution.py:88
  76.8 2.8 %shard_map.94 = (f32[128,128]{1,0:T(8,128)}, bf16[1536,128]{1,0:T(8,128)(2,1)}) custom-call(s32[2]{0:T(128)S(1)} %pad_add_fusion.here_ref, bf16[128,128]{1,0:T(8,128)(2,1)S(1)} %copy-done.2, bf16[128,128]{1,0:T(8,128)(2,1)S(1)} %collective-permute-done.3.rest_1_, bf16[128,128]{1,0:T(8,128)(2,1)S(1)} %collective-permute-done.4.rest_2_, ...), custom_call_target="tpu_custom_call" | custom-call | flops 301989888 | bytes 3000000 | tf_op jit(solution)/shard_map/pallas_call | solution.py:88
  79.7 3.5 %all-to-all-start.4 = ((bf16[8,192,128]{2,1,0:T(8,128)(2,1)}), bf16[8,192,128]{2,1,0:T(8,128)(2,1)S(1)}, u32[]{:S(2)}, u32[]{:S(2)}) async-start(bf16[8,192,128]{2,1,0:T(8,128)(2,1)} %bitcast.63), calls=%async_computation.4 | async-start | bytes 786432 | tf_op jit(solution)/shard_map/all_to_all | solution.py:382
  83.2 7.2 %shard_map.95 = (f32[3072,128]{1,0:T(8,128)}, f32[1536,128]{1,0:T(8,128)S(1)}) custom-call(f32[4,1024,128]{2,1,0:T(8,128)} %get-tuple-element.58.part_ref, bf16[4,1024,1024]{2,1,0:T(8,128)(2,1)} %matrix_ref.26, bf16[1024,128]{1,0:T(8,128)(2,1)} %get-tuple-element.61.margin_ref, f32[3072,128]{1,0:T(8,128)} %base_ref.5, ...), custom_call_target="tpu_custom_call" | custom-call | flops 2415919104 | bytes 8000000 | tf_op jit(solution)/shard_map/pallas_call | solution.py:79
  90.4 1.1 all-to-all-done.4
  91.5 2.1 %shard_map.97 = bf16[1536,128]{1,0:T(8,128)(2,1)} custom-call(f32[1536,128]{1,0:T(8,128)S(1)} %get-tuple-element.73.sent_ref, bf16[1536,128]{1,0:T(8,128)(2,1)S(1)} %bitcast.41, s32[1536,128]{1,0:T(8,128)S(1)} %get-tuple-element.55.column_ref, s32[1,1536]{1,0:T(1,128)S(1)} %sub.24.row_ref), custom_call_target="tpu_custom_call" | custom-call | flops 603979776 | bytes 3000000 | tf_op jit(solution)/shard_map/pallas_call | solution.py:88
  93.6 3.5 %all-to-all-start.5 = ((bf16[8,192,128]{2,1,0:T(8,128)(2,1)}), bf16[8,192,128]{2,1,0:T(8,128)(2,1)S(1)}, u32[]{:S(2)}, u32[]{:S(2)}) async-start(bf16[8,192,128]{2,1,0:T(8,128)(2,1)} %bitcast.58), calls=%async_computation.5 | async-start | bytes 786432 | tf_op jit(solution)/shard_map/all_to_all | solution.py:382
  97.0 7.8 %shard_map.96 = (f32[3072,128]{1,0:T(8,128)}, f32[4,1024,128]{2,1,0:T(8,128)}) custom-call(f32[3072,128]{1,0:T(8,128)} %get-tuple-element.70.base_ref, bf16[1536,128]{1,0:T(8,128)(2,1)S(1)} %bitcast.42, s32[1,1536]{1,0:T(1,128)S(1)} %sub.24.row_ref, bf16[4,1024,1024]{2,1,0:T(8,128)(2,1)} %matrix_ref.29), custom_call_target="tpu_custom_call" | custom-call | flops 2013265920 | bytes 14000000 | tf_op jit(solution)/shard_map/pallas_call | solution.py:79
  104.9 0.5 all-to-all-done.5
  105.3 4.0 %shard_map.98 = (bf16[1024,128]{1,0:T(8,128)(2,1)}, bf16[1536,128]{1,0:T(8,128)(2,1)}) custom-call(bf16[1536,128]{1,0:T(8,128)(2,1)S(1)} %bitcast.45, s32[1024,128]{1,0:T(8,128)} %get-tuple-element.53.placed_ref, s32[1,1024]{1,0:T(1,128)} %copy-done, bf16[4,1024,1024]{2,1,0:T(8,128)(2,1)} %matrix_ref.29, f32[4,1024,128]{2,1,0:T(8,128)} %get-tuple-element.72.part_ref), custom_call_target="tpu_custom_call" | custom-call | flops 1207959552 | bytes 3000000 | tf_op jit(solution)/shard_map/pallas_call | solution.py:88
  109.3 3.7 %all-to-all-start.6 = ((bf16[8,192,128]{2,1,0:T(8,128)(2,1)}), bf16[8,192,128]{2,1,0:T(8,128)(2,1)S(1)}, u32[]{:S(2)}, u32[]{:S(2)}) async-start(bf16[8,192,128]{2,1,0:T(8,128)(2,1)} %bitcast.66), calls=%async_computation.6 | async-start | bytes 786432 | tf_op jit(solution)/shard_map/all_to_all | solution.py:382
  113.0 6.9 %shard_map.99 = (f32[3072,128]{1,0:T(8,128)}, f32[1536,128]{1,0:T(8,128)S(1)}) custom-call(f32[4,1024,128]{2,1,0:T(8,128)} %get-tuple-element.72.part_ref, bf16[4,1024,1024]{2,1,0:T(8,128)(2,1)} %matrix_ref.29, bf16[1024,128]{1,0:T(8,128)(2,1)} %get-tuple-element.74.margin_ref, f32[3072,128]{1,0:T(8,128)} %base_ref.7, ...), custom_call_target="tpu_custom_call" | custom-call | flops 2415919104 | bytes 8000000 | tf_op jit(solution)/shard_map/pallas_call | solution.py:79
  119.9 1.5 all-to-all-done.6
  121.4 2.1 %shard_map.101 = bf16[1536,128]{1,0:T(8,128)(2,1)} custom-call(f32[1536,128]{1,0:T(8,128)S(1)} %get-tuple-element.78.sent_ref, bf16[1536,128]{1,0:T(8,128)(2,1)S(1)} %bitcast.37, s32[1536,128]{1,0:T(8,128)S(1)} %get-tuple-element.55.column_ref, s32[1,1536]{1,0:T(1,128)S(1)} %sub.24.row_ref), custom_call_target="tpu_custom_call" | custom-call | flops 603979776 | bytes 3000000 | tf_op jit(solution)/shard_map/pallas_call | solution.py:88
  123.5 3.7 %all-to-all-start.7 = ((bf16[8,192,128]{2,1,0:T(8,128)(2,1)}), bf16[8,192,128]{2,1,0:T(8,128)(2,1)S(1)}, u32[]{:S(2)}, u32[]{:S(2)}) async-start(bf16[8,192,128]{2,1,0:T(8,128)(2,1)} %bitcast.59), calls=%async_computation.7 | async-start | bytes 786432 | tf_op jit(solution)/shard_map/all_to_all | solution.py:382
  127.2 8.3 %shard_map.100 = (f32[4,1024,128]{2,1,0:T(8,128)}, f32[128,128]{1,0:T(8,128)}) custom-call(f32[3072,128]{1,0:T(8,128)} %get-tuple-element.75.base_ref, bf16[1536,128]{1,0:T(8,128)(2,1)S(1)} %bitcast.38, s32[1,1536]{1,0:T(1,128)S(1)} %sub.24.row_ref, bf16[4,1024,1024]{2,1,0:T(8,128)(2,1)} %matrix_ref.26, bf16[4,32,1024]{2,1,0:T(8,128)(2,1)} %bitcast.53), custom_call_target="tpu_custom_call" | custom-call | flops 2013265920 | bytes 14000000 | tf_op jit(solution)/shard_map/pallas_call | solution.py:79
  135.5 2.9 %shard_map.102 = (bf16[1024,128]{1,0:T(8,128)(2,1)}, bf16[128,128]{1,0:T(8,128)(2,1)}) custom-call(bf16[1536,128]{1,0:T(8,128)(2,1)S(1)} %bitcast.48, s32[1024,128]{1,0:T(8,128)} %get-tuple-element.53.placed_ref, bf16[4,32,1024]{2,1,0:T(8,128)(2,1)} %bitcast.54, f32[128,128]{1,0:T(8,128)} %get-tuple-element.79.proj_ref), custom_call_target="tpu_custom_call" | custom-call | flops 603979776 | bytes 2000000 | tf_op jit(solution)/shard_map/pallas_call | solution.py:88
  138.3 0.4 collective-permute-start.10
  138.8 2.6 %collective-permute-start.15 = (bf16[128,128]{1,0:T(8,128)(2,1)}, bf16[128,128]{1,0:T(8,128)(2,1)S(1)}, u32[]{:S(2)}, u32[]{:S(2)}) collective-permute-start(bf16[128,128]{1,0:T(8,128)(2,1)} %get-tuple-element.82.rest_0_), channel_id=1, source_target_pairs={{0,24},{4,28},{8,16},{12,20},{16,8},{20,12},{24,0},{28,4},{1,25},{... | collective-permute-start | bytes 98312 | tf_op jit(solution)/shard_map/ppermute | solution.py:514
  141.4 0.5 collective-permute-start.13
  142.3 2.6 %collective-permute-start.16 = (bf16[128,128]{1,0:T(8,128)(2,1)S(1)}, bf16[128,128]{1,0:T(8,128)(2,1)S(1)}, u32[]{:S(2)}, u32[]{:S(2)}) collective-permute-start(bf16[128,128]{1,0:T(8,128)(2,1)S(1)} %collective-permute-done.10.rest_1_), channel_id=1, source_target_pairs={{0,24},{4,28},{8,16},{12,20},{16,8},{20,12},{24,0},{28,4},{1,25},{... | collective-permute-start | bytes 98312 | tf_op jit(solution)/shard_map/ppermute | solution.py:514
  144.9 0.5 collective-permute-start.14
  145.8 3.4 %shard_map.103 = (f32[1536,128]{1,0:T(8,128)S(1)}, bf16[1536,128]{1,0:T(8,128)(2,1)S(1)}) custom-call(bf16[1024,128]{1,0:T(8,128)(2,1)} %get-tuple-element.80.margin_ref, s32[1,1024]{1,0:T(1,128)} %copy-done, bf16[4,1024,1024]{2,1,0:T(8,128)(2,1)} %matrix_ref.26, f32[4,1024,128]{2,1,0:T(8,128)} %get-tuple-element.77.part_ref, bf16[4,32,1024]{2,1,0:T(8,128)(2,1)} %bitcast.55), custom_call_target="tpu_custom_call" | custom-call | flops 1207959552 | bytes 3000000 | tf_op jit(solution)/shard_map/pallas_call | solution.py:88
  149.4 2.8 %shard_map.104 = (f32[128,128]{1,0:T(8,128)}, bf16[1536,128]{1,0:T(8,128)(2,1)}) custom-call(s32[2]{0:T(128)S(1)} %pad_add_fusion.here_ref, bf16[128,128]{1,0:T(8,128)(2,1)S(1)} %copy-done.1, bf16[128,128]{1,0:T(8,128)(2,1)S(1)} %collective-permute-done.10.rest_1_, bf16[128,128]{1,0:T(8,128)(2,1)S(1)} %collective-permute-done.11.rest_2_, ...), custom_call_target="tpu_custom_call" | custom-call | flops 301989888 | bytes 3000000 | tf_op jit(solution)/shard_map/pallas_call | solution.py:88
  152.2 3.8 %all-to-all-start.8 = ((bf16[8,192,128]{2,1,0:T(8,128)(2,1)}), bf16[8,192,128]{2,1,0:T(8,128)(2,1)S(1)}, u32[]{:S(2)}, u32[]{:S(2)}) async-start(bf16[8,192,128]{2,1,0:T(8,128)(2,1)} %bitcast.62), calls=%async_computation.8 | async-start | bytes 786432 | tf_op jit(solution)/shard_map/all_to_all | solution.py:382
  156.0 7.2 %shard_map.105 = (f32[3072,128]{1,0:T(8,128)}, f32[1536,128]{1,0:T(8,128)S(1)}) custom-call(f32[4,1024,128]{2,1,0:T(8,128)} %get-tuple-element.77.part_ref, bf16[4,1024,1024]{2,1,0:T(8,128)(2,1)} %matrix_ref.26, bf16[1024,128]{1,0:T(8,128)(2,1)} %get-tuple-element.80.margin_ref, f32[3072,128]{1,0:T(8,128)} %get-tuple-element.81.base_ref, ...), custom_call_target="tpu_custom_call" | custom-call | flops 2415919104 | bytes 8000000 | tf_op jit(solution)/shard_map/pallas_call | solution.py:79
  163.2 1.2 all-to-all-done.8
  164.3 2.1 %shard_map.107 = bf16[1536,128]{1,0:T(8,128)(2,1)} custom-call(f32[1536,128]{1,0:T(8,128)S(1)} %get-tuple-element.90.sent_ref, bf16[1536,128]{1,0:T(8,128)(2,1)S(1)} %bitcast.39, s32[1536,128]{1,0:T(8,128)S(1)} %get-tuple-element.55.column_ref, s32[1,1536]{1,0:T(1,128)S(1)} %sub.24.row_ref), custom_call_target="tpu_custom_call" | custom-call | flops 603979776 | bytes 3000000 | tf_op jit(solution)/shard_map/pallas_call | solution.py:88
  166.4 3.5 %all-to-all-start.9 = ((bf16[8,192,128]{2,1,0:T(8,128)(2,1)}), bf16[8,192,128]{2,1,0:T(8,128)(2,1)S(1)}, u32[]{:S(2)}, u32[]{:S(2)}) async-start(bf16[8,192,128]{2,1,0:T(8,128)(2,1)} %bitcast.60), calls=%async_computation.9 | async-start | bytes 786432 | tf_op jit(solution)/shard_map/all_to_all | solution.py:382
  169.9 7.8 %shard_map.106 = (f32[3072,128]{1,0:T(8,128)}, f32[4,1024,128]{2,1,0:T(8,128)}) custom-call(f32[3072,128]{1,0:T(8,128)} %get-tuple-element.86.base_ref, bf16[1536,128]{1,0:T(8,128)(2,1)S(1)} %bitcast.40, s32[1,1536]{1,0:T(1,128)S(1)} %sub.24.row_ref, bf16[4,1024,1024]{2,1,0:T(8,128)(2,1)} %matrix_ref.29), custom_call_target="tpu_custom_call" | custom-call | flops 2013265920 | bytes 14000000 | tf_op jit(solution)/shard_map/pallas_call | solution.py:79
  177.7 0.4 all-to-all-done.9
  178.2 4.0 %shard_map.108 = (bf16[1024,128]{1,0:T(8,128)(2,1)}, bf16[1536,128]{1,0:T(8,128)(2,1)}) custom-call(bf16[1536,128]{1,0:T(8,128)(2,1)S(1)} %bitcast.44, s32[1024,128]{1,0:T(8,128)} %get-tuple-element.53.placed_ref, s32[1,1024]{1,0:T(1,128)} %copy-done, bf16[4,1024,1024]{2,1,0:T(8,128)(2,1)} %matrix_ref.29, f32[4,1024,128]{2,1,0:T(8,128)} %get-tuple-element.89.part_ref), custom_call_target="tpu_custom_call" | custom-call | flops 1207959552 | bytes 3000000 | tf_op jit(solution)/shard_map/pallas_call | solution.py:88
  182.2 3.7 %all-to-all-start.10 = ((bf16[8,192,128]{2,1,0:T(8,128)(2,1)}), bf16[8,192,128]{2,1,0:T(8,128)(2,1)S(1)}, u32[]{:S(2)}, u32[]{:S(2)}) async-start(bf16[8,192,128]{2,1,0:T(8,128)(2,1)} %bitcast.64), calls=%async_computation.10 | async-start | bytes 786432 | tf_op jit(solution)/shard_map/all_to_all | solution.py:382
  185.9 6.8 %shard_map.109 = (f32[3072,128]{1,0:T(8,128)S(1)}, f32[1536,128]{1,0:T(8,128)}) custom-call(f32[4,1024,128]{2,1,0:T(8,128)} %get-tuple-element.89.part_ref, bf16[4,1024,1024]{2,1,0:T(8,128)(2,1)} %matrix_ref.29, bf16[1024,128]{1,0:T(8,128)(2,1)} %get-tuple-element.91.margin_ref, f32[3072,128]{1,0:T(8,128)} %base_ref.7, ...), custom_call_target="tpu_custom_call" | custom-call | flops 2415919104 | bytes 8000000 | tf_op jit(solution)/shard_map/pallas_call | solution.py:79
  192.8 1.5 all-to-all-done.10
  194.2 3.5 %shard_map.110 = f32[3072,128]{1,0:T(8,128)} custom-call(f32[3072,128]{1,0:T(8,128)S(1)} %get-tuple-element.92.base_ref, bf16[1536,128]{1,0:T(8,128)(2,1)S(1)} %bitcast.47, s32[1,1536]{1,0:T(1,128)S(1)} %sub.24.row_ref), custom_call_target="tpu_custom_call" | custom-call | flops 1207959552 | bytes 4000000 | tf_op jit(solution)/shard_map/pallas_call | solution.py:88
  (48 shorter events, 1.4 us)
Async XLA Ops:
  3.4 9.9 %all-to-all-start = ((s32[8,1,192]{2,1,0:T(1,128)}), s32[8,1,192]{2,1,0:T(1,128)S(1)}, u32[]{:S(2)}, u32[]{:S(2)}) async-start(s32[8,1,192]{2,1,0:T(1,128)} %copy.9), calls=%async_computation | async-start | bytes 16384 | tf_op jit(solution)/shard_map/all_to_all | solution.py:385
  10.0 8.1 %copy-start = (s32[1,1024]{1,0:T(1,128)}, s32[1,1024]{1,0:T(1,128)S(1)}, u32[]{:S(2)}) copy-start(s32[1,1024]{1,0:T(1,128)S(1)} %fusion.6.place_ref) | copy-start | bytes 12292
  11.0 14.4 %copy-start.3 = (bf16[128,256]{1,0:T(8,128)(2,1)}, bf16[128,256]{1,0:T(8,128)(2,1)S(1)}, u32[]{:S(2)}) copy-start(bf16[128,256]{1,0:T(8,128)(2,1)S(1)} %convert_element_type.27.rest_8_) | copy-start | bytes 196612
  18.2 14.1 %all-to-all-start.1 = ((bf16[8,192,128]{2,1,0:T(8,128)(2,1)}), bf16[8,192,128]{2,1,0:T(8,128)(2,1)S(1)}, u32[]{:S(2)}, u32[]{:S(2)}) async-start(bf16[8,192,128]{2,1,0:T(8,128)(2,1)} %bitcast.61), calls=%async_computation.1 | async-start | bytes 786432 | tf_op jit(solution)/shard_map/all_to_all | solution.py:382
  21.7 10.5 %collective-permute-start.2 = (bf16[128,256]{1,0:T(8,128)(2,1)S(1)}, bf16[128,256]{1,0:T(8,128)(2,1)S(1)}, u32[]{:S(2)}, u32[]{:S(2)}) collective-permute-start(bf16[128,256]{1,0:T(8,128)(2,1)S(1)} %convert_element_type.27.rest_8_), channel_id=1, source_target_pairs={{0,3},{1,2},{2,1},{3,0},{4,7},{5,6},{6,5},{7,4},{8,11},{9,10},{10,... | collective-permute-start | bytes 196616 | tf_op jit(solution)/shard_map/ppermute | solution.py:414
  25.3 6.9 %collective-permute-start.1 = (bf16[128,256]{1,0:T(8,128)(2,1)S(1)}, bf16[128,256]{1,0:T(8,128)(2,1)S(1)}, u32[]{:S(2)}, u32[]{:S(2)}) collective-permute-start(bf16[128,256]{1,0:T(8,128)(2,1)S(1)} %convert_element_type.27.rest_8_), channel_id=1, source_target_pairs={{0,2},{1,3},{2,0},{3,1},{4,6},{5,7},{6,4},{7,5},{8,10},{9,11},{10,... | collective-permute-start | bytes 196616 | tf_op jit(solution)/shard_map/ppermute | solution.py:414
  25.3 6.9 %collective-permute-start = (bf16[128,256]{1,0:T(8,128)(2,1)S(1)}, bf16[128,256]{1,0:T(8,128)(2,1)S(1)}, u32[]{:S(2)}, u32[]{:S(2)}) collective-permute-start(bf16[128,256]{1,0:T(8,128)(2,1)S(1)} %convert_element_type.27.rest_8_), channel_id=1, source_target_pairs={{0,1},{1,0},{2,3},{3,2},{4,5},{5,4},{6,7},{7,6},{8,9},{9,8},{10,11... | collective-permute-start | bytes 196616 | tf_op jit(solution)/shard_map/ppermute | solution.py:414
  32.2 4.1 %copy-start.4 = (bf16[128,256]{1,0:T(8,128)(2,1)}, bf16[128,256]{1,0:T(8,128)(2,1)S(1)}, u32[]{:S(2)}) copy-start(bf16[128,256]{1,0:T(8,128)(2,1)S(1)} %collective-permute-done.2.rest_11_) | copy-start | bytes 196612
  32.2 4.1 %copy-start.5 = (bf16[128,256]{1,0:T(8,128)(2,1)}, bf16[128,256]{1,0:T(8,128)(2,1)S(1)}, u32[]{:S(2)}) copy-start(bf16[128,256]{1,0:T(8,128)(2,1)S(1)} %collective-permute-done.1.rest_10_) | copy-start | bytes 196612
  32.2 4.1 %copy-start.6 = (bf16[128,256]{1,0:T(8,128)(2,1)}, bf16[128,256]{1,0:T(8,128)(2,1)S(1)}, u32[]{:S(2)}) copy-start(bf16[128,256]{1,0:T(8,128)(2,1)S(1)} %collective-permute-done.rest_9_) | copy-start | bytes 196612
  36.4 12.4 %all-to-all-start.2 = ((bf16[8,192,128]{2,1,0:T(8,128)(2,1)}), bf16[8,192,128]{2,1,0:T(8,128)(2,1)S(1)}, u32[]{:S(2)}, u32[]{:S(2)}) async-start(bf16[8,192,128]{2,1,0:T(8,128)(2,1)} %bitcast.65), calls=%async_computation.2 | async-start | bytes 786432 | tf_op jit(solution)/shard_map/all_to_all | solution.py:382
  50.9 11.9 %all-to-all-start.3 = ((bf16[8,192,128]{2,1,0:T(8,128)(2,1)}), bf16[8,192,128]{2,1,0:T(8,128)(2,1)S(1)}, u32[]{:S(2)}, u32[]{:S(2)}) async-start(bf16[8,192,128]{2,1,0:T(8,128)(2,1)} %bitcast.57), calls=%async_computation.3 | async-start | bytes 786432 | tf_op jit(solution)/shard_map/all_to_all | solution.py:382
  65.7 6.8 %collective-permute-start.8 = (bf16[128,128]{1,0:T(8,128)(2,1)}, bf16[128,128]{1,0:T(8,128)(2,1)S(1)}, u32[]{:S(2)}, u32[]{:S(2)}) collective-permute-start(bf16[128,128]{1,0:T(8,128)(2,1)} %get-tuple-element.62.rest_0_), channel_id=1, source_target_pairs={{0,24},{4,28},{8,16},{12,20},{16,8},{20,12},{24,0},{28,4},{1,25},{... | collective-permute-start | bytes 98312 | tf_op jit(solution)/shard_map/ppermute | solution.py:514
  68.4 1.4 collective-permute-start.3
  68.5 8.3 %collective-permute-start.6 = (bf16[128,128]{1,0:T(8,128)(2,1)}, bf16[128,128]{1,0:T(8,128)(2,1)S(1)}, u32[]{:S(2)}, u32[]{:S(2)}) collective-permute-start(bf16[128,128]{1,0:T(8,128)(2,1)} %get-tuple-element.62.rest_0_), channel_id=1, source_target_pairs={{0,16},{4,20},{8,24},{12,28},{16,0},{20,4},{24,8},{28,12},{1,17},{... | collective-permute-start | bytes 98312 | tf_op jit(solution)/shard_map/ppermute | solution.py:514
  69.1 7.7 %collective-permute-start.4 = (bf16[128,128]{1,0:T(8,128)(2,1)}, bf16[128,128]{1,0:T(8,128)(2,1)S(1)}, u32[]{:S(2)}, u32[]{:S(2)}) collective-permute-start(bf16[128,128]{1,0:T(8,128)(2,1)} %get-tuple-element.62.rest_0_), channel_id=1, source_target_pairs={{0,8},{4,12},{8,0},{12,4},{16,24},{20,28},{24,16},{28,20},{1,9},{5... | collective-permute-start | bytes 98312 | tf_op jit(solution)/shard_map/ppermute | solution.py:514
  69.9 6.9 %collective-permute-start.9 = (bf16[128,128]{1,0:T(8,128)(2,1)S(1)}, bf16[128,128]{1,0:T(8,128)(2,1)S(1)}, u32[]{:S(2)}, u32[]{:S(2)}) collective-permute-start(bf16[128,128]{1,0:T(8,128)(2,1)S(1)} %collective-permute-done.3.rest_1_), channel_id=1, source_target_pairs={{0,24},{4,28},{8,16},{12,20},{16,8},{20,12},{24,0},{28,4},{1,25},{... | collective-permute-start | bytes 98312 | tf_op jit(solution)/shard_map/ppermute | solution.py:514
  72.0 4.8 %collective-permute-start.7 = (bf16[128,128]{1,0:T(8,128)(2,1)S(1)}, bf16[128,128]{1,0:T(8,128)(2,1)S(1)}, u32[]{:S(2)}, u32[]{:S(2)}) collective-permute-start(bf16[128,128]{1,0:T(8,128)(2,1)S(1)} %collective-permute-done.3.rest_1_), channel_id=1, source_target_pairs={{0,16},{4,20},{8,24},{12,28},{16,0},{20,4},{24,8},{28,12},{1,17},{... | collective-permute-start | bytes 98312 | tf_op jit(solution)/shard_map/ppermute | solution.py:514
  72.6 4.2 %collective-permute-start.5 = (bf16[128,128]{1,0:T(8,128)(2,1)S(1)}, bf16[128,128]{1,0:T(8,128)(2,1)S(1)}, u32[]{:S(2)}, u32[]{:S(2)}) collective-permute-start(bf16[128,128]{1,0:T(8,128)(2,1)S(1)} %collective-permute-done.3.rest_1_), channel_id=1, source_target_pairs={{0,8},{4,12},{8,0},{12,4},{16,24},{20,28},{24,16},{28,20},{1,9},{5... | collective-permute-start | bytes 98312 | tf_op jit(solution)/shard_map/ppermute | solution.py:514
  73.3 3.5 %copy-start.2 = (bf16[128,128]{1,0:T(8,128)(2,1)S(1)}, bf16[128,128]{1,0:T(8,128)(2,1)}, u32[]{:S(2)}) copy-start(bf16[128,128]{1,0:T(8,128)(2,1)} %get-tuple-element.62.rest_0_) | copy-start | bytes 98308
  79.7 11.8 %all-to-all-start.4 = ((bf16[8,192,128]{2,1,0:T(8,128)(2,1)}), bf16[8,192,128]{2,1,0:T(8,128)(2,1)S(1)}, u32[]{:S(2)}, u32[]{:S(2)}) async-start(bf16[8,192,128]{2,1,0:T(8,128)(2,1)} %bitcast.63), calls=%async_computation.4 | async-start | bytes 786432 | tf_op jit(solution)/shard_map/all_to_all | solution.py:382
  93.6 11.7 %all-to-all-start.5 = ((bf16[8,192,128]{2,1,0:T(8,128)(2,1)}), bf16[8,192,128]{2,1,0:T(8,128)(2,1)S(1)}, u32[]{:S(2)}, u32[]{:S(2)}) async-start(bf16[8,192,128]{2,1,0:T(8,128)(2,1)} %bitcast.58), calls=%async_computation.5 | async-start | bytes 786432 | tf_op jit(solution)/shard_map/all_to_all | solution.py:382
  109.3 12.0 %all-to-all-start.6 = ((bf16[8,192,128]{2,1,0:T(8,128)(2,1)}), bf16[8,192,128]{2,1,0:T(8,128)(2,1)S(1)}, u32[]{:S(2)}, u32[]{:S(2)}) async-start(bf16[8,192,128]{2,1,0:T(8,128)(2,1)} %bitcast.66), calls=%async_computation.6 | async-start | bytes 786432 | tf_op jit(solution)/shard_map/all_to_all | solution.py:382
  123.5 12.0 %all-to-all-start.7 = ((bf16[8,192,128]{2,1,0:T(8,128)(2,1)}), bf16[8,192,128]{2,1,0:T(8,128)(2,1)S(1)}, u32[]{:S(2)}, u32[]{:S(2)}) async-start(bf16[8,192,128]{2,1,0:T(8,128)(2,1)} %bitcast.59), calls=%async_computation.7 | async-start | bytes 786432 | tf_op jit(solution)/shard_map/all_to_all | solution.py:382
  138.3 3.9 %collective-permute-start.10 = (bf16[128,128]{1,0:T(8,128)(2,1)}, bf16[128,128]{1,0:T(8,128)(2,1)S(1)}, u32[]{:S(2)}, u32[]{:S(2)}) collective-permute-start(bf16[128,128]{1,0:T(8,128)(2,1)} %get-tuple-element.82.rest_0_), channel_id=1, source_target_pairs={{0,4},{4,0},{8,12},{12,8},{16,20},{20,16},{24,28},{28,24},{1,5},{5... | collective-permute-start | bytes 98312 | tf_op jit(solution)/shard_map/ppermute | solution.py:510
  138.8 6.7 %collective-permute-start.15 = (bf16[128,128]{1,0:T(8,128)(2,1)}, bf16[128,128]{1,0:T(8,128)(2,1)S(1)}, u32[]{:S(2)}, u32[]{:S(2)}) collective-permute-start(bf16[128,128]{1,0:T(8,128)(2,1)} %get-tuple-element.82.rest_0_), channel_id=1, source_target_pairs={{0,24},{4,28},{8,16},{12,20},{16,8},{20,12},{24,0},{28,4},{1,25},{... | collective-permute-start | bytes 98312 | tf_op jit(solution)/shard_map/ppermute | solution.py:514
  141.4 7.8 %collective-permute-start.13 = (bf16[128,128]{1,0:T(8,128)(2,1)}, bf16[128,128]{1,0:T(8,128)(2,1)S(1)}, u32[]{:S(2)}, u32[]{:S(2)}) collective-permute-start(bf16[128,128]{1,0:T(8,128)(2,1)} %get-tuple-element.82.rest_0_), channel_id=1, source_target_pairs={{0,16},{4,20},{8,24},{12,28},{16,0},{20,4},{24,8},{28,12},{1,17},{... | collective-permute-start | bytes 98312 | tf_op jit(solution)/shard_map/ppermute | solution.py:514
  141.9 7.3 %collective-permute-start.11 = (bf16[128,128]{1,0:T(8,128)(2,1)}, bf16[128,128]{1,0:T(8,128)(2,1)S(1)}, u32[]{:S(2)}, u32[]{:S(2)}) collective-permute-start(bf16[128,128]{1,0:T(8,128)(2,1)} %get-tuple-element.82.rest_0_), channel_id=1, source_target_pairs={{0,8},{4,12},{8,0},{12,4},{16,24},{20,28},{24,16},{28,20},{1,9},{5... | collective-permute-start | bytes 98312 | tf_op jit(solution)/shard_map/ppermute | solution.py:514
  142.3 6.9 %collective-permute-start.16 = (bf16[128,128]{1,0:T(8,128)(2,1)S(1)}, bf16[128,128]{1,0:T(8,128)(2,1)S(1)}, u32[]{:S(2)}, u32[]{:S(2)}) collective-permute-start(bf16[128,128]{1,0:T(8,128)(2,1)S(1)} %collective-permute-done.10.rest_1_), channel_id=1, source_target_pairs={{0,24},{4,28},{8,16},{12,20},{16,8},{20,12},{24,0},{28,4},{1,25},{... | collective-permute-start | bytes 98312 | tf_op jit(solution)/shard_map/ppermute | solution.py:514
  144.9 4.3 %collective-permute-start.14 = (bf16[128,128]{1,0:T(8,128)(2,1)S(1)}, bf16[128,128]{1,0:T(8,128)(2,1)S(1)}, u32[]{:S(2)}, u32[]{:S(2)}) collective-permute-start(bf16[128,128]{1,0:T(8,128)(2,1)S(1)} %collective-permute-done.10.rest_1_), channel_id=1, source_target_pairs={{0,16},{4,20},{8,24},{12,28},{16,0},{20,4},{24,8},{28,12},{1,17},{... | collective-permute-start | bytes 98312 | tf_op jit(solution)/shard_map/ppermute | solution.py:514
  145.4 3.9 %collective-permute-start.12 = (bf16[128,128]{1,0:T(8,128)(2,1)S(1)}, bf16[128,128]{1,0:T(8,128)(2,1)S(1)}, u32[]{:S(2)}, u32[]{:S(2)}) collective-permute-start(bf16[128,128]{1,0:T(8,128)(2,1)S(1)} %collective-permute-done.10.rest_1_), channel_id=1, source_target_pairs={{0,8},{4,12},{8,0},{12,4},{16,24},{20,28},{24,16},{28,20},{1,9},{5... | collective-permute-start | bytes 98312 | tf_op jit(solution)/shard_map/ppermute | solution.py:514
  145.8 3.6 %copy-start.1 = (bf16[128,128]{1,0:T(8,128)(2,1)S(1)}, bf16[128,128]{1,0:T(8,128)(2,1)}, u32[]{:S(2)}) copy-start(bf16[128,128]{1,0:T(8,128)(2,1)} %get-tuple-element.82.rest_0_) | copy-start | bytes 98308
  152.2 12.1 %all-to-all-start.8 = ((bf16[8,192,128]{2,1,0:T(8,128)(2,1)}), bf16[8,192,128]{2,1,0:T(8,128)(2,1)S(1)}, u32[]{:S(2)}, u32[]{:S(2)}) async-start(bf16[8,192,128]{2,1,0:T(8,128)(2,1)} %bitcast.62), calls=%async_computation.8 | async-start | bytes 786432 | tf_op jit(solution)/shard_map/all_to_all | solution.py:382
  166.4 11.7 %all-to-all-start.9 = ((bf16[8,192,128]{2,1,0:T(8,128)(2,1)}), bf16[8,192,128]{2,1,0:T(8,128)(2,1)S(1)}, u32[]{:S(2)}, u32[]{:S(2)}) async-start(bf16[8,192,128]{2,1,0:T(8,128)(2,1)} %bitcast.60), calls=%async_computation.9 | async-start | bytes 786432 | tf_op jit(solution)/shard_map/all_to_all | solution.py:382
  182.2 12.0 %all-to-all-start.10 = ((bf16[8,192,128]{2,1,0:T(8,128)(2,1)}), bf16[8,192,128]{2,1,0:T(8,128)(2,1)S(1)}, u32[]{:S(2)}, u32[]{:S(2)}) async-start(bf16[8,192,128]{2,1,0:T(8,128)(2,1)} %bitcast.64), calls=%async_computation.10 | async-start | bytes 786432 | tf_op jit(solution)/shard_map/all_to_all | solution.py:382

commit v6 on v4

--- a/solution.py
+++ b/solution.py
@@ -228,7 +228,7 @@
     finish(stores + pack(place, outer, packed, out_ref, sems, 5))
 
 
-def project_body(in_ref, placed_ref, modes_ref, proj_ref, margin_ref, out_ref, placed, modes, proj, margin, made, sems):
+def project_body(in_ref, placed_ref, modes_ref, proj_ref, margin_ref, out_ref, placed, modes, proj, margin, sems):
     subs, count, margins = modes.shape
     core = modes_ref.shape[2] - margins
     loads = begin(sems, 0, [(placed_ref, placed), (modes_ref.at[:, :, core:], modes), (proj_ref, proj)])
@@ -238,8 +238,8 @@
     finish(loads[1:])
     for s in range(subs):
         at = pl.ds(s * count, count)
-        made[at, :] = (proj[at, :] + dot(modes[s], margin[pl.ds(s * margins, margins), :])).astype(bf16)
-    finish(stores + begin(sems, 4, [(made, out_ref)]))
+        out_ref[at, :] = (proj[at, :] + dot(modes[s], margin[pl.ds(s * margins, margins), :])).astype(bf16)
+    finish(stores)
 
 
 def split(x):
@@ -500,12 +500,9 @@
         came = trade(going)
         part, proj = settle(-1.0, base, back, local_inverse, True)
         margin, projection = flat_call(
-            project_body, (0,), [margin_shape, jax.ShapeDtypeStruct((coarse_rows, cols), bf16)], (),
-            [
-                column_scratch, modes_scratch, pltpu.VMEM((coarse_rows, cols), f32), margin_scratch,
-                pltpu.VMEM((coarse_rows, cols), bf16),
-            ],
-            5, slot_flops // 2, 2e6,
+            project_body, (0,), [margin_shape, jax.ShapeDtypeStruct((coarse_rows, cols), bf16)], (1,),
+            [column_scratch, modes_scratch, pltpu.VMEM((coarse_rows, cols), f32), margin_scratch],
+            4, slot_flops // 2, 2e6,
         )(came, place_column, modes_turned, proj)
         partner = lax.ppermute(projection, "wide", [(i, i ^ 1) for i in range(owners)])
         pair = jnp.concatenate([projection, partner], axis=0)

time: 196 us -> 195 us (level)
  transfers between devices with their start and end apart: 22 -> 22, of which waited for: 12 -> 12; matrix products, arithmetic and copies ran while one was open for 2% -> 1% of each run, Pallas kernels for 41% -> 42%
where the time goes in v6:
time: 195 us; the launch traced here: 193 us
  Pallas kernels  120 us (62%)
  starting transfers between devices  53.3 us (27%)
  waiting for transfers between devices  12.9 us (7%)
  other arithmetic  3.27 us (2%)
    pallas_call x10, Pallas kernels, call(): run(*(placed(i, x, spec) for i, (x, spec) in enumerate(zip(args, in_specs...  73.3 us
    pallas_call x15, Pallas kernels, run(): pl.pallas_call(body, in_specs=[pl.BlockSpec(memory_space=p) for p in plac...  46.9 us
    all_to_all x11, starting transfers between devices, trade(): lax.all_to_all(blocks, 'wide', split_axis=0, concat_axis=0, tiled=True)  41.3 us
    all_to_all x11, waiting for transfers between devices, trade(): lax.all_to_all(blocks, 'wide', split_axis=0, concat_axis=0, tiled=True)  9.81 us
    ppermute x6, starting transfers between devices, shards(): lax.ppermute(pair, 'wide', [(i, i ^ k) for i in range(owners)])  6.98 us
    ppermute x3, starting transfers between devices, shards(): lax.ppermute(own, 'narrow', [(i, i ^ k) for i in range(side)])  4.45 us
  transfers between devices with their start and end apart: 22, of which 12 were waited for; matrix products, arithmetic and copies ran while one was open for 1% of the time, Pallas kernels for 42%

profile of v6, /device:TPU:0, one launch (start us, length us, event | category | flops | bytes accessed | tf_op | source)
XLA Modules:
  0.0 192.8 jit_solution(13416929008779700766)
XLA Ops:
  0.6 0.7 copy.9
  1.3 0.5 fusion.2
  1.8 0.8 select_reduce_fusion
  2.7 0.7 sub.24
  3.4 5.2 %all-to-all-start = ((s32[8,1,192]{2,1,0:T(1,128)}), s32[8,1,192]{2,1,0:T(1,128)S(1)}, u32[]{:S(2)}, u32[]{:S(2)}) async-start(s32[8,1,192]{2,1,0:T(1,128)} %sub.24), calls=%async_computation | async-start | bytes 16384 | tf_op jit(solution)/shard_map/all_to_all | solution.py:382
  8.5 0.7 fusion.9
  9.2 0.7 divide_bitcast_fusion
  10.0 0.9 convert_element_type.27.rest_4_
  10.9 2.3 %all-to-all-done = s32[8,1,192]{2,1,0:T(1,128)S(1)} async-done(((s32[8,1,192]{2,1,0:T(1,128)}), s32[8,1,192]{2,1,0:T(1,128)S(1)}, u32[]{:S(2)}, u32[]{:S(2)}) %all-to-all-start) | async-done | bytes 6176 | tf_op jit(solution)/shard_map/all_to_all | solution.py:382
  13.3 4.8 %shard_map.86 = (bf16[1536,128]{1,0:T(8,128)(2,1)}, s32[1536,128]{1,0:T(8,128)S(1)}, s32[1024,128]{1,0:T(8,128)}) custom-call(s32[1,1536]{1,0:T(1,128)S(1)} %broadcast_in_dim_reshape.3.row_ref, s32[1,1024]{1,0:T(1,128)S(1)} %fusion.6.place_ref, f32[3072,128]{1,0:T(8,128)} %base_ref.5), custom_call_target="tpu_custom_call" | custom-call | flops 1207959552 | bytes 4000000 | tf_op jit(solution)/shard_map/pallas_call | solution.py:88
  18.1 3.5 %all-to-all-start.1 = ((bf16[8,192,128]{2,1,0:T(8,128)(2,1)}), bf16[8,192,128]{2,1,0:T(8,128)(2,1)S(1)}, u32[]{:S(2)}, u32[]{:S(2)}) async-start(bf16[8,192,128]{2,1,0:T(8,128)(2,1)} %bitcast.60), calls=%async_computation.1 | async-start | bytes 786432 | tf_op jit(solution)/shard_map/all_to_all | solution.py:382
  21.6 3.7 %collective-permute-start.2 = (bf16[128,256]{1,0:T(8,128)(2,1)S(1)}, bf16[128,256]{1,0:T(8,128)(2,1)S(1)}, u32[]{:S(2)}, u32[]{:S(2)}) collective-permute-start(bf16[128,256]{1,0:T(8,128)(2,1)S(1)} %convert_element_type.27.rest_4_), channel_id=1, source_target_pairs={{0,3},{1,2},{2,1},{3,0},{4,7},{5,6},{6,5},{7,4},{8,11},{9,10},{10,... | collective-permute-start | bytes 196616 | tf_op jit(solution)/shard_map/ppermute | solution.py:414
  25.3 0.8 collective-permute-start
  26.1 6.1 %shard_map.87.part_ref = f32[4,1024,128]{2,1,0:T(8,128)} custom-call(f32[3072,128]{1,0:T(8,128)} %base_ref.5, bf16[4,1024,1024]{2,1,0:T(8,128)(2,1)} %matrix_ref.29), custom_call_target="tpu_custom_call" | custom-call | flops 805306368 | bytes 10000000 | tf_op jit(solution)/shard_map/pallas_call | solution.py:79
  32.2 4.1 %shard_map.88 = (bf16[1024,128]{1,0:T(8,128)(2,1)}, bf16[1536,128]{1,0:T(8,128)(2,1)}) custom-call(bf16[1536,128]{1,0:T(8,128)(2,1)S(1)} %bitcast.42, s32[1024,128]{1,0:T(8,128)} %get-tuple-element.53.placed_ref, s32[1,1024]{1,0:T(1,128)} %copy-done, bf16[4,1024,1024]{2,1,0:T(8,128)(2,1)} %matrix_ref.29, f32[4,1024,128]{2,1,0:T(8,128)} %shard_map.87.part_ref), custom_call_target="tpu_custom_call" | custom-call | flops 1207959552 | bytes 3000000 | tf_op jit(solution)/shard_map/pallas_call | solution.py:88
  36.3 4.1 %all-to-all-start.2 = ((bf16[8,192,128]{2,1,0:T(8,128)(2,1)}), bf16[8,192,128]{2,1,0:T(8,128)(2,1)S(1)}, u32[]{:S(2)}, u32[]{:S(2)}) async-start(bf16[8,192,128]{2,1,0:T(8,128)(2,1)} %bitcast.64), calls=%async_computation.2 | async-start | bytes 786432 | tf_op jit(solution)/shard_map/all_to_all | solution.py:382
  40.4 6.9 %shard_map.89 = (f32[3072,128]{1,0:T(8,128)}, f32[1536,128]{1,0:T(8,128)S(1)}) custom-call(f32[4,1024,128]{2,1,0:T(8,128)} %shard_map.87.part_ref, bf16[4,1024,1024]{2,1,0:T(8,128)(2,1)} %matrix_ref.29, bf16[1024,128]{1,0:T(8,128)(2,1)} %get-tuple-element.54.margin_ref, f32[3072,128]{1,0:T(8,128)} %base_ref.7, s32[1536,128]{1,0:T(8,128)S(1)} %get-tuple-element.55.column_ref), custom_call_target="tpu_custom_call" | custom-call | flops 2415919104 | bytes 8000000 | tf_op jit(solution)/shard_map/pallas_call | solution.py:79
  47.2 1.5 all-to-all-done.2
  48.7 2.2 %shard_map.91 = bf16[1536,128]{1,0:T(8,128)(2,1)} custom-call(f32[1536,128]{1,0:T(8,128)S(1)} %get-tuple-element.59.sent_ref, bf16[1536,128]{1,0:T(8,128)(2,1)S(1)} %bitcast.34, s32[1536,128]{1,0:T(8,128)S(1)} %get-tuple-element.55.column_ref, s32[1,1536]{1,0:T(1,128)S(1)} %broadcast_in_dim_reshape.3.row_ref), custom_call_target="tpu_custom_call" | custom-call | flops 603979776 | bytes 3000000 | tf_op jit(solution)/shard_map/pallas_call | solution.py:88
  50.9 3.6 %all-to-all-start.3 = ((bf16[8,192,128]{2,1,0:T(8,128)(2,1)}), bf16[8,192,128]{2,1,0:T(8,128)(2,1)S(1)}, u32[]{:S(2)}, u32[]{:S(2)}) async-start(bf16[8,192,128]{2,1,0:T(8,128)(2,1)} %bitcast.56), calls=%async_computation.3 | async-start | bytes 786432 | tf_op jit(solution)/shard_map/all_to_all | solution.py:382
  54.6 8.3 %shard_map.90 = (f32[4,1024,128]{2,1,0:T(8,128)}, f32[128,128]{1,0:T(8,128)}) custom-call(f32[3072,128]{1,0:T(8,128)} %get-tuple-element.56.base_ref, bf16[1536,128]{1,0:T(8,128)(2,1)S(1)} %bitcast.35, s32[1,1536]{1,0:T(1,128)S(1)} %broadcast_in_dim_reshape.3.row_ref, bf16[4,1024,1024]{2,1,0:T(8,128)(2,1)} %matrix_ref.26, bf16[4,32,1024]{2,1,0:T(8,128)(2,1)} %bitcast.48), custom_call_target="tpu_custom_call" | custom-call | flops 2013265920 | bytes 14000000 | tf_op jit(solution)/shard_map/pallas_call | solution.py:79
  62.9 2.8 %shard_map.92 = (bf16[1024,128]{1,0:T(8,128)(2,1)}, bf16[128,128]{1,0:T(8,128)(2,1)S(1)}) custom-call(bf16[1536,128]{1,0:T(8,128)(2,1)S(1)} %bitcast.45, s32[1024,128]{1,0:T(8,128)} %get-tuple-element.53.placed_ref, bf16[4,32,1024]{2,1,0:T(8,128)(2,1)} %bitcast.49, f32[128,128]{1,0:T(8,128)} %get-tuple-element.60.proj_ref), custom_call_target="tpu_custom_call" | custom-call | flops 603979776 | bytes 2000000 | tf_op jit(solution)/shard_map/pallas_call | solution.py:88
  65.7 0.3 collective-permute-start.3
  66.0 1.0 collective-permute-done.3
  67.0 2.7 %collective-permute-start.6 = (bf16[256,128]{1,0:T(8,128)(2,1)S(1)}, bf16[256,128]{1,0:T(8,128)(2,1)S(1)}, u32[]{:S(2)}, u32[]{:S(2)}) collective-permute-start(bf16[256,128]{1,0:T(8,128)(2,1)S(1)} %constant_dynamic-update-slice_fusion.rest_0_), channel_id=1, source_target_pairs={{0,24},{4,28},{8,16},{12,20},{16,8},{20,12},{24,0},{28,4},{1,25},{... | collective-permute-start | bytes 196616 | tf_op jit(solution)/shard_map/ppermute | solution.py:510
  69.6 0.5 collective-permute-start.5
  70.2 0.3 collective-permute-start.4
  70.4 3.4 %shard_map.93 = (f32[1536,128]{1,0:T(8,128)S(1)}, bf16[1536,128]{1,0:T(8,128)(2,1)S(1)}) custom-call(bf16[1024,128]{1,0:T(8,128)(2,1)} %get-tuple-element.61.margin_ref, s32[1,1024]{1,0:T(1,128)} %copy-done, bf16[4,1024,1024]{2,1,0:T(8,128)(2,1)} %matrix_ref.26, f32[4,1024,128]{2,1,0:T(8,128)} %get-tuple-element.58.part_ref, bf16[4,32,1024]{2,1,0:T(8,128)(2,1)} %bitcast.50), custom_call_target="tpu_custom_call" | custom-call | flops 1207959552 | bytes 3000000 | tf_op jit(solution)/shard_map/pallas_call | solution.py:88
  73.9 0.5 collective-permute-done.4.rest_1_
  74.4 2.8 %shard_map.94 = (f32[128,128]{1,0:T(8,128)}, bf16[1536,128]{1,0:T(8,128)(2,1)}) custom-call(s32[2]{0:T(128)S(1)} %pad_add_fusion.here_ref, bf16[256,128]{1,0:T(8,128)(2,1)S(1)} %constant_dynamic-update-slice_fusion.rest_0_, bf16[256,128]{1,0:T(8,128)(2,1)S(1)} %collective-permute-done.4.rest_1_, bf16[256,128]{1,0:T(8,128)(2,1)S(1)} %collective-permute-done.5.rest_2_, ...), custom_call_target="tpu_custom_call" | custom-call | flops 301989888 | bytes 3000000 | tf_op jit(solution)/shard_map/pallas_call | solution.py:88
  77.3 3.5 %all-to-all-start.4 = ((bf16[8,192,128]{2,1,0:T(8,128)(2,1)}), bf16[8,192,128]{2,1,0:T(8,128)(2,1)S(1)}, u32[]{:S(2)}, u32[]{:S(2)}) async-start(bf16[8,192,128]{2,1,0:T(8,128)(2,1)} %bitcast.62), calls=%async_computation.4 | async-start | bytes 786432 | tf_op jit(solution)/shard_map/all_to_all | solution.py:382
  80.7 7.2 %shard_map.95 = (f32[3072,128]{1,0:T(8,128)}, f32[1536,128]{1,0:T(8,128)S(1)}) custom-call(f32[4,1024,128]{2,1,0:T(8,128)} %get-tuple-element.58.part_ref, bf16[4,1024,1024]{2,1,0:T(8,128)(2,1)} %matrix_ref.26, bf16[1024,128]{1,0:T(8,128)(2,1)} %get-tuple-element.61.margin_ref, f32[3072,128]{1,0:T(8,128)} %base_ref.5, ...), custom_call_target="tpu_custom_call" | custom-call | flops 2415919104 | bytes 8000000 | tf_op jit(solution)/shard_map/pallas_call | solution.py:79
  87.9 1.1 all-to-all-done.4
  89.0 2.1 %shard_map.97 = bf16[1536,128]{1,0:T(8,128)(2,1)} custom-call(f32[1536,128]{1,0:T(8,128)S(1)} %get-tuple-element.73.sent_ref, bf16[1536,128]{1,0:T(8,128)(2,1)S(1)} %bitcast.40, s32[1536,128]{1,0:T(8,128)S(1)} %get-tuple-element.55.column_ref, s32[1,1536]{1,0:T(1,128)S(1)} %broadcast_in_dim_reshape.3.row_ref), custom_call_target="tpu_custom_call" | custom-call | flops 603979776 | bytes 3000000 | tf_op jit(solution)/shard_map/pallas_call | solution.py:88
  91.1 3.5 %all-to-all-start.5 = ((bf16[8,192,128]{2,1,0:T(8,128)(2,1)}), bf16[8,192,128]{2,1,0:T(8,128)(2,1)S(1)}, u32[]{:S(2)}, u32[]{:S(2)}) async-start(bf16[8,192,128]{2,1,0:T(8,128)(2,1)} %bitcast.57), calls=%async_computation.5 | async-start | bytes 786432 | tf_op jit(solution)/shard_map/all_to_all | solution.py:382
  94.6 7.8 %shard_map.96 = (f32[3072,128]{1,0:T(8,128)}, f32[4,1024,128]{2,1,0:T(8,128)}) custom-call(f32[3072,128]{1,0:T(8,128)} %get-tuple-element.70.base_ref, bf16[1536,128]{1,0:T(8,128)(2,1)S(1)} %bitcast.41, s32[1,1536]{1,0:T(1,128)S(1)} %broadcast_in_dim_reshape.3.row_ref, bf16[4,1024,1024]{2,1,0:T(8,128)(2,1)} %matrix_ref.29), custom_call_target="tpu_custom_call" | custom-call | flops 2013265920 | bytes 14000000 | tf_op jit(solution)/shard_map/pallas_call | solution.py:79
  102.4 0.4 all-to-all-done.5
  102.9 4.0 %shard_map.98 = (bf16[1024,128]{1,0:T(8,128)(2,1)}, bf16[1536,128]{1,0:T(8,128)(2,1)}) custom-call(bf16[1536,128]{1,0:T(8,128)(2,1)S(1)} %bitcast.44, s32[1024,128]{1,0:T(8,128)} %get-tuple-element.53.placed_ref, s32[1,1024]{1,0:T(1,128)} %copy-done, bf16[4,1024,1024]{2,1,0:T(8,128)(2,1)} %matrix_ref.29, f32[4,1024,128]{2,1,0:T(8,128)} %get-tuple-element.72.part_ref), custom_call_target="tpu_custom_call" | custom-call | flops 1207959552 | bytes 3000000 | tf_op jit(solution)/shard_map/pallas_call | solution.py:88
  106.9 3.7 %all-to-all-start.6 = ((bf16[8,192,128]{2,1,0:T(8,128)(2,1)}), bf16[8,192,128]{2,1,0:T(8,128)(2,1)S(1)}, u32[]{:S(2)}, u32[]{:S(2)}) async-start(bf16[8,192,128]{2,1,0:T(8,128)(2,1)} %bitcast.65), calls=%async_computation.6 | async-start | bytes 786432 | tf_op jit(solution)/shard_map/all_to_all | solution.py:382
  110.6 6.9 %shard_map.99 = (f32[3072,128]{1,0:T(8,128)}, f32[1536,128]{1,0:T(8,128)S(1)}) custom-call(f32[4,1024,128]{2,1,0:T(8,128)} %get-tuple-element.72.part_ref, bf16[4,1024,1024]{2,1,0:T(8,128)(2,1)} %matrix_ref.29, bf16[1024,128]{1,0:T(8,128)(2,1)} %get-tuple-element.74.margin_ref, f32[3072,128]{1,0:T(8,128)} %base_ref.7, ...), custom_call_target="tpu_custom_call" | custom-call | flops 2415919104 | bytes 8000000 | tf_op jit(solution)/shard_map/pallas_call | solution.py:79
  117.5 1.5 all-to-all-done.6
  119.0 2.2 %shard_map.101 = bf16[1536,128]{1,0:T(8,128)(2,1)} custom-call(f32[1536,128]{1,0:T(8,128)S(1)} %get-tuple-element.78.sent_ref, bf16[1536,128]{1,0:T(8,128)(2,1)S(1)} %bitcast.36, s32[1536,128]{1,0:T(8,128)S(1)} %get-tuple-element.55.column_ref, s32[1,1536]{1,0:T(1,128)S(1)} %broadcast_in_dim_reshape.3.row_ref), custom_call_target="tpu_custom_call" | custom-call | flops 603979776 | bytes 3000000 | tf_op jit(solution)/shard_map/pallas_call | solution.py:88
  121.1 3.7 %all-to-all-start.7 = ((bf16[8,192,128]{2,1,0:T(8,128)(2,1)}), bf16[8,192,128]{2,1,0:T(8,128)(2,1)S(1)}, u32[]{:S(2)}, u32[]{:S(2)}) async-start(bf16[8,192,128]{2,1,0:T(8,128)(2,1)} %bitcast.58), calls=%async_computation.7 | async-start | bytes 786432 | tf_op jit(solution)/shard_map/all_to_all | solution.py:382
  124.8 8.3 %shard_map.100 = (f32[4,1024,128]{2,1,0:T(8,128)}, f32[128,128]{1,0:T(8,128)}) custom-call(f32[3072,128]{1,0:T(8,128)} %get-tuple-element.75.base_ref, bf16[1536,128]{1,0:T(8,128)(2,1)S(1)} %bitcast.37, s32[1,1536]{1,0:T(1,128)S(1)} %broadcast_in_dim_reshape.3.row_ref, bf16[4,1024,1024]{2,1,0:T(8,128)(2,1)} %matrix_ref.26, bf16[4,32,1024]{2,1,0:T(8,128)(2,1)} %bitcast.52), custom_call_target="tpu_custom_call" | custom-call | flops 2013265920 | bytes 14000000 | tf_op jit(solution)/shard_map/pallas_call | solution.py:79
  133.1 2.8 %shard_map.102 = (bf16[1024,128]{1,0:T(8,128)(2,1)}, bf16[128,128]{1,0:T(8,128)(2,1)S(1)}) custom-call(bf16[1536,128]{1,0:T(8,128)(2,1)S(1)} %bitcast.47, s32[1024,128]{1,0:T(8,128)} %get-tuple-element.53.placed_ref, bf16[4,32,1024]{2,1,0:T(8,128)(2,1)} %bitcast.53, f32[128,128]{1,0:T(8,128)} %get-tuple-element.79.proj_ref), custom_call_target="tpu_custom_call" | custom-call | flops 603979776 | bytes 2000000 | tf_op jit(solution)/shard_map/pallas_call | solution.py:88
  136.1 1.0 collective-permute-done.7
  137.2 2.6 %collective-permute-start.10 = (bf16[256,128]{1,0:T(8,128)(2,1)S(1)}, bf16[256,128]{1,0:T(8,128)(2,1)S(1)}, u32[]{:S(2)}, u32[]{:S(2)}) collective-permute-start(bf16[256,128]{1,0:T(8,128)(2,1)S(1)} %constant_dynamic-update-slice_fusion.2.rest_0_), channel_id=1, source_target_pairs={{0,24},{4,28},{8,16},{12,20},{16,8},{20,12},{24,0},{28,4},{1,25},{... | collective-permute-start | bytes 196616 | tf_op jit(solution)/shard_map/ppermute | solution.py:510
  139.8 0.5 collective-permute-start.9
  140.3 0.3 collective-permute-start.8
  140.7 3.4 %shard_map.103 = (f32[1536,128]{1,0:T(8,128)S(1)}, bf16[1536,128]{1,0:T(8,128)(2,1)S(1)}) custom-call(bf16[1024,128]{1,0:T(8,128)(2,1)} %get-tuple-element.80.margin_ref, s32[1,1024]{1,0:T(1,128)} %copy-done, bf16[4,1024,1024]{2,1,0:T(8,128)(2,1)} %matrix_ref.26, f32[4,1024,128]{2,1,0:T(8,128)} %get-tuple-element.77.part_ref, bf16[4,32,1024]{2,1,0:T(8,128)(2,1)} %bitcast.54), custom_call_target="tpu_custom_call" | custom-call | flops 1207959552 | bytes 3000000 | tf_op jit(solution)/shard_map/pallas_call | solution.py:88
  144.1 0.5 collective-permute-done.8.rest_1_
  144.6 2.9 %shard_map.104 = (f32[128,128]{1,0:T(8,128)}, bf16[1536,128]{1,0:T(8,128)(2,1)}) custom-call(s32[2]{0:T(128)S(1)} %pad_add_fusion.here_ref, bf16[256,128]{1,0:T(8,128)(2,1)S(1)} %constant_dynamic-update-slice_fusion.2.rest_0_, bf16[256,128]{1,0:T(8,128)(2,1)S(1)} %collective-permute-done.8.rest_1_, bf16[256,128]{1,0:T(8,128)(2,1)S(1)} %collective-permute-done.9.rest_2_, ...), custom_call_target="tpu_custom_call" | custom-call | flops 301989888 | bytes 3000000 | tf_op jit(solution)/shard_map/pallas_call | solution.py:88
  147.4 3.5 %all-to-all-start.8 = ((bf16[8,192,128]{2,1,0:T(8,128)(2,1)}), bf16[8,192,128]{2,1,0:T(8,128)(2,1)S(1)}, u32[]{:S(2)}, u32[]{:S(2)}) async-start(bf16[8,192,128]{2,1,0:T(8,128)(2,1)} %bitcast.61), calls=%async_computation.8 | async-start | bytes 786432 | tf_op jit(solution)/shard_map/all_to_all | solution.py:382
  150.9 7.2 %shard_map.105 = (f32[3072,128]{1,0:T(8,128)}, f32[1536,128]{1,0:T(8,128)S(1)}) custom-call(f32[4,1024,128]{2,1,0:T(8,128)} %get-tuple-element.77.part_ref, bf16[4,1024,1024]{2,1,0:T(8,128)(2,1)} %matrix_ref.26, bf16[1024,128]{1,0:T(8,128)(2,1)} %get-tuple-element.80.margin_ref, f32[3072,128]{1,0:T(8,128)} %get-tuple-element.81.base_ref, ...), custom_call_target="tpu_custom_call" | custom-call | flops 2415919104 | bytes 8000000 | tf_op jit(solution)/shard_map/pallas_call | solution.py:79
  158.1 1.1 all-to-all-done.8
  159.2 2.1 %shard_map.107 = bf16[1536,128]{1,0:T(8,128)(2,1)} custom-call(f32[1536,128]{1,0:T(8,128)S(1)} %get-tuple-element.90.sent_ref, bf16[1536,128]{1,0:T(8,128)(2,1)S(1)} %bitcast.38, s32[1536,128]{1,0:T(8,128)S(1)} %get-tuple-element.55.column_ref, s32[1,1536]{1,0:T(1,128)S(1)} %broadcast_in_dim_reshape.3.row_ref), custom_call_target="tpu_custom_call" | custom-call | flops 603979776 | bytes 3000000 | tf_op jit(solution)/shard_map/pallas_call | solution.py:88
  161.3 3.5 %all-to-all-start.9 = ((bf16[8,192,128]{2,1,0:T(8,128)(2,1)}), bf16[8,192,128]{2,1,0:T(8,128)(2,1)S(1)}, u32[]{:S(2)}, u32[]{:S(2)}) async-start(bf16[8,192,128]{2,1,0:T(8,128)(2,1)} %bitcast.59), calls=%async_computation.9 | async-start | bytes 786432 | tf_op jit(solution)/shard_map/all_to_all | solution.py:382
  164.8 7.8 %shard_map.106 = (f32[3072,128]{1,0:T(8,128)}, f32[4,1024,128]{2,1,0:T(8,128)}) custom-call(f32[3072,128]{1,0:T(8,128)} %get-tuple-element.86.base_ref, bf16[1536,128]{1,0:T(8,128)(2,1)S(1)} %bitcast.39, s32[1,1536]{1,0:T(1,128)S(1)} %broadcast_in_dim_reshape.3.row_ref, bf16[4,1024,1024]{2,1,0:T(8,128)(2,1)} %matrix_ref.29), custom_call_target="tpu_custom_call" | custom-call | flops 2013265920 | bytes 14000000 | tf_op jit(solution)/shard_map/pallas_call | solution.py:79
  172.6 0.4 all-to-all-done.9
  173.1 4.0 %shard_map.108 = (bf16[1024,128]{1,0:T(8,128)(2,1)}, bf16[1536,128]{1,0:T(8,128)(2,1)}) custom-call(bf16[1536,128]{1,0:T(8,128)(2,1)S(1)} %bitcast.43, s32[1024,128]{1,0:T(8,128)} %get-tuple-element.53.placed_ref, s32[1,1024]{1,0:T(1,128)} %copy-done, bf16[4,1024,1024]{2,1,0:T(8,128)(2,1)} %matrix_ref.29, f32[4,1024,128]{2,1,0:T(8,128)} %get-tuple-element.89.part_ref), custom_call_target="tpu_custom_call" | custom-call | flops 1207959552 | bytes 3000000 | tf_op jit(solution)/shard_map/pallas_call | solution.py:88
  177.1 3.7 %all-to-all-start.10 = ((bf16[8,192,128]{2,1,0:T(8,128)(2,1)}), bf16[8,192,128]{2,1,0:T(8,128)(2,1)S(1)}, u32[]{:S(2)}, u32[]{:S(2)}) async-start(bf16[8,192,128]{2,1,0:T(8,128)(2,1)} %bitcast.63), calls=%async_computation.10 | async-start | bytes 786432 | tf_op jit(solution)/shard_map/all_to_all | solution.py:382
  180.8 6.8 %shard_map.109 = (f32[3072,128]{1,0:T(8,128)S(1)}, f32[1536,128]{1,0:T(8,128)}) custom-call(f32[4,1024,128]{2,1,0:T(8,128)} %get-tuple-element.89.part_ref, bf16[4,1024,1024]{2,1,0:T(8,128)(2,1)} %matrix_ref.29, bf16[1024,128]{1,0:T(8,128)(2,1)} %get-tuple-element.91.margin_ref, f32[3072,128]{1,0:T(8,128)} %base_ref.7, ...), custom_call_target="tpu_custom_call" | custom-call | flops 2415919104 | bytes 8000000 | tf_op jit(solution)/shard_map/pallas_call | solution.py:79
  187.7 1.5 all-to-all-done.10
  189.1 3.5 %shard_map.110 = f32[3072,128]{1,0:T(8,128)} custom-call(f32[3072,128]{1,0:T(8,128)S(1)} %get-tuple-element.92.base_ref, bf16[1536,128]{1,0:T(8,128)(2,1)S(1)} %bitcast.46, s32[1,1536]{1,0:T(1,128)S(1)} %broadcast_in_dim_reshape.3.row_ref), custom_call_target="tpu_custom_call" | custom-call | flops 1207959552 | bytes 4000000 | tf_op jit(solution)/shard_map/pallas_call | solution.py:88
  (36 shorter events, 0.6 us)
Async XLA Ops:
  3.4 9.9 %all-to-all-start = ((s32[8,1,192]{2,1,0:T(1,128)}), s32[8,1,192]{2,1,0:T(1,128)S(1)}, u32[]{:S(2)}, u32[]{:S(2)}) async-start(s32[8,1,192]{2,1,0:T(1,128)} %sub.24), calls=%async_computation | async-start | bytes 16384 | tf_op jit(solution)/shard_map/all_to_all | solution.py:382
  10.0 8.1 %copy-start = (s32[1,1024]{1,0:T(1,128)}, s32[1,1024]{1,0:T(1,128)S(1)}, u32[]{:S(2)}) copy-start(s32[1,1024]{1,0:T(1,128)S(1)} %fusion.6.place_ref) | copy-start | bytes 12292
  10.9 14.4 %copy-start.1 = (bf16[128,256]{1,0:T(8,128)(2,1)}, bf16[128,256]{1,0:T(8,128)(2,1)S(1)}, u32[]{:S(2)}) copy-start(bf16[128,256]{1,0:T(8,128)(2,1)S(1)} %convert_element_type.27.rest_4_) | copy-start | bytes 196612
  18.1 14.1 %all-to-all-start.1 = ((bf16[8,192,128]{2,1,0:T(8,128)(2,1)}), bf16[8,192,128]{2,1,0:T(8,128)(2,1)S(1)}, u32[]{:S(2)}, u32[]{:S(2)}) async-start(bf16[8,192,128]{2,1,0:T(8,128)(2,1)} %bitcast.60), calls=%async_computation.1 | async-start | bytes 786432 | tf_op jit(solution)/shard_map/all_to_all | solution.py:382
  21.6 10.6 %collective-permute-start.2 = (bf16[128,256]{1,0:T(8,128)(2,1)S(1)}, bf16[128,256]{1,0:T(8,128)(2,1)S(1)}, u32[]{:S(2)}, u32[]{:S(2)}) collective-permute-start(bf16[128,256]{1,0:T(8,128)(2,1)S(1)} %convert_element_type.27.rest_4_), channel_id=1, source_target_pairs={{0,3},{1,2},{2,1},{3,0},{4,7},{5,6},{6,5},{7,4},{8,11},{9,10},{10,... | collective-permute-start | bytes 196616 | tf_op jit(solution)/shard_map/ppermute | solution.py:414
  25.3 6.9 %collective-permute-start.1 = (bf16[128,256]{1,0:T(8,128)(2,1)S(1)}, bf16[128,256]{1,0:T(8,128)(2,1)S(1)}, u32[]{:S(2)}, u32[]{:S(2)}) collective-permute-start(bf16[128,256]{1,0:T(8,128)(2,1)S(1)} %convert_element_type.27.rest_4_), channel_id=1, source_target_pairs={{0,2},{1,3},{2,0},{3,1},{4,6},{5,7},{6,4},{7,5},{8,10},{9,11},{10,... | collective-permute-start | bytes 196616 | tf_op jit(solution)/shard_map/ppermute | solution.py:414
  25.3 6.9 %collective-permute-start = (bf16[128,256]{1,0:T(8,128)(2,1)S(1)}, bf16[128,256]{1,0:T(8,128)(2,1)S(1)}, u32[]{:S(2)}, u32[]{:S(2)}) collective-permute-start(bf16[128,256]{1,0:T(8,128)(2,1)S(1)} %convert_element_type.27.rest_4_), channel_id=1, source_target_pairs={{0,1},{1,0},{2,3},{3,2},{4,5},{5,4},{6,7},{7,6},{8,9},{9,8},{10,11... | collective-permute-start | bytes 196616 | tf_op jit(solution)/shard_map/ppermute | solution.py:414
  32.2 4.1 %copy-start.2 = (bf16[128,256]{1,0:T(8,128)(2,1)}, bf16[128,256]{1,0:T(8,128)(2,1)S(1)}, u32[]{:S(2)}) copy-start(bf16[128,256]{1,0:T(8,128)(2,1)S(1)} %collective-permute-done.2.rest_7_) | copy-start | bytes 196612
  32.2 4.1 %copy-start.3 = (bf16[128,256]{1,0:T(8,128)(2,1)}, bf16[128,256]{1,0:T(8,128)(2,1)S(1)}, u32[]{:S(2)}) copy-start(bf16[128,256]{1,0:T(8,128)(2,1)S(1)} %collective-permute-done.1.rest_6_) | copy-start | bytes 196612
  32.2 4.1 %copy-start.4 = (bf16[128,256]{1,0:T(8,128)(2,1)}, bf16[128,256]{1,0:T(8,128)(2,1)S(1)}, u32[]{:S(2)}) copy-start(bf16[128,256]{1,0:T(8,128)(2,1)S(1)} %collective-permute-done.rest_5_) | copy-start | bytes 196612
  36.3 12.4 %all-to-all-start.2 = ((bf16[8,192,128]{2,1,0:T(8,128)(2,1)}), bf16[8,192,128]{2,1,0:T(8,128)(2,1)S(1)}, u32[]{:S(2)}, u32[]{:S(2)}) async-start(bf16[8,192,128]{2,1,0:T(8,128)(2,1)} %bitcast.64), calls=%async_computation.2 | async-start | bytes 786432 | tf_op jit(solution)/shard_map/all_to_all | solution.py:382
  50.9 12.0 %all-to-all-start.3 = ((bf16[8,192,128]{2,1,0:T(8,128)(2,1)}), bf16[8,192,128]{2,1,0:T(8,128)(2,1)S(1)}, u32[]{:S(2)}, u32[]{:S(2)}) async-start(bf16[8,192,128]{2,1,0:T(8,128)(2,1)} %bitcast.56), calls=%async_computation.3 | async-start | bytes 786432 | tf_op jit(solution)/shard_map/all_to_all | solution.py:382
  65.7 1.3 collective-permute-start.3
  67.0 6.9 %collective-permute-start.6 = (bf16[256,128]{1,0:T(8,128)(2,1)S(1)}, bf16[256,128]{1,0:T(8,128)(2,1)S(1)}, u32[]{:S(2)}, u32[]{:S(2)}) collective-permute-start(bf16[256,128]{1,0:T(8,128)(2,1)S(1)} %constant_dynamic-update-slice_fusion.rest_0_), channel_id=1, source_target_pairs={{0,24},{4,28},{8,16},{12,20},{16,8},{20,12},{24,0},{28,4},{1,25},{... | collective-permute-start | bytes 196616 | tf_op jit(solution)/shard_map/ppermute | solution.py:510
  69.6 4.3 %collective-permute-start.5 = (bf16[256,128]{1,0:T(8,128)(2,1)S(1)}, bf16[256,128]{1,0:T(8,128)(2,1)S(1)}, u32[]{:S(2)}, u32[]{:S(2)}) collective-permute-start(bf16[256,128]{1,0:T(8,128)(2,1)S(1)} %constant_dynamic-update-slice_fusion.rest_0_), channel_id=1, source_target_pairs={{0,16},{4,20},{8,24},{12,28},{16,0},{20,4},{24,8},{28,12},{1,17},{... | collective-permute-start | bytes 196616 | tf_op jit(solution)/shard_map/ppermute | solution.py:510
  70.2 4.3 %collective-permute-start.4 = (bf16[256,128]{1,0:T(8,128)(2,1)S(1)}, bf16[256,128]{1,0:T(8,128)(2,1)S(1)}, u32[]{:S(2)}, u32[]{:S(2)}) collective-permute-start(bf16[256,128]{1,0:T(8,128)(2,1)S(1)} %constant_dynamic-update-slice_fusion.rest_0_), channel_id=1, source_target_pairs={{0,8},{4,12},{8,0},{12,4},{16,24},{20,28},{24,16},{28,20},{1,9},{5... | collective-permute-start | bytes 196616 | tf_op jit(solution)/shard_map/ppermute | solution.py:510
  77.3 11.8 %all-to-all-start.4 = ((bf16[8,192,128]{2,1,0:T(8,128)(2,1)}), bf16[8,192,128]{2,1,0:T(8,128)(2,1)S(1)}, u32[]{:S(2)}, u32[]{:S(2)}) async-start(bf16[8,192,128]{2,1,0:T(8,128)(2,1)} %bitcast.62), calls=%async_computation.4 | async-start | bytes 786432 | tf_op jit(solution)/shard_map/all_to_all | solution.py:382
  91.1 11.7 %all-to-all-start.5 = ((bf16[8,192,128]{2,1,0:T(8,128)(2,1)}), bf16[8,192,128]{2,1,0:T(8,128)(2,1)S(1)}, u32[]{:S(2)}, u32[]{:S(2)}) async-start(bf16[8,192,128]{2,1,0:T(8,128)(2,1)} %bitcast.57), calls=%async_computation.5 | async-start | bytes 786432 | tf_op jit(solution)/shard_map/all_to_all | solution.py:382
  106.9 12.0 %all-to-all-start.6 = ((bf16[8,192,128]{2,1,0:T(8,128)(2,1)}), bf16[8,192,128]{2,1,0:T(8,128)(2,1)S(1)}, u32[]{:S(2)}, u32[]{:S(2)}) async-start(bf16[8,192,128]{2,1,0:T(8,128)(2,1)} %bitcast.65), calls=%async_computation.6 | async-start | bytes 786432 | tf_op jit(solution)/shard_map/all_to_all | solution.py:382
  121.1 12.0 %all-to-all-start.7 = ((bf16[8,192,128]{2,1,0:T(8,128)(2,1)}), bf16[8,192,128]{2,1,0:T(8,128)(2,1)S(1)}, u32[]{:S(2)}, u32[]{:S(2)}) async-start(bf16[8,192,128]{2,1,0:T(8,128)(2,1)} %bitcast.58), calls=%async_computation.7 | async-start | bytes 786432 | tf_op jit(solution)/shard_map/all_to_all | solution.py:382
  135.9 1.3 collective-permute-start.7
  137.2 6.9 %collective-permute-start.10 = (bf16[256,128]{1,0:T(8,128)(2,1)S(1)}, bf16[256,128]{1,0:T(8,128)(2,1)S(1)}, u32[]{:S(2)}, u32[]{:S(2)}) collective-permute-start(bf16[256,128]{1,0:T(8,128)(2,1)S(1)} %constant_dynamic-update-slice_fusion.2.rest_0_), channel_id=1, source_target_pairs={{0,24},{4,28},{8,16},{12,20},{16,8},{20,12},{24,0},{28,4},{1,25},{... | collective-permute-start | bytes 196616 | tf_op jit(solution)/shard_map/ppermute | solution.py:510
  139.8 4.3 %collective-permute-start.9 = (bf16[256,128]{1,0:T(8,128)(2,1)S(1)}, bf16[256,128]{1,0:T(8,128)(2,1)S(1)}, u32[]{:S(2)}, u32[]{:S(2)}) collective-permute-start(bf16[256,128]{1,0:T(8,128)(2,1)S(1)} %constant_dynamic-update-slice_fusion.2.rest_0_), channel_id=1, source_target_pairs={{0,16},{4,20},{8,24},{12,28},{16,0},{20,4},{24,8},{28,12},{1,17},{... | collective-permute-start | bytes 196616 | tf_op jit(solution)/shard_map/ppermute | solution.py:510
  140.3 4.3 %collective-permute-start.8 = (bf16[256,128]{1,0:T(8,128)(2,1)S(1)}, bf16[256,128]{1,0:T(8,128)(2,1)S(1)}, u32[]{:S(2)}, u32[]{:S(2)}) collective-permute-start(bf16[256,128]{1,0:T(8,128)(2,1)S(1)} %constant_dynamic-update-slice_fusion.2.rest_0_), channel_id=1, source_target_pairs={{0,8},{4,12},{8,0},{12,4},{16,24},{20,28},{24,16},{28,20},{1,9},{5... | collective-permute-start | bytes 196616 | tf_op jit(solution)/shard_map/ppermute | solution.py:510
  147.4 11.8 %all-to-all-start.8 = ((bf16[8,192,128]{2,1,0:T(8,128)(2,1)}), bf16[8,192,128]{2,1,0:T(8,128)(2,1)S(1)}, u32[]{:S(2)}, u32[]{:S(2)}) async-start(bf16[8,192,128]{2,1,0:T(8,128)(2,1)} %bitcast.61), calls=%async_computation.8 | async-start | bytes 786432 | tf_op jit(solution)/shard_map/all_to_all | solution.py:382
  161.3 11.7 %all-to-all-start.9 = ((bf16[8,192,128]{2,1,0:T(8,128)(2,1)}), bf16[8,192,128]{2,1,0:T(8,128)(2,1)S(1)}, u32[]{:S(2)}, u32[]{:S(2)}) async-start(bf16[8,192,128]{2,1,0:T(8,128)(2,1)} %bitcast.59), calls=%async_computation.9 | async-start | bytes 786432 | tf_op jit(solution)/shard_map/all_to_all | solution.py:382
  177.1 12.0 %all-to-all-start.10 = ((bf16[8,192,128]{2,1,0:T(8,128)(2,1)}), bf16[8,192,128]{2,1,0:T(8,128)(2,1)S(1)}, u32[]{:S(2)}, u32[]{:S(2)}) async-start(bf16[8,192,128]{2,1,0:T(8,128)(2,1)} %bitcast.63), calls=%async_computation.10 | async-start | bytes 786432 | tf_op jit(solution)/shard_map/all_to_all | solution.py:382
